TPU v7x, 128 devices: a whole 4x4x4 slice. The times are simulated.
128 devices in a mesh: gx: 16 (over z, x), gy: 8 (over y, core).
Axes of the slice: x: 4, y: 4, z: 4, core: 2. Of those that a mesh axis runs over, the one named last changes fastest.
Arguments:
- fine_feats: bfloat16 [24576, 8, 512], P(('gx', 'gy')), may hold values from -6 to 6
- owner_of: int32 [24576], P(('gx', 'gy')), may hold values from 0 to 127, as said below
- arrival_slot: int32 [98304], P(('gx', 'gy')), may hold values from -1 to 383, as said below
- w_stride: bfloat16 [512, 128], replicated, may hold values from -0.25 to 0.25
- w_conv: bfloat16 [27, 128, 128], replicated, may hold values from -0.109375 to 0.109375
- w_head: bfloat16 [128, 8], replicated, may hold values from -4 to 4
- labels: int32 [128, 64, 48], P('gx', 'gy'), may hold values from 0 to 7
Outputs:
- grad_fine: bfloat16 [24576, 8, 512], P(('gx', 'gy'))
- grad_stride: float32 [512, 128], replicated
- grad_conv: float32 [27, 128, 128], replicated
Inputs may be any that keep to these rules, and one draw needn't show every extreme that they name: `owner_of`: one device's rows name one owner at most 6 times, and some device reaches 6. `arrival_slot`: entry d * 128 * 6 + s * 6 + p is the slot (0 to 383) of the p-th fine brick that device s sends to owner d, in row order, and -1 where s sends fewer; one owner's slots are distinct, and some owner fills all of its slots.
All inputs are finite; a program needn't handle non-finite values.
Results may differ from a plain program's by a relative error of at most 0.012.
Values may be sent and summed in bfloat16 or wider, within the bound.
No kernel may reach another device: no remote copies, remote signals or barrier semaphores. Data moves between devices by JAX's collectives and lax.ppermute only.
A program may use at most 128 MiB of HBM per device.

v0:
```python
import functools
import math

import jax
import jax.numpy as jnp
from jax import lax
from jax.experimental import pallas as pl
from jax.experimental.pallas import tpu as pltpu
from jax.sharding import PartitionSpec as P

BX = 2
BY = 2
BR = 4
SX = 8
SY = 8
SZ = 48
CH = 128
CELLS = 8
FX = SX + 4
FY = SY + 4
ROWS = SY * SZ
CODE = 16
SIDE = 2 * SZ
BRICKS = 384
BACK = 80
VMEM = pltpu.CompilerParams(vmem_limit_bytes=48 * 1024 * 1024)
BF = jnp.bfloat16
F32 = jnp.float32


def whole(shape):
    return pl.BlockSpec(shape, lambda: (0,) * len(shape))


def smem():
    return pl.BlockSpec(memory_space=pltpu.SMEM)


def matmul(a, b):
    return jnp.dot(a, b, preferred_element_type=F32)


def iota(shape, dim):
    return lax.broadcasted_iota(jnp.int32, shape, dim)


def send_kernel(cap, owner, feats, w_stride, buf, place, rows, count):
    per_dev = owner.shape[0]
    devs = count.shape[0]

    def clear(i, c):
        count[i] = 0
        return c

    lax.fori_loop(0, devs, clear, 0, unroll=8)
    buf[...] = jnp.zeros_like(buf)
    rows[...] = matmul(feats[...], w_stride[...]).reshape(rows.shape)

    def put(i, c):
        who = owner[i]
        pos = count[who]
        count[who] = pos + 1
        place[i] = (who * (BACK // 16) + pos // 2) * 2 + pos % 2
        buf[who * cap + pos] = rows[i].astype(BF)
        return c

    lax.fori_loop(0, per_dev, put, 0, unroll=4)


def send(feats, owner, w_stride, devs, cap):
    per_dev = owner.shape[0]
    return pl.pallas_call(
        functools.partial(send_kernel, cap),
        out_shape=(
            jax.ShapeDtypeStruct((devs * cap, CELLS, CH), BF),
            jax.ShapeDtypeStruct((per_dev,), jnp.int32),
        ),
        in_specs=[smem(), whole(feats.shape), whole(w_stride.shape)],
        out_specs=(whole((devs * cap, CELLS, CH)), smem()),
        scratch_shapes=[pltpu.VMEM((per_dev, CELLS, CH), F32), pltpu.SMEM((devs,), jnp.int32)],
        compiler_params=VMEM,
        name="send_bricks",
    )(owner, feats, w_stride)


def brick_order():
    row = iota((4 * SZ, 4 * SZ), 0)
    col = iota((4 * SZ, 4 * SZ), 1)
    z = row % SZ
    return (col == (z // 2) * 8 + (row // SZ) * 2 + z % 2).astype(BF)


def land_kernel(index, arrived, order, code, slab, first, last, held):
    held[...] = jnp.zeros_like(held)

    def put(j, c):
        held[index[j]] = arrived[j].astype(F32)
        return c

    lax.fori_loop(0, index.shape[0], put, 0, unroll=8)
    for big_x in range(SX // 2):
        for big_y in range(SY // 2):
            start = (big_x * (SY // 2) + big_y) * (SZ // 2)
            block = held[start : start + SZ // 2].reshape(4 * SZ, CH).astype(BF)
            moved = matmul(order[...], block).astype(BF)
            for i in range(2):
                for l in range(2):
                    piece = moved[(2 * i + l) * SZ : (2 * i + l + 1) * SZ]
                    row = (2 * big_y + l) * SZ
                    slab[2 * big_x + i, row : row + SZ, :] = piece
    slab[:, ROWS:, :] = code[...]
    first[...] = slab[:2]
    last[...] = slab[SX - 2 :]


def land(arrived, index, order, code):
    shapes = ((SX, ROWS + CODE, CH), (2, ROWS + CODE, CH), (2, ROWS + CODE, CH))
    return pl.pallas_call(
        land_kernel,
        out_shape=tuple(jax.ShapeDtypeStruct(s, BF) for s in shapes),
        in_specs=[smem(), whole(arrived.shape), whole(order.shape), whole(code.shape)],
        out_specs=tuple(whole(s) for s in shapes),
        scratch_shapes=[pltpu.VMEM((BRICKS + 8, CELLS, CH), F32)],
        compiler_params=VMEM,
        name="land_bricks",
    )(index, arrived, order, code)


def sides_kernel(slab, before, after, up, down):
    row = iota((CODE // 2, CH), 0)
    none = jnp.zeros((CODE // 2, CH), F32)
    for x in range(FX):
        if x < 2:
            ref, at = before, x
        elif x < 2 + SX:
            ref, at = slab, x - 2
        else:
            ref, at = after, x - 2 - SX
        up[x, :SIDE, :] = ref[at, ROWS - SIDE : ROWS, :]
        down[x, :SIDE, :] = ref[at, :SIDE, :]
        codes = ref[at, ROWS:, :].astype(F32)
        upper = jnp.where(row < 2, codes[8:], 0.0)
        lower = jnp.where((row == 2) | (row == 3), codes[:8], 0.0)
        up[x, SIDE:, :] = jnp.concatenate([upper, none], axis=0).astype(BF)
        down[x, SIDE:, :] = jnp.concatenate([none, lower], axis=0).astype(BF)


def sides(slab, before, after):
    shape = (FX, SIDE + CODE, CH)
    return pl.pallas_call(
        sides_kernel,
        out_shape=(jax.ShapeDtypeStruct(shape, BF),) * 2,
        in_specs=[whole(slab.shape), whole(before.shape), whole(after.shape)],
        out_specs=(whole(shape),) * 2,
        compiler_params=VMEM,
        name="y_sides",
    )(slab, before, after)


def shifted(vals, z, by):
    rows = vals.shape[0]
    turned = pltpu.roll(vals, by % rows, 0)
    return jnp.where(z == (0 if by == 1 else SZ - 1), 0.0, turned)


def core_kernel(
    index, slab, before, after, left, right, w_fwd, w_bwd, head, head_t, order_t, back,
    grid, codes, grad, grad3, total, coarse, held,
):
    grid[:2, SIDE : SIDE + ROWS, :] = before[:, :ROWS, :]
    grid[2 : 2 + SX, SIDE : SIDE + ROWS, :] = slab[:, :ROWS, :]
    grid[2 + SX :, SIDE : SIDE + ROWS, :] = after[:, :ROWS, :]
    grid[:, :SIDE, :] = left[:, :SIDE, :]
    grid[:, SIDE + ROWS :, :] = right[:, :SIDE, :]
    codes[:2] = before[:, ROWS:, :].astype(F32)
    codes[2 : 2 + SX] = slab[:, ROWS:, :].astype(F32)
    codes[2 + SX :] = after[:, ROWS:, :].astype(F32)
    codes[...] += left[:, SIDE:, :].astype(F32) + right[:, SIDE:, :].astype(F32)

    wide = ROWS + SIDE
    lane = iota((wide, CH), 1)
    z_wide = iota((wide // SZ, SZ, CH), 1).reshape(wide, CH)
    z_own = iota((SY, SZ, CH), 1).reshape(ROWS, CH)
    eye = (iota((SZ, CH), 0) == iota((SZ, CH), 1)).astype(F32)
    ones = jnp.ones((CH, CH), BF)

    def forward(x, carry):
        taps = jnp.concatenate(
            [grid[x + e, f * SZ : f * SZ + wide, :] for e in range(3) for f in range(3)], axis=1
        )
        parts = matmul(taps, w_fwd[...])
        pre = (
            shifted(parts[:, :CH], z_wide, 1)
            + parts[:, CH : 2 * CH]
            + shifted(parts[:, 2 * CH :], z_wide, -1)
        )
        here = codes[x + 1]
        spread = jnp.concatenate([eye * here[y + 1 : y + 2, :] for y in range(SY + 2)], axis=0)
        code = matmul(spread.astype(BF), ones)
        mask = code > 0.5
        pre = jnp.where(mask, pre, 0.0)
        gate = jax.nn.sigmoid(pre)
        logits = matmul((pre * gate).astype(BF), head[...])
        target = (code - 1.0 == (lane % 8).astype(F32)).astype(F32)
        grad_logits = jnp.where(mask, jax.nn.sigmoid(logits) - target, 0.0)
        high = grad_logits.astype(BF).astype(F32)
        terms = jnp.where(lane < 8, high, jnp.where(lane < 16, grad_logits - high, 0.0))
        grad_act = matmul(terms.astype(BF), head_t[...])
        grad_pre = (grad_act * gate * (1.0 + pre * (1.0 - gate))).astype(BF)
        grad[x] = grad_pre
        own = grad_pre[SZ : SZ + ROWS].astype(F32)
        grad3[x, :, :CH] = shifted(own, z_own, -1).astype(BF)
        grad3[x, :, CH : 2 * CH] = grad_pre[SZ : SZ + ROWS]
        grad3[x, :, 2 * CH :] = shifted(own, z_own, 1).astype(BF)
        return carry

    lax.fori_loop(0, SX + 2, forward, 0)

    total[...] = jnp.zeros_like(total)

    def weights(x, carry):
        for e in range(3):
            taps = jnp.concatenate(
                [grid[x + 1 + e, (1 + f) * SZ : (1 + f) * SZ + ROWS, :] for f in range(3)], axis=1
            )
            total[e] += lax.dot_general(
                taps, grad3[x + 1], (((0,), (0,)), ((), ())), preferred_element_type=F32
            )
        return carry

    lax.fori_loop(0, SX, weights, 0)

    def backward(x, carry):
        taps = jnp.concatenate(
            [
                grad[x + 2 - e, (2 - f) * SZ : (2 - f) * SZ + ROWS, :]
                for e in range(3)
                for f in range(3)
            ],
            axis=1,
        )
        parts = matmul(taps, w_bwd[...])
        coarse[x] = (
            shifted(parts[:, :CH], z_own, -1)
            + parts[:, CH : 2 * CH]
            + shifted(parts[:, 2 * CH :], z_own, 1)
        ).astype(BF)
        return carry

    lax.fori_loop(0, SX, backward, 0)

    for big_x in range(SX // 2):
        for big_y in range(SY // 2):
            block = jnp.concatenate(
                [
                    coarse[2 * big_x + i, (2 * big_y + l) * SZ : (2 * big_y + l + 1) * SZ, :]
                    for i in range(2)
                    for l in range(2)
                ],
                axis=0,
            )
            start = (big_x * (SY // 2) + big_y) * (SZ // 2)
            held[start : start + SZ // 2] = matmul(order_t[...], block).reshape(SZ // 2, CELLS, CH)

    def put(d, carry):
        for pair in range(3):
            j = d * 6 + 2 * pair
            both = jnp.concatenate([held[index[j]], held[index[j + 1]]], axis=0)
            back[d, 16 * pair : 16 * pair + 16, :] = both.astype(BF)
        return carry

    lax.fori_loop(0, back.shape[0], put, 0, unroll=2)

    for tap in range(27):
        e, f, g = tap // 9, tap // 3 % 3, tap % 3
        block = total[e, f * CH : (f + 1) * CH, g * CH : (g + 1) * CH].astype(BF)
        back[4 * tap : 4 * tap + 4, 48:, :] = block.reshape(4, 32, CH)
    back[108:, 48:, :] = jnp.zeros((back.shape[0] - 108, 32, CH), BF)


def core(index, slab, before, after, left, right, w_fwd, w_bwd, head, head_t, order_t, devs):
    wide = ROWS + SIDE
    arrays = (slab, before, after, left, right, w_fwd, w_bwd, head, head_t, order_t)
    return pl.pallas_call(
        core_kernel,
        out_shape=jax.ShapeDtypeStruct((devs, BACK, CH), BF),
        in_specs=[smem()] + [whole(a.shape) for a in arrays],
        out_specs=whole((devs, BACK, CH)),
        scratch_shapes=[
            pltpu.VMEM((FX, FY * SZ, CH), BF),
            pltpu.VMEM((FX, CODE, CH), F32),
            pltpu.VMEM((SX + 2, wide, CH), BF),
            pltpu.VMEM((SX + 2, ROWS, 3 * CH), BF),
            pltpu.VMEM((3, 3 * CH, 3 * CH), F32),
            pltpu.VMEM((SX, ROWS, CH), BF),
            pltpu.VMEM((BRICKS, CELLS, CH), F32),
        ],
        compiler_params=VMEM,
        name="conv_both_ways",
    )(index, *arrays)


def last_kernel(place, came, feats, w_stride, grad_fine, stride, conv, mine):
    per_dev = place.shape[0]

    def take(i, carry):
        at = place[i]
        both = came[at // 2].astype(F32)
        mine[i] = jnp.where(at % 2 == 0, both[:8], both[8:])
        return carry

    lax.fori_loop(0, per_dev, take, 0, unroll=4)
    vals = mine[...].reshape(per_dev * CELLS, CH).astype(BF)
    grad_fine[...] = lax.dot_general(
        vals, w_stride[...], (((1,), (1,)), ((), ())), preferred_element_type=F32
    ).astype(BF)
    stride[...] = lax.dot_general(
        feats[...], vals, (((0,), (0,)), ((), ())), preferred_element_type=F32
    ).astype(BF)
    per = BACK // 16

    def add(d, sums):
        return (sums[0] + came[d * per + 3].astype(F32), sums[1] + came[d * per + 4].astype(F32))

    none = jnp.zeros((16, CH), F32)
    low, high = lax.fori_loop(0, came.shape[0] // per, add, (none, none), unroll=4)
    conv[:16, :] = low
    conv[16:, :] = high


def last(came, place, feats, w_stride):
    per_dev = place.shape[0]
    return pl.pallas_call(
        last_kernel,
        out_shape=(
            jax.ShapeDtypeStruct(feats.shape, BF),
            jax.ShapeDtypeStruct(w_stride.shape, BF),
            jax.ShapeDtypeStruct((32, CH), F32),
        ),
        in_specs=[smem(), whole(came.shape), whole(feats.shape), whole(w_stride.shape)],
        out_specs=(whole(feats.shape), whole(w_stride.shape), whole((32, CH))),
        scratch_shapes=[pltpu.VMEM((per_dev, CELLS, CH), F32)],
        compiler_params=VMEM,
        name="grad_fine_and_terms",
    )(place, came, feats, w_stride)


def to_all(buffer):
    return lax.all_to_all(buffer, ("gx", "gy"), split_axis=0, concat_axis=0, tiled=True)


def both_ways(first, last_part, axis):
    peers = lax.axis_size(axis)
    up = [(i, i + 1) for i in range(peers - 1)]
    down = [(i + 1, i) for i in range(peers - 1)]
    return lax.ppermute(last_part, axis, up), lax.ppermute(first, axis, down)


def label_codes(arrival_slot, labels):
    bricks = BX * BY * SZ // BR
    filled = jnp.any(
        (arrival_slot >> 3)[None, :] == jnp.arange(bricks, dtype=jnp.int32)[:, None], axis=1
    ).reshape(BX, 1, BY, 1, SZ // BR, 1)
    cells = labels.reshape(BX, BR, BY, BR, SZ // BR, BR)
    codes = jnp.where(filled, cells + 1, 0).reshape(SX, SY, SZ).astype(BF)
    return jnp.pad(codes, ((0, 0), (2, CODE - 2 - SY), (0, CH - SZ)))


def per_device(fine_feats, owner_of, arrival_slot, w_stride, w_conv, w_head, labels):
    devs = lax.axis_size("gx") * lax.axis_size("gy")
    per_dev, cells, in_width = fine_feats.shape
    cap = arrival_slot.shape[0] // devs
    feats = fine_feats.reshape(per_dev * cells, in_width)
    buffer, place = send(feats, owner_of, w_stride, devs, cap)

    brick, octant = arrival_slot >> 3, arrival_slot & 7
    deep = SZ // BR
    big_x = 2 * (brick // (BY * deep)) + (octant >> 2)
    big_y = 2 * (brick // deep % BY) + ((octant >> 1) & 1)
    big_z = 2 * (brick % deep) + (octant & 1)
    index = jnp.where(arrival_slot >= 0, (big_x * (SY // 2) + big_y) * (SZ // 2) + big_z, BRICKS)
    code = label_codes(arrival_slot, labels)
    order = brick_order()
    taps = w_conv.reshape(9, 3, CH, CH)
    w_fwd = taps.transpose(0, 2, 1, 3).reshape(9 * CH, 3 * CH)
    w_bwd = taps.transpose(0, 3, 1, 2).reshape(9 * CH, 3 * CH)
    head = jnp.pad(jnp.concatenate([w_head, w_head], axis=1), ((0, 0), (0, CH - 16)))

    arrived = to_all(buffer)
    slab, first, last_part = land(arrived, index, order, code)
    before, after = both_ways(first, last_part, "gx")
    up, down = sides(slab, before, after)
    left, right = both_ways(down, up, "gy")
    returned = core(
        jnp.minimum(index, BRICKS - 1),
        slab,
        before,
        after,
        left,
        right,
        w_fwd,
        w_bwd,
        head,
        head.T,
        order.T,
        devs,
    )
    came = to_all(returned)
    grad_fine, stride, conv = last(
        came.reshape(devs * BACK // 16, 16, CH), place, feats, w_stride
    )
    share = in_width // devs
    terms = to_all(stride.reshape(devs, share, CH))
    stride_sum = jnp.sum(terms.astype(F32), axis=0)
    block = jnp.concatenate([conv, stride_sum], axis=0).astype(BF)
    sums = to_all(jnp.broadcast_to(block[None], (devs,) + block.shape))
    scale = 1.0 / math.sqrt(per_dev * devs * cells)
    grad_conv = sums[:, :32].reshape(devs * 32, CH)[: 27 * CH].astype(F32) * scale
    grad_stride = sums[:, 32:].reshape(in_width, CH).astype(F32) * scale
    return (
        grad_fine.reshape(per_dev, cells, in_width),
        grad_stride,
        grad_conv.reshape(27, CH, CH),
    )


def solution(mesh):
    return jax.shard_map(
        per_device,
        mesh=mesh,
        in_specs=(
            P(("gx", "gy"), None, None),
            P(("gx", "gy")),
            P(("gx", "gy")),
            P(),
            P(),
            P(),
            P("gx", "gy", None),
        ),
        out_specs=(P(("gx", "gy"), None, None), P(), P()),
        check_vma=False,
    )
```

profile of v0, /device:TPU:1, one launch (start us, length us, event | category | flops | bytes accessed | tf_op | source)
XLA Modules:
  0.0 187.5 jit_solution(1846997462057006127)
XLA Ops:
  0.6 1.4 copy-done
  2.0 0.9 copy-done.2
  2.9 0.7 copy-done.4
  3.6 4.6 %send_bricks.1 = (bf16[768,8,128]{2,1,0:T(8,128)(2,1)}, s32[192]{0:T(256)S(1)}) custom-call(s32[192]{0:T(256)S(1)} %copy-done.4, bf16[1536,512]{1,0:T(8,128)(2,1)S(1)} %bitcast.20, bf16[512,128]{1,0:T(8,128)(2,1)S(1)} %copy-done.2), custom_call_target="tpu_custom_call" | custom-call | tf_op jit(solution)/shard_map/send_bricks/pallas_call | solution.py:72
  8.3 11.5 %all-to-all-start = ((bf16[768,8,128]{2,1,0:T(8,128)(2,1)}), bf16[768,8,128]{2,1,0:T(8,128)(2,1)S(1)}, u32[]{:S(2)}, u32[]{:S(2)}) async-start(bf16[768,8,128]{2,1,0:T(8,128)(2,1)} %get-tuple-element.14), calls=%async_computation | async-start | bytes 3145728 | tf_op jit(solution)/shard_map/all_to_all | solution.py:349
  19.8 0.1 fusion.18
  20.0 0.1 broadcast_in_dim.30
  20.2 0.2 broadcast_in_dim.31
  20.5 0.2 fusion.16
  20.7 23.6 %all-to-all-done.arrived = bf16[768,8,128]{2,1,0:T(8,128)(2,1)S(1)} async-done(((bf16[768,8,128]{2,1,0:T(8,128)(2,1)}), bf16[768,8,128]{2,1,0:T(8,128)(2,1)S(1)}, u32[]{:S(2)}, u32[]{:S(2)}) %all-to-all-start) | async-done | bytes 1572896 | tf_op jit(solution)/shard_map/all_to_all | solution.py:349
  44.3 2.6 %land_bricks.1 = (bf16[8,400,128]{2,1,0:T(8,128)(2,1)S(1)}, bf16[2,400,128]{2,1,0:T(8,128)(2,1)S(1)}, bf16[2,400,128]{2,1,0:T(8,128)(2,1)S(1)}) custom-call(s32[768]{0:T(1024)S(1)} %get-tuple-element.24.index, bf16[768,8,128]{2,1,0:T(8,128)(2,1)S(1)} %all-to-all-done.arrived, bf16[192,192]{1,0:T(8,128)(2,1)S(1)} %get-tuple-element.26.order, ...), custom_call_target="tpu_custom_call" | custom-call | tf_op jit(solution)/shard_map/land_bricks/pallas_call | solution.py:118
  47.0 2.5 %collective-permute-start = (bf16[2,400,128]{2,1,0:T(8,128)(2,1)S(1)}, bf16[2,400,128]{2,1,0:T(8,128)(2,1)S(1)}, u32[]{:S(2)}, u32[]{:S(2)}) collective-permute-start(bf16[2,400,128]{2,1,0:T(8,128)(2,1)S(1)} %get-tuple-element.16), channel_id=1, source_target_pairs={{0,8},{8,16},{16,24},{24,32},{32,40},{40,48},{48,56},{56,64},{64,7... | collective-permute-start | bytes 614408 | tf_op jit(solution)/shard_map/ppermute | solution.py:356
  49.5 1.3 collective-permute-start.1
  50.8 3.3 %copy.17 = bf16[9,3,128,128]{2,1,3,0:T(4,128)(2,1)} copy(bf16[9,3,128,128]{3,2,1,0:T(8,128)(2,1)} %bitcast.24) | data formatting | bytes 1769472 | tf_op jit(solution)/shard_map/reshape | solution.py:384
  54.0 1.8 copy.16
  55.8 0.1 copy.18.head
  56.0 0.5 collective-permute-done.1.after
  56.5 3.6 %collective-permute-start.2 = (bf16[12,112,128]{2,1,0:T(8,128)(2,1)S(1)}, bf16[12,112,128]{2,1,0:T(8,128)(2,1)S(1)}, u32[]{:S(2)}, u32[]{:S(2)}) collective-permute-start(bf16[12,112,128]{2,1,0:T(8,128)(2,1)S(1)} %get-tuple-element.18), channel_id=1, source_target_pairs={{0,1},{1,2},{2,3},{3,4},{4,5},{5,6},{6,7},{8,9},{9,10},{10,11},{11... | collective-permute-start | bytes 1032200 | tf_op jit(solution)/shard_map/ppermute | solution.py:356
  60.2 2.0 %collective-permute-start.3 = (bf16[12,112,128]{2,1,0:T(8,128)(2,1)S(1)}, bf16[12,112,128]{2,1,0:T(8,128)(2,1)S(1)}, u32[]{:S(2)}, u32[]{:S(2)}) collective-permute-start(bf16[12,112,128]{2,1,0:T(8,128)(2,1)S(1)} %get-tuple-element.19), channel_id=1, source_target_pairs={{1,0},{2,1},{3,2},{4,3},{5,4},{6,5},{7,6},{9,8},{10,9},{11,10},{12... | collective-permute-start | bytes 1032200 | tf_op jit(solution)/shard_map/ppermute | solution.py:356
  62.2 1.6 copy_bitcast_fusion
  63.7 0.6 collective-permute-done.2.left
  64.3 4.4 %collective-permute-done.3.right = bf16[12,112,128]{2,1,0:T(8,128)(2,1)S(1)} collective-permute-done((bf16[12,112,128]{2,1,0:T(8,128)(2,1)S(1)}, bf16[12,112,128]{2,1,0:T(8,128)(2,1)S(1)}, u32[]{:S(2)}, u32[]{:S(2)}) %collective-permute-start.3) | collective-permute-done | bytes 344096 | tf_op jit(solution)/shard_map/ppermute | solution.py:356
  68.7 26.9 %conv_both_ways.1 = bf16[128,80,128]{2,1,0:T(8,128)(2,1)} custom-call(s32[768]{0:T(1024)S(1)} %get-tuple-element.23.index, bf16[8,400,128]{2,1,0:T(8,128)(2,1)S(1)} %get-tuple-element.15.slab, bf16[2,400,128]{2,1,0:T(8,128)(2,1)S(1)} %collective-permute-done.before, bf16[2,400,128]{2,1,0:T(8,128)(2,1)S(1)} %collective-permute-done.1.after, ...), custom_call_target="tpu_custom_call" | custom-call | tf_op jit(solution)/shard_map/conv_both_ways/pallas_call | solution.py:284
  95.6 44.6 %all_to_all.20 = bf16[128,80,128]{2,1,0:T(8,128)(2,1)S(1)} all-to-all(bf16[128,80,128]{2,1,0:T(8,128)(2,1)} %conv_both_ways.1), channel_id=1, replica_groups=mesh['gx'=16,'gy'=8] {'gx','gy'}, dimensions={0} | all-to-all | bytes 5242880 | tf_op jit(solution)/shard_map/all_to_all | solution.py:349
  140.2 4.5 %grad_fine_and_terms.1 = (bf16[1536,512]{1,0:T(8,128)(2,1)}, bf16[512,128]{1,0:T(8,128)(2,1)}, f32[32,128]{1,0:T(8,128)S(1)}) custom-call(s32[192]{0:T(256)S(1)} %get-tuple-element.13.place, bf16[640,16,128]{2,1,0:T(8,128)(2,1)S(1)} %bitcast.19, bf16[1536,512]{1,0:T(8,128)(2,1)S(1)} %bitcast.21, bf16[512,128]{1,0:T(8,128)(2,1)S(1)} %copy-done.3), custom_call_target="tpu_custom_call" | custom-call | tf_op jit(solution)/shard_map/grad_fine_and_terms/pallas_call | solution.py:333
  144.8 4.4 %all-to-all-start.2 = ((bf16[128,4,128]{2,1,0:T(4,128)(2,1)}), bf16[128,4,128]{2,1,0:T(4,128)(2,1)S(1)}, u32[]{:S(2)}, u32[]{:S(2)}) async-start(bf16[128,4,128]{2,1,0:T(4,128)(2,1)} %bitcast.7), calls=%async_computation.2 | async-start | bytes 262144 | tf_op jit(solution)/shard_map/all_to_all | solution.py:349
  149.2 10.2 %all-to-all-done.2 = bf16[128,4,128]{2,1,0:T(4,128)(2,1)S(1)} async-done(((bf16[128,4,128]{2,1,0:T(4,128)(2,1)}), bf16[128,4,128]{2,1,0:T(4,128)(2,1)S(1)}, u32[]{:S(2)}, u32[]{:S(2)}) %all-to-all-start.2) | async-done | bytes 131104 | tf_op jit(solution)/shard_map/all_to_all | solution.py:349
  159.3 0.1 reduce
  159.5 0.2 broadcast_in_dim.33
  159.7 25.6 %all_to_all.21 = bf16[128,36,128]{2,1,0:T(8,128)(2,1)S(1)} all-to-all(bf16[128,36,128]{2,1,0:T(8,128)(2,1)S(1)} %broadcast_in_dim.33), channel_id=1, replica_groups=mesh['gx'=16,'gy'=8] {'gx','gy'}, dimensions={0} | all-to-all | bytes 2359296 | tf_op jit(solution)/shard_map/all_to_all | solution.py:349
  185.3 0.8 convert_multiply_fusion.1
  186.0 1.4 convert_multiply_fusion
  (29 shorter events, 0.3 us)
Async XLA Ops:
  0.6 1.4 copy-start
  2.0 0.9 copy-start.2
  2.9 0.7 copy-start.4
  8.3 11.5 %copy-start.8 = (s32[768]{0:T(1024)S(1)}, s32[768]{0:T(1024)}, u32[]{:S(2)}) copy-start(s32[768]{0:T(1024)} %param.9) | copy-start | bytes 9220
  8.3 12.1 %copy-start.7 = (s32[8,8,48]{2,1,0:T(8,128)S(1)}, s32[8,8,48]{2,1,0:T(8,128)}, u32[]{:S(2)}) copy-start(s32[8,8,48]{2,1,0:T(8,128)} %param.13) | copy-start | bytes 36868
  8.3 36.1 %all-to-all-start = ((bf16[768,8,128]{2,1,0:T(8,128)(2,1)}), bf16[768,8,128]{2,1,0:T(8,128)(2,1)S(1)}, u32[]{:S(2)}, u32[]{:S(2)}) async-start(bf16[768,8,128]{2,1,0:T(8,128)(2,1)} %get-tuple-element.14), calls=%async_computation | async-start | bytes 3145728 | tf_op jit(solution)/shard_map/all_to_all | solution.py:349
  47.0 7.1 %copy-start.6 = (bf16[27,128,128]{2,1,0:T(8,128)(2,1)S(1)}, bf16[27,128,128]{2,1,0:T(8,128)(2,1)}, u32[]{:S(2)}) copy-start(bf16[27,128,128]{2,1,0:T(8,128)(2,1)} %param.11) | copy-start | bytes 2654212
  47.0 9.0 %collective-permute-start = (bf16[2,400,128]{2,1,0:T(8,128)(2,1)S(1)}, bf16[2,400,128]{2,1,0:T(8,128)(2,1)S(1)}, u32[]{:S(2)}, u32[]{:S(2)}) collective-permute-start(bf16[2,400,128]{2,1,0:T(8,128)(2,1)S(1)} %get-tuple-element.16), channel_id=1, source_target_pairs={{0,8},{8,16},{16,24},{24,32},{32,40},{40,48},{48,56},{56,64},{64,7... | collective-permute-start | bytes 614408 | tf_op jit(solution)/shard_map/ppermute | solution.py:356
  49.5 7.0 %collective-permute-start.1 = (bf16[2,400,128]{2,1,0:T(8,128)(2,1)S(1)}, bf16[2,400,128]{2,1,0:T(8,128)(2,1)S(1)}, u32[]{:S(2)}, u32[]{:S(2)}) collective-permute-start(bf16[2,400,128]{2,1,0:T(8,128)(2,1)S(1)} %get-tuple-element.17), channel_id=1, source_target_pairs={{8,0},{16,8},{24,16},{32,24},{40,32},{48,40},{56,48},{64,56},{72,6... | collective-permute-start | bytes 614408 | tf_op jit(solution)/shard_map/ppermute | solution.py:356
  50.8 5.0 %copy-start.9 = (bf16[128,8]{0,1:T(8,128)(2,1)S(1)}, bf16[128,8]{0,1:T(8,128)(2,1)}, u32[]{:S(2)}) copy-start(bf16[128,8]{0,1:T(8,128)(2,1)} %param.12) | copy-start | bytes 6148
  55.9 6.2 %copy-start.5 = (bf16[9,3,128,128]{2,1,3,0:T(4,128)(2,1)S(1)}, bf16[9,3,128,128]{2,1,3,0:T(4,128)(2,1)}, u32[]{:S(2)}) copy-start(bf16[9,3,128,128]{2,1,3,0:T(4,128)(2,1)} %copy.17) | copy-start | bytes 2654212
  56.5 7.8 %collective-permute-start.2 = (bf16[12,112,128]{2,1,0:T(8,128)(2,1)S(1)}, bf16[12,112,128]{2,1,0:T(8,128)(2,1)S(1)}, u32[]{:S(2)}, u32[]{:S(2)}) collective-permute-start(bf16[12,112,128]{2,1,0:T(8,128)(2,1)S(1)} %get-tuple-element.18), channel_id=1, source_target_pairs={{0,1},{1,2},{2,3},{3,4},{4,5},{5,6},{6,7},{8,9},{9,10},{10,11},{11... | collective-permute-start | bytes 1032200 | tf_op jit(solution)/shard_map/ppermute | solution.py:356
  60.2 8.6 %collective-permute-start.3 = (bf16[12,112,128]{2,1,0:T(8,128)(2,1)S(1)}, bf16[12,112,128]{2,1,0:T(8,128)(2,1)S(1)}, u32[]{:S(2)}, u32[]{:S(2)}) collective-permute-start(bf16[12,112,128]{2,1,0:T(8,128)(2,1)S(1)} %get-tuple-element.19), channel_id=1, source_target_pairs={{1,0},{2,1},{3,2},{4,3},{5,4},{6,5},{7,6},{9,8},{10,9},{11,10},{12... | collective-permute-start | bytes 1032200 | tf_op jit(solution)/shard_map/ppermute | solution.py:356
  95.6 44.6 %copy-start.1 = (bf16[192,8,512]{2,1,0:T(8,128)(2,1)S(1)}, bf16[192,8,512]{2,1,0:T(8,128)(2,1)}, u32[]{:S(2)}) copy-start(bf16[192,8,512]{2,1,0:T(8,128)(2,1)} %param.7) | copy-start | bytes 4718596
  95.6 44.6 %copy-start.3 = (bf16[512,128]{1,0:T(8,128)(2,1)S(1)}, bf16[512,128]{1,0:T(8,128)(2,1)}, u32[]{:S(2)}) copy-start(bf16[512,128]{1,0:T(8,128)(2,1)} %w_stride.3) | copy-start | bytes 393220
  144.8 14.6 %all-to-all-start.2 = ((bf16[128,4,128]{2,1,0:T(4,128)(2,1)}), bf16[128,4,128]{2,1,0:T(4,128)(2,1)S(1)}, u32[]{:S(2)}, u32[]{:S(2)}) async-start(bf16[128,4,128]{2,1,0:T(4,128)(2,1)} %bitcast.7), calls=%async_computation.2 | async-start | bytes 262144 | tf_op jit(solution)/shard_map/all_to_all | solution.py:349
where the time goes:
time: 188 us; the launch traced here: 187 us
  blocking collectives  70.2 us (37%)
  waiting for transfers between devices  39.3 us (21%)
  Pallas kernels  38.7 us (21%)
  starting transfers between devices  25.3 us (13%)
  local copies, waits for them, and re-layouts  10.3 us (5%)
  other arithmetic  2.81 us (1%)
    all_to_all x2, blocking collectives, to_all(): lax.all_to_all(buffer, ('gx', 'gy'), split_axis=0, concat_axis=0, tiled=T...  70.2 us
    all_to_all x2, waiting for transfers between devices, to_all(): lax.all_to_all(buffer, ('gx', 'gy'), split_axis=0, concat_axis=0, tiled=T...  33.8 us
    pallas_call x1, Pallas kernels, core(): pl.pallas_call(core_kernel, out_shape=jax.ShapeDtypeStruct((devs, BACK, C...  26.9 us
    all_to_all x2, starting transfers between devices, to_all(): lax.all_to_all(buffer, ('gx', 'gy'), split_axis=0, concat_axis=0, tiled=T...  15.9 us
    ppermute x4, starting transfers between devices, both_ways(): return (lax.ppermute(last_part, axis, up), lax.ppermute(first, axis, down))  9.37 us
    ppermute x4, waiting for transfers between devices, both_ways(): return (lax.ppermute(last_part, axis, up), lax.ppermute(first, axis, down))  5.52 us
    reshape x2, local copies, waits for them, and re-layouts, per_device(): taps = w_conv.reshape(9, 3, CH, CH)  5.03 us
    pallas_call x1, Pallas kernels, send(): pl.pallas_call(functools.partial(send_kernel, cap), out_shape=(jax.ShapeD...  4.62 us
  transfers between devices with their start and end apart: 6, of which 5 were waited for; matrix products, arithmetic and copies ran while one was open for 4% of the time, Pallas kernels for 0%

commit v1 on v0

v1 whole, which is shorter than its diff:
```python
import functools
import math

import jax
import jax.numpy as jnp
from jax import lax
from jax.experimental import pallas as pl
from jax.experimental.pallas import tpu as pltpu
from jax.sharding import PartitionSpec as P

BX = 2
BY = 2
BR = 4
SX = 8
SY = 8
SZ = 48
CH = 128
CELLS = 8
FX = SX + 4
FY = SY + 4
ROWS = SY * SZ
CODE = 16
SIDE = 2 * SZ
BRICKS = 384
PARTS = 4
VMEM = pltpu.CompilerParams(vmem_limit_bytes=24 * 1024 * 1024)
ALL_VMEM = pltpu.CompilerParams(vmem_limit_bytes=63 * 1024 * 1024)
BF = jnp.bfloat16
F32 = jnp.float32


def whole(shape):
    return pl.BlockSpec(shape, lambda: (0,) * len(shape))


def anywhere():
    return pl.BlockSpec(memory_space=pl.ANY)


def smem():
    return pl.BlockSpec(memory_space=pltpu.SMEM)


def matmul(a, b):
    return jnp.dot(a, b, preferred_element_type=F32)


def iota(shape, dim):
    return lax.broadcasted_iota(jnp.int32, shape, dim)


def send_kernel(
    cap, owner_hbm, feats_hbm, w_hbm, buf_hbm, place, owner, feats, w_stride, rows, buf, count, sems
):
    per_dev = owner.shape[0]
    devs = count.shape[0]
    part = feats.shape[0] // PARTS
    copies = [
        pltpu.make_async_copy(owner_hbm, owner, sems.at[0]),
        pltpu.make_async_copy(w_hbm, w_stride, sems.at[1]),
    ] + [
        pltpu.make_async_copy(
            feats_hbm.at[pl.ds(i * part, part)], feats.at[pl.ds(i * part, part)], sems.at[2 + i]
        )
        for i in range(PARTS)
    ]
    for copy in copies:
        copy.start()

    def clear(i, c):
        count[i] = 0
        return c

    lax.fori_loop(0, devs, clear, 0, unroll=8)
    buf[...] = jnp.zeros_like(buf)
    copies[0].wait()

    def find(i, c):
        who = owner[i]
        pos = count[who]
        count[who] = pos + 1
        place[i] = who * cap + pos
        return c

    lax.fori_loop(0, per_dev, find, 0, unroll=8)
    copies[1].wait()
    bricks = per_dev // PARTS
    for i in range(PARTS):
        copies[2 + i].wait()
        vals = matmul(feats[i * part : (i + 1) * part, :], w_stride[...])
        rows[i * bricks : (i + 1) * bricks] = vals.reshape(bricks, CELLS, CH)

    def put(i, c):
        buf[place[i]] = rows[i].astype(BF)
        return c

    lax.fori_loop(0, per_dev, put, 0, unroll=8)
    out = pltpu.make_async_copy(buf, buf_hbm, sems.at[0])
    out.start()
    out.wait()


def hbm():
    return pl.BlockSpec(memory_space=pltpu.HBM)


def send(feats, owner, w_stride, devs, cap):
    per_dev = owner.shape[0]
    return pl.pallas_call(
        functools.partial(send_kernel, cap),
        out_shape=(
            jax.ShapeDtypeStruct((devs * cap, CELLS, CH), BF),
            jax.ShapeDtypeStruct((per_dev,), jnp.int32),
        ),
        in_specs=[hbm(), hbm(), hbm()],
        out_specs=(hbm(), smem()),
        scratch_shapes=[
            pltpu.SMEM((per_dev,), jnp.int32),
            pltpu.VMEM(feats.shape, BF),
            pltpu.VMEM(w_stride.shape, BF),
            pltpu.VMEM((per_dev, CELLS, CH), F32),
            pltpu.VMEM((devs * cap, CELLS, CH), BF),
            pltpu.SMEM((devs,), jnp.int32),
            pltpu.SemaphoreType.DMA((2 + PARTS,)),
        ],
        compiler_params=ALL_VMEM,
        name="send_bricks",
    )(owner, feats, w_stride)


def brick_order():
    row = iota((4 * SZ, 4 * SZ), 0)
    col = iota((4 * SZ, 4 * SZ), 1)
    z = row % SZ
    return (col == (z // 2) * 8 + (row // SZ) * 2 + z % 2).astype(BF)


def land_kernel(index, arrived, order, code, slab, first, last, held):
    held[...] = jnp.zeros_like(held)

    def put(j, c):
        held[index[j]] = arrived[j].astype(F32)
        return c

    lax.fori_loop(0, index.shape[0], put, 0, unroll=8)
    for big_x in range(SX // 2):
        for big_y in range(SY // 2):
            start = (big_x * (SY // 2) + big_y) * (SZ // 2)
            block = held[start : start + SZ // 2].reshape(4 * SZ, CH).astype(BF)
            moved = matmul(order[...], block).astype(BF)
            for i in range(2):
                for l in range(2):
                    piece = moved[(2 * i + l) * SZ : (2 * i + l + 1) * SZ]
                    row = (2 * big_y + l) * SZ
                    slab[2 * big_x + i, row : row + SZ, :] = piece
    slab[:, ROWS:, :] = code[...]
    first[...] = slab[:2]
    last[...] = slab[SX - 2 :]


def land(arrived, index, order, code):
    shapes = ((SX, ROWS + CODE, CH), (2, ROWS + CODE, CH), (2, ROWS + CODE, CH))
    return pl.pallas_call(
        land_kernel,
        out_shape=tuple(jax.ShapeDtypeStruct(s, BF) for s in shapes),
        in_specs=[smem(), whole(arrived.shape), whole(order.shape), whole(code.shape)],
        out_specs=tuple(whole(s) for s in shapes),
        scratch_shapes=[pltpu.VMEM((BRICKS + 8, CELLS, CH), F32)],
        compiler_params=VMEM,
        name="land_bricks",
    )(index, arrived, order, code)


def sides_kernel(slab, before, after, inside, up, down):
    row = iota((CODE // 2, CH), 0)
    none = jnp.zeros((CODE // 2, CH), F32)
    for x in range(FX):
        if x < 2:
            ref, at = before, x
        elif x < 2 + SX:
            ref, at = slab, x - 2
        else:
            ref, at = after, x - 2 - SX
        up[x, :SIDE, :] = ref[at, ROWS - SIDE : ROWS, :]
        down[x, :SIDE, :] = ref[at, :SIDE, :]
        codes = ref[at, ROWS:, :].astype(F32)
        upper = jnp.where(row < 2, codes[8:], 0.0)
        lower = jnp.where((row == 2) | (row == 3), codes[:8], 0.0)
        up[x, SIDE:, :] = jnp.concatenate([upper, none], axis=0).astype(BF)
        down[x, SIDE:, :] = jnp.concatenate([none, lower], axis=0).astype(BF)


def sides(slab, before, after, inside):
    shape = (FX, SIDE + CODE, CH)
    return pl.pallas_call(
        sides_kernel,
        out_shape=(jax.ShapeDtypeStruct(shape, BF),) * 2,
        in_specs=[whole(slab.shape), whole(before.shape), whole(after.shape), anywhere()],
        out_specs=(whole(shape),) * 2,
        compiler_params=VMEM,
        name="y_sides",
    )(slab, before, after, inside)


def shifted(vals, z, by):
    rows = vals.shape[0]
    turned = pltpu.roll(vals, by % rows, 0)
    return jnp.where(z == (0 if by == 1 else SZ - 1), 0.0, turned)


def spread_codes(blocks):
    eye = (iota((SZ, CH), 0) == iota((SZ, CH), 1)).astype(F32)
    return jnp.concatenate([eye * block for block in blocks], axis=0).astype(BF)


def front(taps, spread, w_fwd, head, head_t):
    rows = spread.shape[0]
    lane = iota((rows, CH), 1)
    z = iota((rows // SZ, SZ, CH), 1).reshape(rows, CH)
    parts = matmul(jnp.concatenate(taps, axis=1), w_fwd)
    pre = (
        shifted(parts[:, :CH], z, 1)
        + parts[:, CH : 2 * CH]
        + shifted(parts[:, 2 * CH :], z, -1)
    )
    code = matmul(spread, jnp.ones((CH, CH), BF))
    mask = code > 0.5
    pre = jnp.where(mask, pre, 0.0)
    gate = jax.nn.sigmoid(pre)
    logits = matmul((pre * gate).astype(BF), head)
    target = (code - 1.0 == (lane % 8).astype(F32)).astype(F32)
    grad_logits = jnp.where(mask, jax.nn.sigmoid(logits) - target, 0.0)
    high = grad_logits.astype(BF).astype(F32)
    terms = jnp.where(lane < 8, high, jnp.where(lane < 16, grad_logits - high, 0.0))
    grad_act = matmul(terms.astype(BF), head_t)
    return (grad_act * gate * (1.0 + pre * (1.0 - gate))).astype(BF)


INNER = (SY - 2) * SZ


def front_cost(slabs):
    flops = 2 * 9 * 3 * CH * CH * INNER * slabs
    return pl.CostEstimate(flops=flops, bytes_accessed=4 * 2**20, transcendentals=0)


def inner_kernel(slab, w_fwd, head, head_t, grad):
    def step(x, carry):
        taps = [slab[x + e, f * SZ : f * SZ + INNER, :] for e in range(3) for f in range(3)]
        codes = slab[x + 1, ROWS:, :].astype(F32)
        spread = spread_codes([codes[y : y + 1] for y in range(3, SY + 1)])
        grad[x] = front(taps, spread, w_fwd[...], head[...], head_t[...])
        return carry

    lax.fori_loop(0, SX - 2, step, 0, unroll=2)


def inner(slab, w_fwd, head, head_t):
    arrays = (slab, w_fwd, head, head_t)
    shape = (SX - 2, INNER, CH)
    return pl.pallas_call(
        inner_kernel,
        out_shape=jax.ShapeDtypeStruct(shape, BF),
        in_specs=[whole(a.shape) for a in arrays],
        out_specs=whole(shape),
        compiler_params=VMEM,
        cost_estimate=front_cost(SX - 2),
        name="grad_pre_inside",
    )(*arrays)


def x_sides_kernel(slab, before, after, w_fwd, head, head_t, grad):
    def source(x):
        if x < 2:
            return before, x
        return (slab, x - 2) if x < SX + 2 else (after, x - SX - 2)

    for i, x in enumerate((0, 1, SX, SX + 1)):
        taps = []
        for e in range(3):
            ref, at = source(x + e)
            taps += [ref[at, f * SZ : f * SZ + INNER, :] for f in range(3)]
        ref, at = source(x + 1)
        codes = ref[at, ROWS:, :].astype(F32)
        spread = spread_codes([codes[y : y + 1] for y in range(3, SY + 1)])
        grad[i] = front(taps, spread, w_fwd[...], head[...], head_t[...])


def x_sides(slab, before, after, w_fwd, head, head_t):
    arrays = (slab, before, after, w_fwd, head, head_t)
    shape = (4, INNER, CH)
    return pl.pallas_call(
        x_sides_kernel,
        out_shape=jax.ShapeDtypeStruct(shape, BF),
        in_specs=[whole(a.shape) for a in arrays],
        out_specs=whole(shape),
        compiler_params=VMEM,
        cost_estimate=front_cost(4),
        name="grad_pre_x_sides",
    )(*arrays)


def core_kernel(
    index, slab, before, after, left, right, inside, at_x, w_fwd, w_bwd, head, head_t, order_t,
    back_hbm, grid_hbm, own_hbm, low, high, codes, grad, coarse, held, back, sems,
):
    middle = pl.ds(SIDE, ROWS)
    pairs = (
        (slab.at[:, pl.ds(0, ROWS)], grid_hbm.at[pl.ds(2, SX), middle]),
        (before.at[:, pl.ds(0, ROWS)], grid_hbm.at[pl.ds(0, 2), middle]),
        (after.at[:, pl.ds(0, ROWS)], grid_hbm.at[pl.ds(2 + SX, 2), middle]),
        (left.at[:, pl.ds(0, SIDE)], grid_hbm.at[:, pl.ds(0, SIDE)]),
        (right.at[:, pl.ds(0, SIDE)], grid_hbm.at[:, pl.ds(SIDE + ROWS, SIDE)]),
    )
    copies = [pltpu.make_async_copy(a, b, sems.at[i]) for i, (a, b) in enumerate(pairs)]
    for copy in copies:
        copy.start()
    for at, ref in ((0, before), (2, slab), (2 + SX, after)):
        many = ref.shape[0]
        low[at : at + many, SIDE:, :] = ref[:, :SIDE, :]
        high[at : at + many, :SIDE, :] = ref[:, ROWS - SIDE : ROWS, :]
        codes[at : at + many] = ref[:, ROWS:, :].astype(F32)
    low[:, :SIDE, :] = left[:, :SIDE, :]
    high[:, SIDE:, :] = right[:, :SIDE, :]
    codes[...] += left[:, SIDE:, :].astype(F32) + right[:, SIDE:, :].astype(F32)
    grad[:2, SIDE : SIDE + INNER, :] = at_x[:2]
    grad[2:SX, SIDE : SIDE + INNER, :] = inside[...]
    grad[SX:, SIDE : SIDE + INNER, :] = at_x[2:]

    z_own = iota((SY, SZ, CH), 1).reshape(ROWS, CH)

    def forward(pair, carry):
        x = 2 * pair
        taps = [
            jnp.concatenate(
                [
                    ref[x + i + e, f * SZ : f * SZ + SIDE, :]
                    for i in range(2)
                    for ref in (low, high)
                ],
                axis=0,
            )
            for e in range(3)
            for f in range(3)
        ]
        blocks = []
        for i in range(2):
            here = codes[x + i + 1]
            blocks += [here[y : y + 1] for y in (1, 2, SY + 1, SY + 2)]
        vals = front(taps, spread_codes(blocks), w_fwd[...], head[...], head_t[...])
        for i in range(2):
            grad[x + i, :SIDE, :] = vals[2 * i * SIDE : (2 * i + 1) * SIDE]
            grad[x + i, SIDE + INNER :, :] = vals[(2 * i + 1) * SIDE : (2 * i + 2) * SIDE]
        return carry

    lax.fori_loop(0, SX // 2 + 1, forward, 0, unroll=5)
    out = pltpu.make_async_copy(
        grad.at[pl.ds(1, SX), pl.ds(SZ, ROWS)], own_hbm, sems.at[len(pairs)]
    )
    out.start()
    copies.append(out)

    def backward(x, carry):
        taps = jnp.concatenate(
            [
                grad[x + 2 - e, (2 - f) * SZ : (2 - f) * SZ + ROWS, :]
                for e in range(3)
                for f in range(3)
            ],
            axis=1,
        )
        parts = matmul(taps, w_bwd[...])
        coarse[x] = (
            shifted(parts[:, :CH], z_own, -1)
            + parts[:, CH : 2 * CH]
            + shifted(parts[:, 2 * CH :], z_own, 1)
        ).astype(BF)
        return carry

    lax.fori_loop(0, SX, backward, 0, unroll=2)

    for big_x in range(SX // 2):
        for big_y in range(SY // 2):
            block = jnp.concatenate(
                [
                    coarse[2 * big_x + i, (2 * big_y + l) * SZ : (2 * big_y + l + 1) * SZ, :]
                    for i in range(2)
                    for l in range(2)
                ],
                axis=0,
            )
            start = (big_x * (SY // 2) + big_y) * (SZ // 2)
            held[start : start + SZ // 2] = matmul(order_t[...], block).reshape(SZ // 2, CELLS, CH)

    def put(j, carry):
        back[j] = held[index[j]].astype(BF)
        return carry

    part = index.shape[0] // PARTS
    for i in range(PARTS):
        lax.fori_loop(i * part, (i + 1) * part, put, 0, unroll=8)
        rows = pl.ds(i * part, part)
        copy = pltpu.make_async_copy(back.at[rows], back_hbm.at[rows], sems.at[6 + i])
        copy.start()
        copies.append(copy)
    for copy in copies:
        copy.wait()


def core(
    index, slab, before, after, left, right, inside, at_x, w_fwd, w_bwd, head, head_t, order_t
):
    arrays = (
        slab, before, after, left, right, inside, at_x, w_fwd, w_bwd, head, head_t, order_t
    )
    shapes = ((index.shape[0], CELLS, CH), (FX, FY * SZ, CH), (SX, ROWS, CH))
    return pl.pallas_call(
        core_kernel,
        out_shape=tuple(jax.ShapeDtypeStruct(s, BF) for s in shapes),
        in_specs=[smem()] + [whole(a.shape) for a in arrays],
        out_specs=(hbm(),) * 3,
        scratch_shapes=[
            pltpu.VMEM((FX, 2 * SIDE, CH), BF),
            pltpu.VMEM((FX, 2 * SIDE, CH), BF),
            pltpu.VMEM((FX, CODE, CH), F32),
            pltpu.VMEM((SX + 2, ROWS + SIDE, CH), BF),
            pltpu.VMEM((SX, ROWS, CH), BF),
            pltpu.VMEM((BRICKS, CELLS, CH), F32),
            pltpu.VMEM((index.shape[0], CELLS, CH), BF),
            pltpu.SemaphoreType.DMA((6 + PARTS,)),
        ],
        compiler_params=VMEM,
        name="conv_both_ways",
    )(index, *arrays)


def weights_kernel(half, grid, grad, keep, give, total, taps_out):
    z_own = iota((SY, SZ, CH), 1).reshape(ROWS, CH)
    total[...] = jnp.zeros_like(total)

    def add(x, carry):
        mid = grad[x].astype(F32)
        grads = jnp.concatenate(
            [shifted(mid, z_own, -1).astype(BF), grad[x], shifted(mid, z_own, 1).astype(BF)],
            axis=1,
        )
        for e in range(3):
            taps = jnp.concatenate(
                [grid[x + 1 + e, (1 + f) * SZ : (1 + f) * SZ + ROWS, :] for f in range(3)], axis=1
            )
            total[e] += lax.dot_general(
                taps, grads, (((0,), (0,)), ((), ())), preferred_element_type=F32
            )
        return carry

    lax.fori_loop(0, SX, add, 0, unroll=2)
    for tap in range(27):
        e, f, g = tap // 9, tap // 3 % 3, tap % 3
        taps_out[tap] = total[e, f * CH : (f + 1) * CH, g * CH : (g + 1) * CH]
    taps_out[27:] = jnp.zeros((5, CH, CH), F32)
    mine = half[0]
    keep[...] = taps_out[pl.ds(16 * mine, 16)]
    give[...] = taps_out[pl.ds(16 * (1 - mine), 16)].astype(BF)


def weights(half, grid, grad):
    shape = (16, CH, CH)
    return pl.pallas_call(
        weights_kernel,
        out_shape=(jax.ShapeDtypeStruct(shape, F32), jax.ShapeDtypeStruct(shape, BF)),
        in_specs=[smem(), whole(grid.shape), whole(grad.shape)],
        out_specs=(whole(shape),) * 2,
        scratch_shapes=[pltpu.VMEM((3, 3 * CH, 3 * CH), F32), pltpu.VMEM((32, CH, CH), F32)],
        compiler_params=ALL_VMEM,
        cost_estimate=pl.CostEstimate(
            flops=2 * 27 * CH * CH * SX * ROWS, bytes_accessed=6 * 2**20, transcendentals=0
        ),
        name="conv_weight_grad",
    )(half, grid, grad)


def pair_kernel(me, keep, got, mine, *others):
    share = mine.shape[0]
    for by, out in enumerate((mine,) + others):
        at = pl.ds(share * lax.rem(me[0] + by, len(others) + 1), share)
        out[...] = (keep[at] + got[at].astype(F32)).astype(out.dtype)


def add_pair(y, keep, got, ring):
    shape = (keep.shape[0] // ring, CH, CH)
    kinds = (F32,) + (BF,) * (ring - 1)
    return pl.pallas_call(
        pair_kernel,
        out_shape=tuple(jax.ShapeDtypeStruct(shape, kind) for kind in kinds),
        in_specs=[smem(), whole(keep.shape), whole(got.shape)],
        out_specs=(whole(shape),) * ring,
        compiler_params=ALL_VMEM,
        name="add_pair",
    )(y, keep, got)


def sum_over_gy(keep, give):
    me = lax.axis_index("gy")
    y = me // 2
    peers = lax.axis_size("gy")
    ring = peers // 2
    got = lax.ppermute(give, "gy", [(i, i ^ 1) for i in range(peers)])
    total, *others = add_pair(y.astype(jnp.int32).reshape(1), keep, got, ring)
    for by, part in enumerate(others, 1):
        perm = [(i, (i + 2 * by) % peers) for i in range(peers)]
        total = total + lax.ppermute(part, "gy", perm).astype(F32)
    return total.transpose(1, 0, 2).astype(BF)


def last_kernel(place, came, feats, mine, stride, rows):
    per_dev = place.shape[0]

    def take(i, carry):
        rows[i] = came[place[i]].astype(F32)
        return carry

    lax.fori_loop(0, per_dev, take, 0, unroll=8)
    vals = rows[...].reshape(per_dev * CELLS, CH).astype(BF)
    mine[...] = vals
    stride[...] = lax.dot_general(
        feats[...], vals, (((0,), (0,)), ((), ())), preferred_element_type=F32
    ).astype(BF)


def last(came, place, feats):
    shapes = ((feats.shape[0], CH), (feats.shape[1], CH))
    return pl.pallas_call(
        last_kernel,
        out_shape=tuple(jax.ShapeDtypeStruct(s, BF) for s in shapes),
        in_specs=[smem(), whole(came.shape), whole(feats.shape)],
        out_specs=tuple(whole(s) for s in shapes),
        scratch_shapes=[pltpu.VMEM((place.shape[0], CELLS, CH), F32)],
        compiler_params=VMEM,
        name="stride_term",
    )(place, came, feats)


def to_all(buffer):
    return lax.all_to_all(buffer, ("gx", "gy"), split_axis=0, concat_axis=0, tiled=True)


def both_ways(first, last_part, axis):
    peers = lax.axis_size(axis)
    up = [(i, i + 1) for i in range(peers - 1)]
    down = [(i + 1, i) for i in range(peers - 1)]
    return lax.ppermute(last_part, axis, up), lax.ppermute(first, axis, down)


def label_codes(arrival_slot, labels):
    bricks = BX * BY * SZ // BR
    filled = jnp.any(
        (arrival_slot >> 3)[None, :] == jnp.arange(bricks, dtype=jnp.int32)[:, None], axis=1
    ).reshape(BX, 1, BY, 1, SZ // BR, 1)
    cells = labels.reshape(BX, BR, BY, BR, SZ // BR, BR)
    codes = jnp.where(filled, cells + 1, 0).reshape(SX, SY, SZ).astype(BF)
    return jnp.pad(codes, ((0, 0), (2, CODE - 2 - SY), (0, CH - SZ)))


def per_device(fine_feats, owner_of, arrival_slot, w_stride, w_conv, w_head, labels):
    devs = lax.axis_size("gx") * lax.axis_size("gy")
    per_dev, cells, in_width = fine_feats.shape
    cap = arrival_slot.shape[0] // devs
    feats = fine_feats.reshape(per_dev * cells, in_width)
    buffer, place = send(feats, owner_of, w_stride, devs, cap)

    brick, octant = arrival_slot >> 3, arrival_slot & 7
    deep = SZ // BR
    big_x = 2 * (brick // (BY * deep)) + (octant >> 2)
    big_y = 2 * (brick // deep % BY) + ((octant >> 1) & 1)
    big_z = 2 * (brick % deep) + (octant & 1)
    index = jnp.where(arrival_slot >= 0, (big_x * (SY // 2) + big_y) * (SZ // 2) + big_z, BRICKS)
    code = label_codes(arrival_slot, labels)
    order = brick_order()
    place, w_conv = lax.optimization_barrier((place, w_conv))
    taps = w_conv.reshape(9, 3, CH, CH)
    w_fwd = taps.transpose(0, 2, 1, 3).reshape(9 * CH, 3 * CH)
    w_bwd = taps.transpose(0, 3, 1, 2).reshape(9 * CH, 3 * CH)
    head = jnp.pad(jnp.concatenate([w_head, w_head], axis=1), ((0, 0), (0, CH - 16)))

    arrived, w_fwd, w_bwd = lax.optimization_barrier((to_all(buffer), w_fwd, w_bwd))
    slab, first, last_part = land(arrived, index, order, code)
    before, after = both_ways(first, last_part, "gx")
    inside = inner(slab, w_fwd, head, head.T)
    up, down = sides(slab, before, after, inside)
    left, right = both_ways(down, up, "gy")
    at_x = x_sides(slab, before, after, w_fwd, head, head.T)
    returned, grid, grad = core(
        jnp.minimum(index, BRICKS - 1),
        slab,
        before,
        after,
        left,
        right,
        inside,
        at_x,
        w_fwd,
        w_bwd,
        head,
        head.T,
        order.T,
    )
    came = to_all(returned)
    half = (lax.axis_index("gy") % 2).astype(jnp.int32).reshape(1)
    conv = sum_over_gy(*weights(half, grid, grad))
    mine, stride = last(came, place, feats)
    share = in_width // devs
    terms = to_all(jnp.concatenate([conv, stride.reshape(devs, share, CH)], axis=1))
    grad_fine = lax.dot_general(
        mine, w_stride, (((1,), (1,)), ((), ())), preferred_element_type=F32
    ).astype(BF)
    terms = terms.astype(F32).reshape(lax.axis_size("gx"), lax.axis_size("gy"), 4 + share, CH)
    by_part = jnp.sum(terms, axis=0)
    conv_sum = by_part[:, :4].reshape(-1, 2, 4, CH).transpose(1, 0, 2, 3).reshape(32, CH)
    block = jnp.concatenate([conv_sum, jnp.sum(by_part[:, 4:], axis=0)], axis=0).astype(BF)
    sums = to_all(jnp.broadcast_to(block[None], (devs,) + block.shape))
    scale = 1.0 / math.sqrt(per_dev * devs * cells)
    grad_conv = sums[:, :27].transpose(1, 0, 2).astype(F32) * scale
    grad_stride = sums[:, 32:].reshape(in_width, CH).astype(F32) * scale
    return (
        grad_fine.reshape(per_dev, cells, in_width),
        grad_stride,
        grad_conv,
    )


def solution(mesh):
    return jax.shard_map(
        per_device,
        mesh=mesh,
        in_specs=(
            P(("gx", "gy"), None, None),
            P(("gx", "gy")),
            P(("gx", "gy")),
            P(),
            P(),
            P(),
            P("gx", "gy", None),
        ),
        out_specs=(P(("gx", "gy"), None, None), P(), P()),
        check_vma=False,
    )
```

time: 188 us -> 173 us (0.920)
  blocking collectives: 70.2 us -> 17.5 us
  waiting for transfers between devices: 39.3 us -> 52.3 us
  starting transfers between devices: 25.3 us -> 38.2 us
  local copies, waits for them, and re-layouts: 10.3 us -> 17.6 us
  Pallas kernels: 38.7 us -> 41.5 us
    all_to_all x2 -> x1, blocking collectives: 70.2 us -> 17.5 us  [to_all(): lax.all_to_all(buffer, ('gx', 'gy'), split_axis=0, concat_axis=0, tiled=T...]
    ppermute x0 -> x4, waiting for transfers between devices: none -> 11.4 us  [the longest x3 9.68 us: sum_over_gy(): total = total + lax.ppermute(part, 'gy', perm).astype(F32)]
    all_to_all x2 -> x3, starting transfers between devices: 15.9 us -> 24.7 us  [to_all(): lax.all_to_all(buffer, ('gx', 'gy'), split_axis=0, concat_axis=0, tiled=T...]
    unnamed x20 -> x27, local copies, waits for them, and re-layouts: 3.02 us -> 9.34 us
    ppermute x0 -> x4, starting transfers between devices: none -> 4.11 us  [the longest x3 3 us: sum_over_gy(): total = total + lax.ppermute(part, 'gy', perm).astype(F32)]
    all_to_all x2 -> x3, waiting for transfers between devices: 33.8 us -> 37.3 us  [to_all(): lax.all_to_all(buffer, ('gx', 'gy'), split_axis=0, concat_axis=0, tiled=T...]
    ppermute x4, waiting for transfers between devices: 5.52 us -> 3.55 us  [both_ways(): return (lax.ppermute(last_part, axis, up), lax.ppermute(first, axis, down))]
    pallas_call x2 -> x6, Pallas kernels: 31.4 us -> 33 us  [the longest x1 12.6 us: core(): pl.pallas_call(core_kernel, out_shape=tuple((jax.ShapeDtypeStruct(s, BF)...]
  transfers between devices with their start and end apart: 6 -> 11, of which waited for: 5 -> 7; matrix products, arithmetic and copies ran while one was open for 4% -> 6% of each run, Pallas kernels for 0% -> 10%
where the time goes in v1:
time: 173 us; the launch traced here: 172 us
  waiting for transfers between devices  52.3 us (30%)
  Pallas kernels  41.5 us (24%)
  starting transfers between devices  38.2 us (22%)
  local copies, waits for them, and re-layouts  17.6 us (10%)
  blocking collectives  17.5 us (10%)
  other arithmetic  2.59 us (1%)
    all_to_all x3, waiting for transfers between devices, to_all(): lax.all_to_all(buffer, ('gx', 'gy'), split_axis=0, concat_axis=0, tiled=T...  37.3 us
    all_to_all x3, starting transfers between devices, to_all(): lax.all_to_all(buffer, ('gx', 'gy'), split_axis=0, concat_axis=0, tiled=T...  24.7 us
    all_to_all x1, blocking collectives, to_all(): lax.all_to_all(buffer, ('gx', 'gy'), split_axis=0, concat_axis=0, tiled=T...  17.5 us
    pallas_call x1, Pallas kernels, core(): pl.pallas_call(core_kernel, out_shape=tuple((jax.ShapeDtypeStruct(s, BF)...  12.6 us
    ppermute x3, waiting for transfers between devices, sum_over_gy(): total = total + lax.ppermute(part, 'gy', perm).astype(F32)  9.68 us
    ppermute x4, starting transfers between devices, both_ways(): return (lax.ppermute(last_part, axis, up), lax.ppermute(first, axis, down))  9.4 us
    unnamed x27, local copies, waits for them, and re-layouts  9.34 us
    pallas_call x1, Pallas kernels, weights(): pl.pallas_call(weights_kernel, out_shape=(jax.ShapeDtypeStruct(shape, F32...  8.29 us
  transfers between devices with their start and end apart: 11, of which 7 were waited for; matrix products, arithmetic and copies ran while one was open for 6% of the time, Pallas kernels for 10%

profile of v1, /device:TPU:1, one launch (start us, length us, event | category | flops | bytes accessed | tf_op | source)
XLA Modules:
  0.0 172.5 jit_solution(13217894621107956058)
XLA Ops:
  0.6 5.2 %send_bricks.1 = (bf16[768,8,128]{2,1,0:T(8,128)(2,1)}, s32[192]{0:T(256)}) custom-call(s32[192]{0:T(256)} %owner_hbm.1, bf16[1536,512]{1,0:T(8,128)(2,1)} %bitcast.32, bf16[512,128]{1,0:T(8,128)(2,1)} %w_hbm.1), custom_call_target="tpu_custom_call" | custom-call | tf_op jit(solution)/shard_map/send_bricks/pallas_call | solution.py:109
  5.8 11.5 %all-to-all-start = ((bf16[768,8,128]{2,1,0:T(8,128)(2,1)}), bf16[768,8,128]{2,1,0:T(8,128)(2,1)S(1)}, u32[]{:S(2)}, u32[]{:S(2)}) async-start(bf16[768,8,128]{2,1,0:T(8,128)(2,1)} %get-tuple-element.28), calls=%async_computation | async-start | bytes 3145728 | tf_op jit(solution)/shard_map/all_to_all | solution.py:544
  17.4 2.0 %copy.50 = bf16[9,3,128,128]{2,1,3,0:T(4,128)(2,1)} copy(bf16[9,3,128,128]{3,2,1,0:T(8,128)(2,1)S(1)} %bitcast.37) | data formatting | bytes 1769472 | tf_op jit(solution)/shard_map/reshape | solution.py:580
  19.4 1.8 %copy.49 = bf16[9,3,128,128]{3,1,2,0:T(4,128)(2,1)} copy(bf16[9,3,128,128]{3,2,1,0:T(8,128)(2,1)S(1)} %bitcast.38) | data formatting | bytes 1769472 | tf_op jit(solution)/shard_map/reshape | solution.py:580
  22.6 1.9 %copy_bitcast_fusion = (bf16[1152,384]{1,0:T(8,128)(2,1)S(1)}, bf16[1152,384]{1,0:T(8,128)(2,1)S(1)}) fusion(bf16[144,8,3,128]{3,2,1,0:T(4,128)(2,1)} %bitcast.35, bf16[144,8,3,128]{3,2,1,0:T(4,128)(2,1)} %bitcast.36), kind=kLoop, calls=%fused_computation.3 | loop fusion | bytes 3538944 | tf_op jit(solution)/shard_map/reshape | solution.py:582
  24.6 17.3 %all-to-all-done.arrived = bf16[768,8,128]{2,1,0:T(8,128)(2,1)S(1)} async-done(((bf16[768,8,128]{2,1,0:T(8,128)(2,1)}), bf16[768,8,128]{2,1,0:T(8,128)(2,1)S(1)}, u32[]{:S(2)}, u32[]{:S(2)}) %all-to-all-start) | async-done | bytes 1572896 | tf_op jit(solution)/shard_map/all_to_all | solution.py:544
  42.6 3.3 %land_bricks.1 = (bf16[8,400,128]{2,1,0:T(8,128)(2,1)S(1)}, bf16[2,400,128]{2,1,0:T(8,128)(2,1)}, bf16[2,400,128]{2,1,0:T(8,128)(2,1)}) custom-call(s32[768]{0:T(1024)S(1)} %get-tuple-element.59.index, bf16[768,8,128]{2,1,0:T(8,128)(2,1)S(1)} %all-to-all-done.arrived, bf16[192,192]{1,0:T(8,128)(2,1)S(1)} %get-tuple-element.61.order, ...), custom_call_target="tpu_custom_call" | custom-call | tf_op jit(solution)/shard_map/land_bricks/pallas_call | solution.py:163
  46.9 2.3 %collective-permute-start = (bf16[2,400,128]{2,1,0:T(8,128)(2,1)}, bf16[2,400,128]{2,1,0:T(8,128)(2,1)S(1)}, u32[]{:S(2)}, u32[]{:S(2)}) collective-permute-start(bf16[2,400,128]{2,1,0:T(8,128)(2,1)} %get-tuple-element.32), channel_id=1, source_target_pairs={{0,8},{8,16},{16,24},{24,32},{32,40},{40,48},{48,56},{56,64},{64,7... | collective-permute-start | bytes 614408 | tf_op jit(solution)/shard_map/ppermute | solution.py:551
  49.2 1.3 collective-permute-start.1
  50.7 1.1 copy-done.2
  51.8 4.6 %grad_pre_inside.1.inside = bf16[6,288,128]{2,1,0:T(8,128)(2,1)S(1)} custom-call(bf16[8,400,128]{2,1,0:T(8,128)(2,1)S(1)} %copy-done.2, bf16[1152,384]{1,0:T(8,128)(2,1)S(1)} %get-tuple-element.34.w_fwd, bf16[128,128]{1,0:T(8,128)(2,1)S(1)} %copy.51.head, bf16[128,128]{1,0:T(8,128)(2,1)S(1)} %get-tuple-element.63.head_t), custom_call_target="tpu_custom_call" | custom-call | flops 1528823808 | bytes 4194304 | tf_op jit(solution)/shard_map/grad_pre_inside/pallas_call | solution.py:261
  56.5 3.6 %collective-permute-start.2 = (bf16[12,112,128]{2,1,0:T(8,128)(2,1)S(1)}, bf16[12,112,128]{2,1,0:T(8,128)(2,1)S(1)}, u32[]{:S(2)}, u32[]{:S(2)}) collective-permute-start(bf16[12,112,128]{2,1,0:T(8,128)(2,1)S(1)} %get-tuple-element.35), channel_id=1, source_target_pairs={{0,1},{1,2},{2,3},{3,4},{4,5},{5,6},{6,7},{8,9},{9,10},{10,11},{11... | collective-permute-start | bytes 1032200 | tf_op jit(solution)/shard_map/ppermute | solution.py:551
  60.1 2.2 %collective-permute-start.3 = (bf16[12,112,128]{2,1,0:T(8,128)(2,1)S(1)}, bf16[12,112,128]{2,1,0:T(8,128)(2,1)S(1)}, u32[]{:S(2)}, u32[]{:S(2)}) collective-permute-start(bf16[12,112,128]{2,1,0:T(8,128)(2,1)S(1)} %get-tuple-element.36), channel_id=1, source_target_pairs={{1,0},{2,1},{3,2},{4,3},{5,4},{6,5},{7,6},{9,8},{10,9},{11,10},{12... | collective-permute-start | bytes 1032200 | tf_op jit(solution)/shard_map/ppermute | solution.py:551
  62.3 2.9 %grad_pre_x_sides.1.at_x = bf16[4,288,128]{2,1,0:T(8,128)(2,1)S(1)} custom-call(bf16[8,400,128]{2,1,0:T(8,128)(2,1)S(1)} %copy-done.2, bf16[2,400,128]{2,1,0:T(8,128)(2,1)S(1)} %collective-permute-done.before, bf16[2,400,128]{2,1,0:T(8,128)(2,1)S(1)} %collective-permute-done.1.after, bf16[1152,384]{1,0:T(8,128)(2,1)S(1)} %get-tuple-element.34.w_fwd, ...), custom_call_target="tpu_custom_call" | custom-call | flops 1019215872 | bytes 4194304 | tf_op jit(solution)/shard_map/grad_pre_x_sides/pallas_call | solution.py:292
  65.2 3.5 %collective-permute-done.3.right = bf16[12,112,128]{2,1,0:T(8,128)(2,1)S(1)} collective-permute-done((bf16[12,112,128]{2,1,0:T(8,128)(2,1)S(1)}, bf16[12,112,128]{2,1,0:T(8,128)(2,1)S(1)}, u32[]{:S(2)}, u32[]{:S(2)}) %collective-permute-start.3) | collective-permute-done | bytes 344096 | tf_op jit(solution)/shard_map/ppermute | solution.py:551
  68.7 12.6 %conv_both_ways.1 = (bf16[768,8,128]{2,1,0:T(8,128)(2,1)}, bf16[12,576,128]{2,1,0:T(8,128)(2,1)S(1)}, bf16[8,384,128]{2,1,0:T(8,128)(2,1)S(1)}) custom-call(s32[768]{0:T(1024)S(1)} %get-tuple-element.58.index, bf16[8,400,128]{2,1,0:T(8,128)(2,1)S(1)} %copy-done.2, bf16[2,400,128]{2,1,0:T(8,128)(2,1)S(1)} %collective-permute-done.before, ...), custom_call_target="tpu_custom_call" | custom-call | tf_op jit(solution)/shard_map/conv_both_ways/pallas_call | solution.py:417
  81.3 1.2 copy-done.5
  83.4 8.9 %all-to-all-start.1 = ((bf16[768,8,128]{2,1,0:T(8,128)(2,1)}), bf16[768,8,128]{2,1,0:T(8,128)(2,1)}, u32[]{:S(2)}, u32[]{:S(2)}) async-start(bf16[768,8,128]{2,1,0:T(8,128)(2,1)} %get-tuple-element.38), calls=%async_computation.1 | async-start | bytes 3145728 | tf_op jit(solution)/shard_map/all_to_all | solution.py:544
  92.3 8.3 %conv_weight_grad.1 = (f32[16,128,128]{2,1,0:T(8,128)}, bf16[16,128,128]{2,1,0:T(8,128)(2,1)}) custom-call(s32[1]{0:T(128)} %bitcast.7.half, bf16[12,576,128]{2,1,0:T(8,128)(2,1)} %copy-done.5, bf16[8,384,128]{2,1,0:T(8,128)(2,1)} %copy-done.6), custom_call_target="tpu_custom_call" | custom-call | flops 2717908992 | bytes 6291456 | tf_op jit(solution)/shard_map/conv_weight_grad/pallas_call | solution.py:468
  101.7 1.7 %collective-permute-done.4.got = bf16[16,128,128]{2,1,0:T(8,128)(2,1)S(1)} collective-permute-done((bf16[16,128,128]{2,1,0:T(8,128)(2,1)}, bf16[16,128,128]{2,1,0:T(8,128)(2,1)S(1)}, u32[]{:S(2)}, u32[]{:S(2)}) %collective-permute-start.4) | collective-permute-done | bytes 524320 | tf_op jit(solution)/shard_map/ppermute | solution.py:507
  104.2 2.3 %add_pair.1 = (f32[4,128,128]{2,1,0:T(8,128)}, bf16[4,128,128]{2,1,0:T(8,128)(2,1)}, bf16[4,128,128]{2,1,0:T(8,128)(2,1)}, bf16[4,128,128]{2,1,0:T(8,128)(2,1)}) custom-call(s32[1]{0:T(128)} %bitcast.6.me, f32[16,128,128]{2,1,0:T(8,128)} %get-tuple-element.42.keep, bf16[16,128,128]{2,1,0:T(8,128)(2,1)} %copy-done.9), custom_call_target="tpu_custom_call" | custom-call | tf_op jit(solution)/shard_map/add_pair/pallas_call | solution.py:492
  106.5 1.9 %collective-permute-start.7 = (bf16[4,128,128]{2,1,0:T(8,128)(2,1)}, bf16[4,128,128]{2,1,0:T(8,128)(2,1)S(1)}, u32[]{:S(2)}, u32[]{:S(2)}) collective-permute-start(bf16[4,128,128]{2,1,0:T(8,128)(2,1)} %get-tuple-element.47), channel_id=1, source_target_pairs={{0,6},{1,7},{2,0},{3,1},{4,2},{5,3},{6,4},{7,5},{8,14},{9,15},{10,... | collective-permute-start | bytes 393224 | tf_op jit(solution)/shard_map/ppermute | solution.py:511
  109.5 5.5 %collective-permute-done.7 = bf16[4,128,128]{2,1,0:T(8,128)(2,1)S(1)} collective-permute-done((bf16[4,128,128]{2,1,0:T(8,128)(2,1)}, bf16[4,128,128]{2,1,0:T(8,128)(2,1)S(1)}, u32[]{:S(2)}, u32[]{:S(2)}) %collective-permute-start.7) | collective-permute-done | bytes 131104 | tf_op jit(solution)/shard_map/ppermute | solution.py:511
  115.7 3.5 %collective-permute-done.5 = bf16[4,128,128]{2,1,0:T(8,128)(2,1)S(1)} collective-permute-done((bf16[4,128,128]{2,1,0:T(8,128)(2,1)}, bf16[4,128,128]{2,1,0:T(8,128)(2,1)S(1)}, u32[]{:S(2)}, u32[]{:S(2)}) %collective-permute-start.5) | collective-permute-done | bytes 131104 | tf_op jit(solution)/shard_map/ppermute | solution.py:511
  120.2 1.4 copy-done
  121.6 2.4 %stride_term.1 = (bf16[1536,128]{1,0:T(8,128)(2,1)S(1)}, bf16[512,128]{1,0:T(8,128)(2,1)S(1)}) custom-call(s32[192]{0:T(256)S(1)} %copy-done.4, bf16[768,8,128]{2,1,0:T(8,128)(2,1)} %all-to-all-done.1.came, bf16[1536,512]{1,0:T(8,128)(2,1)S(1)} %bitcast.33), custom_call_target="tpu_custom_call" | custom-call | tf_op jit(solution)/shard_map/stride_term/pallas_call | solution.py:532
  124.2 17.5 %all_to_all.20 = bf16[128,8,128]{2,1,0:T(8,128)(2,1)S(1)} all-to-all(bf16[128,8,128]{2,1,0:T(8,128)(2,1)S(1)} %copy.55), channel_id=1, replica_groups=mesh['gx'=16,'gy'=8] {'gx','gy'}, dimensions={0} | all-to-all | bytes 524288 | tf_op jit(solution)/shard_map/all_to_all | solution.py:544
  141.9 1.2 broadcast_in_dim.33
  143.1 4.3 %all-to-all-start.3 = ((bf16[128,36,128]{2,1,0:T(8,128)(2,1)}), bf16[128,36,128]{2,1,0:T(8,128)(2,1)S(1)}, u32[]{:S(2)}, u32[]{:S(2)}) async-start(bf16[128,36,128]{2,1,0:T(8,128)(2,1)} %broadcast_in_dim.33), calls=%async_computation.3 | async-start | bytes 2621440 | tf_op jit(solution)/shard_map/all_to_all | solution.py:544
  147.4 1.7 fusion
  149.2 20.0 %all-to-all-done.3 = bf16[128,36,128]{2,1,0:T(8,128)(2,1)S(1)} async-done(((bf16[128,36,128]{2,1,0:T(8,128)(2,1)}), bf16[128,36,128]{2,1,0:T(8,128)(2,1)S(1)}, u32[]{:S(2)}, u32[]{:S(2)}) %all-to-all-start.3) | async-done | bytes 1179680 | tf_op jit(solution)/shard_map/all_to_all | solution.py:544
  169.5 2.2 %copy.58 = f32[27,128,128]{2,1,0:T(8,128)} copy(f32[27,128,128]{2,0,1:T(8,128)S(1)} %multiply_bitcast_fusion) | data formatting | bytes 3538944
  (57 shorter events, 10.3 us)
Async XLA Ops:
  5.8 11.5 %copy-start.11 = (s32[768]{0:T(1024)S(1)}, s32[768]{0:T(1024)}, u32[]{:S(2)}) copy-start(s32[768]{0:T(1024)} %param.9) | copy-start | bytes 9220
  5.8 11.6 %copy-start.7 = (bf16[27,128,128]{2,1,0:T(8,128)(2,1)S(1)}, bf16[27,128,128]{2,1,0:T(8,128)(2,1)}, u32[]{:S(2)}) copy-start(bf16[27,128,128]{2,1,0:T(8,128)(2,1)} %param.11) | copy-start | bytes 2654212
  5.8 36.1 %all-to-all-start = ((bf16[768,8,128]{2,1,0:T(8,128)(2,1)}), bf16[768,8,128]{2,1,0:T(8,128)(2,1)S(1)}, u32[]{:S(2)}, u32[]{:S(2)}) async-start(bf16[768,8,128]{2,1,0:T(8,128)(2,1)} %get-tuple-element.28), calls=%async_computation | async-start | bytes 3145728 | tf_op jit(solution)/shard_map/all_to_all | solution.py:544
  19.4 2.3 %copy-start.10 = (s32[8,8,48]{2,1,0:T(8,128)S(1)}, s32[8,8,48]{2,1,0:T(8,128)}, u32[]{:S(2)}) copy-start(s32[8,8,48]{2,1,0:T(8,128)} %param.13) | copy-start | bytes 36868
  24.6 25.9 %copy-start.12 = (bf16[128,8]{0,1:T(8,128)(2,1)S(1)}, bf16[128,8]{0,1:T(8,128)(2,1)}, u32[]{:S(2)}) copy-start(bf16[128,8]{0,1:T(8,128)(2,1)} %param.12) | copy-start | bytes 6148
  41.9 0.8 copy-start.3
  46.0 0.9 copy-start.1
  46.9 9.6 %collective-permute-start = (bf16[2,400,128]{2,1,0:T(8,128)(2,1)}, bf16[2,400,128]{2,1,0:T(8,128)(2,1)S(1)}, u32[]{:S(2)}, u32[]{:S(2)}) collective-permute-start(bf16[2,400,128]{2,1,0:T(8,128)(2,1)} %get-tuple-element.32), channel_id=1, source_target_pairs={{0,8},{8,16},{16,24},{24,32},{32,40},{40,48},{48,56},{56,64},{64,7... | collective-permute-start | bytes 614408 | tf_op jit(solution)/shard_map/ppermute | solution.py:551
  49.2 7.2 %collective-permute-start.1 = (bf16[2,400,128]{2,1,0:T(8,128)(2,1)}, bf16[2,400,128]{2,1,0:T(8,128)(2,1)S(1)}, u32[]{:S(2)}, u32[]{:S(2)}) collective-permute-start(bf16[2,400,128]{2,1,0:T(8,128)(2,1)} %get-tuple-element.33), channel_id=1, source_target_pairs={{8,0},{16,8},{24,16},{32,24},{40,32},{48,40},{56,48},{64,56},{72,6... | collective-permute-start | bytes 614408 | tf_op jit(solution)/shard_map/ppermute | solution.py:551
  50.7 1.2 copy-start.2
  56.5 8.7 %collective-permute-start.2 = (bf16[12,112,128]{2,1,0:T(8,128)(2,1)S(1)}, bf16[12,112,128]{2,1,0:T(8,128)(2,1)S(1)}, u32[]{:S(2)}, u32[]{:S(2)}) collective-permute-start(bf16[12,112,128]{2,1,0:T(8,128)(2,1)S(1)} %get-tuple-element.35), channel_id=1, source_target_pairs={{0,1},{1,2},{2,3},{3,4},{4,5},{5,6},{6,7},{8,9},{9,10},{10,11},{11... | collective-permute-start | bytes 1032200 | tf_op jit(solution)/shard_map/ppermute | solution.py:551
  60.1 8.6 %collective-permute-start.3 = (bf16[12,112,128]{2,1,0:T(8,128)(2,1)S(1)}, bf16[12,112,128]{2,1,0:T(8,128)(2,1)S(1)}, u32[]{:S(2)}, u32[]{:S(2)}) collective-permute-start(bf16[12,112,128]{2,1,0:T(8,128)(2,1)S(1)} %get-tuple-element.36), channel_id=1, source_target_pairs={{1,0},{2,1},{3,2},{4,3},{5,4},{6,5},{7,6},{9,8},{10,9},{11,10},{12... | collective-permute-start | bytes 1032200 | tf_op jit(solution)/shard_map/ppermute | solution.py:551
  81.3 1.2 copy-start.5
  82.5 0.9 copy-start.6
  83.4 36.8 %all-to-all-start.1 = ((bf16[768,8,128]{2,1,0:T(8,128)(2,1)}), bf16[768,8,128]{2,1,0:T(8,128)(2,1)}, u32[]{:S(2)}, u32[]{:S(2)}) async-start(bf16[768,8,128]{2,1,0:T(8,128)(2,1)} %get-tuple-element.38), calls=%async_computation.1 | async-start | bytes 3145728 | tf_op jit(solution)/shard_map/all_to_all | solution.py:544
  100.6 19.6 %copy-start.4 = (s32[192]{0:T(256)S(1)}, s32[192]{0:T(256)}, u32[]{:S(2)}) copy-start(s32[192]{0:T(256)} %get-tuple-element.27.place) | copy-start | bytes 2308
  100.6 2.9 %collective-permute-start.4 = (bf16[16,128,128]{2,1,0:T(8,128)(2,1)}, bf16[16,128,128]{2,1,0:T(8,128)(2,1)S(1)}, u32[]{:S(2)}, u32[]{:S(2)}) collective-permute-start(bf16[16,128,128]{2,1,0:T(8,128)(2,1)} %get-tuple-element.43), channel_id=1, source_target_pairs={{0,1},{1,0},{2,3},{3,2},{4,5},{5,4},{6,7},{7,6},{8,9},{9,8},{10,11... | collective-permute-start | bytes 1572872 | tf_op jit(solution)/shard_map/ppermute | solution.py:507
  103.4 0.8 copy-start.9
  106.5 8.5 %collective-permute-start.7 = (bf16[4,128,128]{2,1,0:T(8,128)(2,1)}, bf16[4,128,128]{2,1,0:T(8,128)(2,1)S(1)}, u32[]{:S(2)}, u32[]{:S(2)}) collective-permute-start(bf16[4,128,128]{2,1,0:T(8,128)(2,1)} %get-tuple-element.47), channel_id=1, source_target_pairs={{0,6},{1,7},{2,0},{3,1},{4,2},{5,3},{6,4},{7,5},{8,14},{9,15},{10,... | collective-permute-start | bytes 393224 | tf_op jit(solution)/shard_map/ppermute | solution.py:511
  108.4 7.3 %collective-permute-start.6 = (bf16[4,128,128]{2,1,0:T(8,128)(2,1)}, bf16[4,128,128]{2,1,0:T(8,128)(2,1)S(1)}, u32[]{:S(2)}, u32[]{:S(2)}) collective-permute-start(bf16[4,128,128]{2,1,0:T(8,128)(2,1)} %get-tuple-element.46), channel_id=1, source_target_pairs={{0,4},{1,5},{2,6},{3,7},{4,0},{5,1},{6,2},{7,3},{8,12},{9,13},{10,... | collective-permute-start | bytes 393224 | tf_op jit(solution)/shard_map/ppermute | solution.py:511
  108.9 10.2 %collective-permute-start.5 = (bf16[4,128,128]{2,1,0:T(8,128)(2,1)}, bf16[4,128,128]{2,1,0:T(8,128)(2,1)S(1)}, u32[]{:S(2)}, u32[]{:S(2)}) collective-permute-start(bf16[4,128,128]{2,1,0:T(8,128)(2,1)} %get-tuple-element.45), channel_id=1, source_target_pairs={{0,2},{1,3},{2,4},{3,5},{4,6},{5,7},{6,0},{7,1},{8,10},{9,11},{10,... | collective-permute-start | bytes 393224 | tf_op jit(solution)/shard_map/ppermute | solution.py:511
  120.2 1.4 copy-start
  143.1 4.3 %copy-start.8 = (bf16[512,128]{1,0:T(8,128)(2,1)S(1)}, bf16[512,128]{1,0:T(8,128)(2,1)}, u32[]{:S(2)}) copy-start(bf16[512,128]{1,0:T(8,128)(2,1)} %w_hbm.1) | copy-start | bytes 393220
  143.1 26.1 %all-to-all-start.3 = ((bf16[128,36,128]{2,1,0:T(8,128)(2,1)}), bf16[128,36,128]{2,1,0:T(8,128)(2,1)S(1)}, u32[]{:S(2)}, u32[]{:S(2)}) async-start(bf16[128,36,128]{2,1,0:T(8,128)(2,1)} %broadcast_in_dim.33), calls=%async_computation.3 | async-start | bytes 2621440 | tf_op jit(solution)/shard_map/all_to_all | solution.py:544

commit v2 on v1

--- a/solution.py
+++ b/solution.py
@@ -166,7 +166,7 @@
         in_specs=[smem(), whole(arrived.shape), whole(order.shape), whole(code.shape)],
         out_specs=tuple(whole(s) for s in shapes),
         scratch_shapes=[pltpu.VMEM((BRICKS + 8, CELLS, CH), F32)],
-        compiler_params=VMEM,
+        compiler_params=ALL_VMEM,
         name="land_bricks",
     )(index, arrived, order, code)
 
@@ -302,15 +302,15 @@
 
 def core_kernel(
     index, slab, before, after, left, right, inside, at_x, w_fwd, w_bwd, head, head_t, order_t,
-    back_hbm, grid_hbm, own_hbm, low, high, codes, grad, coarse, held, back, sems,
+    back_hbm, kept_hbm, low, high, codes, grad, coarse, held, back, sems,
 ):
     middle = pl.ds(SIDE, ROWS)
     pairs = (
-        (slab.at[:, pl.ds(0, ROWS)], grid_hbm.at[pl.ds(2, SX), middle]),
-        (before.at[:, pl.ds(0, ROWS)], grid_hbm.at[pl.ds(0, 2), middle]),
-        (after.at[:, pl.ds(0, ROWS)], grid_hbm.at[pl.ds(2 + SX, 2), middle]),
-        (left.at[:, pl.ds(0, SIDE)], grid_hbm.at[:, pl.ds(0, SIDE)]),
-        (right.at[:, pl.ds(0, SIDE)], grid_hbm.at[:, pl.ds(SIDE + ROWS, SIDE)]),
+        (slab.at[:, pl.ds(0, ROWS)], kept_hbm.at[pl.ds(2, SX), middle]),
+        (before.at[:, pl.ds(0, ROWS)], kept_hbm.at[pl.ds(0, 2), middle]),
+        (after.at[:, pl.ds(0, ROWS)], kept_hbm.at[pl.ds(2 + SX, 2), middle]),
+        (left.at[:, pl.ds(0, SIDE)], kept_hbm.at[pl.ds(0, FX), pl.ds(0, SIDE)]),
+        (right.at[:, pl.ds(0, SIDE)], kept_hbm.at[pl.ds(0, FX), pl.ds(SIDE + ROWS, SIDE)]),
     )
     copies = [pltpu.make_async_copy(a, b, sems.at[i]) for i, (a, b) in enumerate(pairs)]
     for copy in copies:
@@ -355,7 +355,9 @@
 
     lax.fori_loop(0, SX // 2 + 1, forward, 0, unroll=5)
     out = pltpu.make_async_copy(
-        grad.at[pl.ds(1, SX), pl.ds(SZ, ROWS)], own_hbm, sems.at[len(pairs)]
+        grad.at[pl.ds(1, SX), pl.ds(SZ, ROWS)],
+        kept_hbm.at[pl.ds(FX, SX), pl.ds(0, ROWS)],
+        sems.at[len(pairs)],
     )
     out.start()
     copies.append(out)
@@ -413,12 +415,12 @@
     arrays = (
         slab, before, after, left, right, inside, at_x, w_fwd, w_bwd, head, head_t, order_t
     )
-    shapes = ((index.shape[0], CELLS, CH), (FX, FY * SZ, CH), (SX, ROWS, CH))
+    shapes = ((index.shape[0], CELLS, CH), (FX + SX, FY * SZ, CH))
     return pl.pallas_call(
         core_kernel,
         out_shape=tuple(jax.ShapeDtypeStruct(s, BF) for s in shapes),
         in_specs=[smem()] + [whole(a.shape) for a in arrays],
-        out_specs=(hbm(),) * 3,
+        out_specs=(hbm(),) * 2,
         scratch_shapes=[
             pltpu.VMEM((FX, 2 * SIDE, CH), BF),
             pltpu.VMEM((FX, 2 * SIDE, CH), BF),
@@ -434,19 +436,20 @@
     )(index, *arrays)
 
 
-def weights_kernel(half, grid, grad, keep, give, total, taps_out):
+def weights_kernel(half, kept, keep, give, total, taps_out):
     z_own = iota((SY, SZ, CH), 1).reshape(ROWS, CH)
     total[...] = jnp.zeros_like(total)
 
     def add(x, carry):
-        mid = grad[x].astype(F32)
+        here = kept[FX + x, :ROWS, :]
+        mid = here.astype(F32)
         grads = jnp.concatenate(
-            [shifted(mid, z_own, -1).astype(BF), grad[x], shifted(mid, z_own, 1).astype(BF)],
+            [shifted(mid, z_own, -1).astype(BF), here, shifted(mid, z_own, 1).astype(BF)],
             axis=1,
         )
         for e in range(3):
             taps = jnp.concatenate(
-                [grid[x + 1 + e, (1 + f) * SZ : (1 + f) * SZ + ROWS, :] for f in range(3)], axis=1
+                [kept[x + 1 + e, (1 + f) * SZ : (1 + f) * SZ + ROWS, :] for f in range(3)], axis=1
             )
             total[e] += lax.dot_general(
                 taps, grads, (((0,), (0,)), ((), ())), preferred_element_type=F32
@@ -463,32 +466,37 @@
     give[...] = taps_out[pl.ds(16 * (1 - mine), 16)].astype(BF)
 
 
-def weights(half, grid, grad):
+def weights(half, kept):
     shape = (16, CH, CH)
     return pl.pallas_call(
         weights_kernel,
         out_shape=(jax.ShapeDtypeStruct(shape, F32), jax.ShapeDtypeStruct(shape, BF)),
-        in_specs=[smem(), whole(grid.shape), whole(grad.shape)],
+        in_specs=[smem(), whole(kept.shape)],
         out_specs=(whole(shape),) * 2,
         scratch_shapes=[pltpu.VMEM((3, 3 * CH, 3 * CH), F32), pltpu.VMEM((32, CH, CH), F32)],
-        compiler_params=ALL_VMEM,
+        compiler_params=VMEM,
         cost_estimate=pl.CostEstimate(
             flops=2 * 27 * CH * CH * SX * ROWS, bytes_accessed=6 * 2**20, transcendentals=0
         ),
         name="conv_weight_grad",
-    )(half, grid, grad)
-
-
-def pair_kernel(me, keep, got, mine, *others):
-    share = mine.shape[0]
-    for by, out in enumerate((mine,) + others):
-        at = pl.ds(share * lax.rem(me[0] + by, len(others) + 1), share)
-        out[...] = (keep[at] + got[at].astype(F32)).astype(out.dtype)
-
-
-def add_pair(y, keep, got, ring):
-    shape = (keep.shape[0] // ring, CH, CH)
+    )(half, kept)
+
+
+def pair_kernel(me, keep, got, *outs):
+    both = keep[...] + got[...].astype(F32).reshape(keep.shape)
+    turned = jnp.concatenate([both[:, :, 4:], both[:, :, :4]], axis=2)
+    for by, out in enumerate(outs):
+        y = lax.rem(me[0] + by, len(outs))
+        part = jnp.where(y % 2 == 0, both, turned)
+        part = jnp.where(y < 2, part[:, 0], part[:, 1])
+        out[...] = part[:, :4].astype(out.dtype)
+
+
+def add_pair(y, keep, got, ring, devs):
+    shape = (devs, 4, CH)
     kinds = (F32,) + (BF,) * (ring - 1)
+    keep = keep.reshape(devs, 2, 8, CH)
+    got = got.reshape(devs, 16, CH)
     return pl.pallas_call(
         pair_kernel,
         out_shape=tuple(jax.ShapeDtypeStruct(shape, kind) for kind in kinds),
@@ -499,17 +507,17 @@
     )(y, keep, got)
 
 
-def sum_over_gy(keep, give):
+def sum_over_gy(keep, give, devs):
     me = lax.axis_index("gy")
     y = me // 2
     peers = lax.axis_size("gy")
     ring = peers // 2
     got = lax.ppermute(give, "gy", [(i, i ^ 1) for i in range(peers)])
-    total, *others = add_pair(y.astype(jnp.int32).reshape(1), keep, got, ring)
-    for by, part in enumerate(others, 1):
-        perm = [(i, (i + 2 * by) % peers) for i in range(peers)]
-        total = total + lax.ppermute(part, "gy", perm).astype(F32)
-    return total.transpose(1, 0, 2).astype(BF)
+    parts = add_pair(y.astype(jnp.int32).reshape(1), keep, got, ring, devs)
+    perms = [[(i, (i + 2 * by) % peers) for i in range(peers)] for by in range(ring)]
+    return parts[:1] + tuple(
+        lax.ppermute(part, "gy", perm) for part, perm in zip(parts[1:], perms[1:])
+    )
 
 
 def last_kernel(place, came, feats, mine, stride, rows):
@@ -535,7 +543,7 @@
         in_specs=[smem(), whole(came.shape), whole(feats.shape)],
         out_specs=tuple(whole(s) for s in shapes),
         scratch_shapes=[pltpu.VMEM((place.shape[0], CELLS, CH), F32)],
-        compiler_params=VMEM,
+        compiler_params=ALL_VMEM,
         name="stride_term",
     )(place, came, feats)
 
@@ -589,7 +597,7 @@
     up, down = sides(slab, before, after, inside)
     left, right = both_ways(down, up, "gy")
     at_x = x_sides(slab, before, after, w_fwd, head, head.T)
-    returned, grid, grad = core(
+    returned, kept = core(
         jnp.minimum(index, BRICKS - 1),
         slab,
         before,
@@ -606,21 +614,38 @@
     )
     came = to_all(returned)
     half = (lax.axis_index("gy") % 2).astype(jnp.int32).reshape(1)
-    conv = sum_over_gy(*weights(half, grid, grad))
+    terms = sum_over_gy(*weights(half, kept), devs)
     mine, stride = last(came, place, feats)
+    terms, stride = lax.optimization_barrier((terms, stride))
+    conv = sum(term.astype(F32) for term in terms).astype(BF)
     share = in_width // devs
+    rows = conv.shape[1]
     terms = to_all(jnp.concatenate([conv, stride.reshape(devs, share, CH)], axis=1))
     grad_fine = lax.dot_general(
         mine, w_stride, (((1,), (1,)), ((), ())), preferred_element_type=F32
     ).astype(BF)
-    terms = terms.astype(F32).reshape(lax.axis_size("gx"), lax.axis_size("gy"), 4 + share, CH)
+    terms = terms.astype(F32).reshape(lax.axis_size("gx"), -1, 2, rows + share, CH)
     by_part = jnp.sum(terms, axis=0)
-    conv_sum = by_part[:, :4].reshape(-1, 2, 4, CH).transpose(1, 0, 2, 3).reshape(32, CH)
-    block = jnp.concatenate([conv_sum, jnp.sum(by_part[:, 4:], axis=0)], axis=0).astype(BF)
-    sums = to_all(jnp.broadcast_to(block[None], (devs,) + block.shape))
+    conv_sum = by_part[:, :, :rows].transpose(1, 0, 2, 3).reshape(2, -1, CH)
+    stride_sum = jnp.sum(by_part[:, :, rows:], axis=(0, 1))
+    block = jnp.concatenate(
+        [conv_sum, jnp.broadcast_to(stride_sum, (2,) + stride_sum.shape)], axis=1
+    ).astype(BF)
+    block, grad_fine = lax.optimization_barrier((block, grad_fine))
+    sums = to_all(jnp.broadcast_to(block, (devs // 2,) + block.shape).reshape(devs, -1, CH))
     scale = 1.0 / math.sqrt(per_dev * devs * cells)
-    grad_conv = sums[:, :27].transpose(1, 0, 2).astype(F32) * scale
-    grad_stride = sums[:, 32:].reshape(in_width, CH).astype(F32) * scale
+    mine = sums[:, :-share].reshape(-1, CH)
+    swap = [(i, i ^ 1) for i in range(lax.axis_size("gy"))]
+    other = lax.ppermute(mine, "gy", swap)
+    first_core = half[0] == 0
+    grad_conv = jnp.concatenate(
+        [
+            jnp.where(first_core, mine, other),
+            jnp.where(first_core, other, mine)[: 27 * CH - mine.shape[0]],
+        ],
+        axis=0,
+    ).astype(F32).reshape(27, CH, CH) * scale
+    grad_stride = sums[:, -share:].reshape(in_width, CH).astype(F32) * scale
     return (
         grad_fine.reshape(per_dev, cells, in_width),
         grad_stride,

time: 173 us -> 164 us (0.948)
  waiting for transfers between devices: 52.3 us -> 41 us
  local copies, waits for them, and re-layouts: 17.6 us -> 9.83 us
  other arithmetic: 2.59 us -> 6.62 us
  starting transfers between devices: 38.2 us -> 41.8 us
  blocking collectives: 17.5 us -> 20.3 us
    ppermute x3 -> x4, waiting for transfers between devices: 9.68 us -> 0.79 us  [the longest x1 0.78 us: per_device(): other = lax.ppermute(mine, 'gy', swap)]
    unnamed x27 -> x28, local copies, waits for them, and re-layouts: 9.34 us -> 5.7 us
    pallas_call x1, Pallas kernels: 8.29 us -> 5.46 us  [weights(): pl.pallas_call(weights_kernel, out_shape=(jax.ShapeDtypeStruct(shape, F32...]
    all_to_all x1, blocking collectives: 17.5 us -> 20.3 us  [to_all(): lax.all_to_all(buffer, ('gx', 'gy'), split_axis=0, concat_axis=0, tiled=T...]
    ppermute x3 -> x4, starting transfers between devices: 3 us -> 5.51 us  [the longest x3 4.21 us: sum_over_gy(): lax.ppermute(part, 'gy', perm)]
    reshape x2, local copies, waits for them, and re-layouts: 3.77 us -> 1.61 us  [per_device(): taps = w_conv.reshape(9, 3, CH, CH)]
    all_to_all x3, starting transfers between devices: 24.7 us -> 26.6 us  [to_all(): lax.all_to_all(buffer, ('gx', 'gy'), split_axis=0, concat_axis=0, tiled=T...]
    concatenate x1, other arithmetic: 0.03 us -> 1.78 us  [per_device(): jnp.concatenate([conv, stride.reshape(devs, share, CH)], axis=1)]
  transfers between devices with their start and end apart: 11 -> 12, of which waited for: 7 -> 6; matrix products, arithmetic and copies ran while one was open for 6% -> 5% of each run, Pallas kernels for 10% -> 12%
where the time goes in v2:
time: 164 us; the launch traced here: 163 us
  starting transfers between devices  41.8 us (25%)
  Pallas kernels  41 us (25%)
  waiting for transfers between devices  41 us (25%)
  blocking collectives  20.3 us (12%)
  local copies, waits for them, and re-layouts  9.83 us (6%)
  other arithmetic  6.62 us (4%)
  matrix products  1.71 us (1%)
    all_to_all x3, waiting for transfers between devices, to_all(): lax.all_to_all(buffer, ('gx', 'gy'), split_axis=0, concat_axis=0, tiled=T...  35.7 us
    all_to_all x3, starting transfers between devices, to_all(): lax.all_to_all(buffer, ('gx', 'gy'), split_axis=0, concat_axis=0, tiled=T...  26.6 us
    all_to_all x1, blocking collectives, to_all(): lax.all_to_all(buffer, ('gx', 'gy'), split_axis=0, concat_axis=0, tiled=T...  20.3 us
    pallas_call x1, Pallas kernels, core(): pl.pallas_call(core_kernel, out_shape=tuple((jax.ShapeDtypeStruct(s, BF)...  12.5 us
    ppermute x4, starting transfers between devices, both_ways(): return (lax.ppermute(last_part, axis, up), lax.ppermute(first, axis, down))  8.61 us
    unnamed x28, local copies, waits for them, and re-layouts  5.7 us
    pallas_call x1, Pallas kernels, weights(): pl.pallas_call(weights_kernel, out_shape=(jax.ShapeDtypeStruct(shape, F32...  5.46 us
    pallas_call x1, Pallas kernels, send(): pl.pallas_call(functools.partial(send_kernel, cap), out_shape=(jax.ShapeD...  5.15 us
  transfers between devices with their start and end apart: 12, of which 6 were waited for; matrix products, arithmetic and copies ran while one was open for 5% of the time, Pallas kernels for 12%

profile of v2, /device:TPU:1, one launch (start us, length us, event | category | flops | bytes accessed | tf_op | source)
XLA Modules:
  0.0 163.2 jit_solution(2765735085924431786)
XLA Ops:
  0.6 5.2 %send_bricks.1 = (bf16[768,8,128]{2,1,0:T(8,128)(2,1)}, s32[192]{0:T(256)}) custom-call(s32[192]{0:T(256)} %owner_hbm.1, bf16[1536,512]{1,0:T(8,128)(2,1)} %bitcast.33, bf16[512,128]{1,0:T(8,128)(2,1)} %w_hbm.1), custom_call_target="tpu_custom_call" | custom-call | tf_op jit(solution)/shard_map/send_bricks/pallas_call | solution.py:109
  5.8 11.9 %all-to-all-start = ((bf16[768,8,128]{2,1,0:T(8,128)(2,1)}), bf16[768,8,128]{2,1,0:T(8,128)(2,1)}, u32[]{:S(2)}, u32[]{:S(2)}) async-start(bf16[768,8,128]{2,1,0:T(8,128)(2,1)} %get-tuple-element.32), calls=%async_computation | async-start | bytes 3145728 | tf_op jit(solution)/shard_map/all_to_all | solution.py:552
  22.1 1.2 copy_bitcast_fusion
  23.3 18.7 %all-to-all-done.arrived = bf16[768,8,128]{2,1,0:T(8,128)(2,1)} async-done(((bf16[768,8,128]{2,1,0:T(8,128)(2,1)}), bf16[768,8,128]{2,1,0:T(8,128)(2,1)}, u32[]{:S(2)}, u32[]{:S(2)}) %all-to-all-start) | async-done | bytes 1572896 | tf_op jit(solution)/shard_map/all_to_all | solution.py:552
  42.0 4.5 %land_bricks.1 = (bf16[8,400,128]{2,1,0:T(8,128)(2,1)}, bf16[2,400,128]{2,1,0:T(8,128)(2,1)}, bf16[2,400,128]{2,1,0:T(8,128)(2,1)}) custom-call(s32[768]{0:T(1024)} %get-tuple-element.62.index, bf16[768,8,128]{2,1,0:T(8,128)(2,1)} %all-to-all-done.arrived, bf16[192,192]{1,0:T(8,128)(2,1)} %get-tuple-element.64.order, bf16[8,16,128]{2,1,0:T(8,128)(2,1)} %pad.8.code), custom_call_target="tpu_custom_call" | custom-call | tf_op jit(solution)/shard_map/land_bricks/pallas_call | solution.py:163
  46.5 2.3 %collective-permute-start = (bf16[2,400,128]{2,1,0:T(8,128)(2,1)}, bf16[2,400,128]{2,1,0:T(8,128)(2,1)S(1)}, u32[]{:S(2)}, u32[]{:S(2)}) collective-permute-start(bf16[2,400,128]{2,1,0:T(8,128)(2,1)} %get-tuple-element.37), channel_id=1, source_target_pairs={{0,8},{8,16},{16,24},{24,32},{32,40},{40,48},{48,56},{56,64},{64,7... | collective-permute-start | bytes 614408 | tf_op jit(solution)/shard_map/ppermute | solution.py:559
  48.8 1.3 collective-permute-start.1
  51.0 1.2 copy-done
  52.2 1.1 copy-done.2
  53.3 4.5 %grad_pre_inside.1.inside = bf16[6,288,128]{2,1,0:T(8,128)(2,1)S(1)} custom-call(bf16[8,400,128]{2,1,0:T(8,128)(2,1)S(1)} %copy-done.2, bf16[1152,384]{1,0:T(8,128)(2,1)S(1)} %copy-done, bf16[128,128]{1,0:T(8,128)(2,1)S(1)} %copy.33.head, bf16[128,128]{1,0:T(8,128)(2,1)S(1)} %get-tuple-element.66.head_t), custom_call_target="tpu_custom_call" | custom-call | flops 1528823808 | bytes 4194304 | tf_op jit(solution)/shard_map/grad_pre_inside/pallas_call | solution.py:261
  58.0 2.2 %collective-permute-start.2 = (bf16[12,112,128]{2,1,0:T(8,128)(2,1)S(1)}, bf16[12,112,128]{2,1,0:T(8,128)(2,1)S(1)}, u32[]{:S(2)}, u32[]{:S(2)}) collective-permute-start(bf16[12,112,128]{2,1,0:T(8,128)(2,1)S(1)} %get-tuple-element.40), channel_id=1, source_target_pairs={{0,1},{1,2},{2,3},{3,4},{4,5},{5,6},{6,7},{8,9},{9,10},{10,11},{11... | collective-permute-start | bytes 1032200 | tf_op jit(solution)/shard_map/ppermute | solution.py:559
  60.2 2.8 %collective-permute-start.3 = (bf16[12,112,128]{2,1,0:T(8,128)(2,1)S(1)}, bf16[12,112,128]{2,1,0:T(8,128)(2,1)S(1)}, u32[]{:S(2)}, u32[]{:S(2)}) collective-permute-start(bf16[12,112,128]{2,1,0:T(8,128)(2,1)S(1)} %get-tuple-element.41), channel_id=1, source_target_pairs={{1,0},{2,1},{3,2},{4,3},{5,4},{6,5},{7,6},{9,8},{10,9},{11,10},{12... | collective-permute-start | bytes 1032200 | tf_op jit(solution)/shard_map/ppermute | solution.py:559
  63.0 2.8 %grad_pre_x_sides.1.at_x = bf16[4,288,128]{2,1,0:T(8,128)(2,1)S(1)} custom-call(bf16[8,400,128]{2,1,0:T(8,128)(2,1)S(1)} %copy-done.2, bf16[2,400,128]{2,1,0:T(8,128)(2,1)S(1)} %collective-permute-done.before, bf16[2,400,128]{2,1,0:T(8,128)(2,1)S(1)} %collective-permute-done.1.after, bf16[1152,384]{1,0:T(8,128)(2,1)S(1)} %copy-done.1, ...), custom_call_target="tpu_custom_call" | custom-call | flops 1019215872 | bytes 4194304 | tf_op jit(solution)/shard_map/grad_pre_x_sides/pallas_call | solution.py:292
  65.8 2.9 %collective-permute-done.3.right = bf16[12,112,128]{2,1,0:T(8,128)(2,1)S(1)} collective-permute-done((bf16[12,112,128]{2,1,0:T(8,128)(2,1)S(1)}, bf16[12,112,128]{2,1,0:T(8,128)(2,1)S(1)}, u32[]{:S(2)}, u32[]{:S(2)}) %collective-permute-start.3) | collective-permute-done | bytes 344096 | tf_op jit(solution)/shard_map/ppermute | solution.py:559
  68.7 12.5 %conv_both_ways.1 = (bf16[768,8,128]{2,1,0:T(8,128)(2,1)}, bf16[20,576,128]{2,1,0:T(8,128)(2,1)S(1)}) custom-call(s32[768]{0:T(1024)S(1)} %copy-done.4, bf16[8,400,128]{2,1,0:T(8,128)(2,1)S(1)} %copy-done.2, bf16[2,400,128]{2,1,0:T(8,128)(2,1)S(1)} %collective-permute-done.before, bf16[2,400,128]{2,1,0:T(8,128)(2,1)S(1)} %collective-permute-done.1.after, ...), custom_call_target="tpu_custom_call" | custom-call | tf_op jit(solution)/shard_map/conv_both_ways/pallas_call | solution.py:419
  81.3 1.6 copy-done.5
  82.8 9.1 %all-to-all-start.1 = ((bf16[768,8,128]{2,1,0:T(8,128)(2,1)}), bf16[768,8,128]{2,1,0:T(8,128)(2,1)}, u32[]{:S(2)}, u32[]{:S(2)}) async-start(bf16[768,8,128]{2,1,0:T(8,128)(2,1)} %get-tuple-element.51), calls=%async_computation.1 | async-start | bytes 3145728 | tf_op jit(solution)/shard_map/all_to_all | solution.py:552
  92.0 5.5 %conv_weight_grad.1 = (f32[16,128,128]{2,1,0:T(8,128)S(1)}, bf16[16,128,128]{2,1,0:T(8,128)(2,1)S(1)}) custom-call(s32[1]{0:T(128)} %bitcast.1.half, bf16[20,576,128]{2,1,0:T(8,128)(2,1)S(1)} %copy-done.6), custom_call_target="tpu_custom_call" | custom-call | flops 2717908992 | bytes 6291456 | tf_op jit(solution)/shard_map/conv_weight_grad/pallas_call | solution.py:471
  98.4 1.1 collective-permute-start.4
  99.6 1.5 collective-permute-done.4
  101.9 2.5 %add_pair.1 = (f32[128,4,128]{2,1,0:T(4,128)}, bf16[128,4,128]{2,1,0:T(4,128)(2,1)}, bf16[128,4,128]{2,1,0:T(4,128)(2,1)}, bf16[128,4,128]{2,1,0:T(4,128)(2,1)}) custom-call(s32[1]{0:T(128)} %bitcast.me, f32[128,2,8,128]{3,2,1,0:T(8,128)} %bitcast.32, bf16[128,16,128]{2,1,0:T(8,128)(2,1)} %bitcast.45), custom_call_target="tpu_custom_call" | custom-call | tf_op jit(solution)/shard_map/add_pair/pallas_call | solution.py:500
  105.0 2.4 %collective-permute-start.6 = (bf16[128,4,128]{2,1,0:T(4,128)(2,1)}, bf16[128,4,128]{2,1,0:T(4,128)(2,1)S(1)}, u32[]{:S(2)}, u32[]{:S(2)}) collective-permute-start(bf16[128,4,128]{2,1,0:T(4,128)(2,1)} %get-tuple-element.48), channel_id=1, source_target_pairs={{0,4},{1,5},{2,6},{3,7},{4,0},{5,1},{6,2},{7,3},{8,12},{9,13},{10,... | collective-permute-start | bytes 393224 | tf_op jit(solution)/shard_map/ppermute | solution.py:519
  107.4 1.1 collective-permute-start.7
  108.6 7.7 %all-to-all-done.1.came = bf16[768,8,128]{2,1,0:T(8,128)(2,1)} async-done(((bf16[768,8,128]{2,1,0:T(8,128)(2,1)}), bf16[768,8,128]{2,1,0:T(8,128)(2,1)}, u32[]{:S(2)}, u32[]{:S(2)}) %all-to-all-start.1) | async-done | bytes 1572896 | tf_op jit(solution)/shard_map/all_to_all | solution.py:552
  116.3 3.5 %stride_term.1 = (bf16[1536,128]{1,0:T(8,128)(2,1)}, bf16[512,128]{1,0:T(8,128)(2,1)}) custom-call(s32[192]{0:T(256)} %get-tuple-element.50.place, bf16[768,8,128]{2,1,0:T(8,128)(2,1)} %all-to-all-done.1.came, bf16[1536,512]{1,0:T(8,128)(2,1)} %bitcast.34), custom_call_target="tpu_custom_call" | custom-call | tf_op jit(solution)/shard_map/stride_term/pallas_call | solution.py:540
  119.9 1.8 %pad_maximum_fusion = bf16[128,8,128]{2,1,0:T(8,128)(2,1)} fusion(bf16[128,4,128]{2,1,0:T(4,128)(2,1)} %bitcast.47, bf16[128,4,128]{2,1,0:T(4,128)(2,1)S(1)} %add_convert_fusion), kind=kLoop, calls=%fused_computation.23 | loop fusion | flops 524288 | bytes 524288 | tf_op jit(solution)/shard_map/concatenate | solution.py:623
  121.7 5.6 %all-to-all-start.2 = ((bf16[128,8,128]{2,1,0:T(8,128)(2,1)}), bf16[128,8,128]{2,1,0:T(8,128)(2,1)S(1)}, u32[]{:S(2)}, u32[]{:S(2)}) async-start(bf16[128,8,128]{2,1,0:T(8,128)(2,1)} %pad_maximum_fusion), calls=%async_computation.2 | async-start | bytes 524288 | tf_op jit(solution)/shard_map/all_to_all | solution.py:552
  127.3 1.7 %convolution_convert_fusion = bf16[1536,512]{1,0:T(8,128)(2,1)} fusion(bf16[1536,128]{1,0:T(8,128)(2,1)S(1)} %copy-done.10, bf16[512,128]{1,0:T(8,128)(2,1)S(1)} %copy-done.8), kind=kOutput, calls=%fused_computation | convolution fusion | flops 202113024 | bytes 2097152 | tf_op jit(solution)/shard_map/dot_general | solution.py:624
  129.0 9.4 %all-to-all-done.2 = bf16[128,8,128]{2,1,0:T(8,128)(2,1)S(1)} async-done(((bf16[128,8,128]{2,1,0:T(8,128)(2,1)}), bf16[128,8,128]{2,1,0:T(8,128)(2,1)S(1)}, u32[]{:S(2)}, u32[]{:S(2)}) %all-to-all-start.2) | async-done | bytes 262176 | tf_op jit(solution)/shard_map/all_to_all | solution.py:552
  138.6 20.3 %all_to_all.20 = bf16[128,20,128]{2,1,0:T(8,128)(2,1)S(1)} all-to-all(bf16[128,20,128]{2,1,0:T(8,128)(2,1)S(1)} %bitcast.41), channel_id=1, replica_groups=mesh['gx'=16,'gy'=8] {'gx','gy'}, dimensions={0} | all-to-all | bytes 1310720 | tf_op jit(solution)/shard_map/all_to_all | solution.py:552
  158.9 1.3 collective-permute-start.8
  161.9 1.3 convert_multiply_fusion
  (61 shorter events, 9.7 us)
Async XLA Ops:
  5.8 11.9 %copy-start.13 = (s32[768]{0:T(1024)S(1)}, s32[768]{0:T(1024)}, u32[]{:S(2)}) copy-start(s32[768]{0:T(1024)} %param.9) | copy-start | bytes 9220
  5.8 12.6 %copy-start.7 = (bf16[27,128,128]{2,1,0:T(8,128)(2,1)S(1)}, bf16[27,128,128]{2,1,0:T(8,128)(2,1)}, u32[]{:S(2)}) copy-start(bf16[27,128,128]{2,1,0:T(8,128)(2,1)} %param.11) | copy-start | bytes 2654212
  5.8 36.2 %all-to-all-start = ((bf16[768,8,128]{2,1,0:T(8,128)(2,1)}), bf16[768,8,128]{2,1,0:T(8,128)(2,1)}, u32[]{:S(2)}, u32[]{:S(2)}) async-start(bf16[768,8,128]{2,1,0:T(8,128)(2,1)} %get-tuple-element.32), calls=%async_computation | async-start | bytes 3145728 | tf_op jit(solution)/shard_map/all_to_all | solution.py:552
  19.1 1.4 copy-start.12
  46.5 11.4 %collective-permute-start = (bf16[2,400,128]{2,1,0:T(8,128)(2,1)}, bf16[2,400,128]{2,1,0:T(8,128)(2,1)S(1)}, u32[]{:S(2)}, u32[]{:S(2)}) collective-permute-start(bf16[2,400,128]{2,1,0:T(8,128)(2,1)} %get-tuple-element.37), channel_id=1, source_target_pairs={{0,8},{8,16},{16,24},{24,32},{32,40},{40,48},{48,56},{56,64},{64,7... | collective-permute-start | bytes 614408 | tf_op jit(solution)/shard_map/ppermute | solution.py:559
  48.8 9.1 %collective-permute-start.1 = (bf16[2,400,128]{2,1,0:T(8,128)(2,1)}, bf16[2,400,128]{2,1,0:T(8,128)(2,1)S(1)}, u32[]{:S(2)}, u32[]{:S(2)}) collective-permute-start(bf16[2,400,128]{2,1,0:T(8,128)(2,1)} %get-tuple-element.38), channel_id=1, source_target_pairs={{8,0},{16,8},{24,16},{32,24},{40,32},{48,40},{56,48},{64,56},{72,6... | collective-permute-start | bytes 614408 | tf_op jit(solution)/shard_map/ppermute | solution.py:559
  51.0 1.2 copy-start
  52.2 1.1 copy-start.2
  57.9 5.1 %copy-start.1 = (bf16[1152,384]{1,0:T(8,128)(2,1)S(1)}, bf16[1152,384]{1,0:T(8,128)(2,1)}, u32[]{:S(2)}) copy-start(bf16[1152,384]{1,0:T(8,128)(2,1)} %get-tuple-element.39.w_fwd) | copy-start | bytes 2654212
  58.0 7.8 %collective-permute-start.2 = (bf16[12,112,128]{2,1,0:T(8,128)(2,1)S(1)}, bf16[12,112,128]{2,1,0:T(8,128)(2,1)S(1)}, u32[]{:S(2)}, u32[]{:S(2)}) collective-permute-start(bf16[12,112,128]{2,1,0:T(8,128)(2,1)S(1)} %get-tuple-element.40), channel_id=1, source_target_pairs={{0,1},{1,2},{2,3},{3,4},{4,5},{5,6},{6,7},{8,9},{9,10},{10,11},{11... | collective-permute-start | bytes 1032200 | tf_op jit(solution)/shard_map/ppermute | solution.py:559
  60.2 8.6 %copy-start.4 = (s32[768]{0:T(1024)S(1)}, s32[768]{0:T(1024)}, u32[]{:S(2)}) copy-start(s32[768]{0:T(1024)} %get-tuple-element.61.index) | copy-start | bytes 9220
  60.2 8.6 %collective-permute-start.3 = (bf16[12,112,128]{2,1,0:T(8,128)(2,1)S(1)}, bf16[12,112,128]{2,1,0:T(8,128)(2,1)S(1)}, u32[]{:S(2)}, u32[]{:S(2)}) collective-permute-start(bf16[12,112,128]{2,1,0:T(8,128)(2,1)S(1)} %get-tuple-element.41), channel_id=1, source_target_pairs={{1,0},{2,1},{3,2},{4,3},{5,4},{6,5},{7,6},{9,8},{10,9},{11,10},{12... | collective-permute-start | bytes 1032200 | tf_op jit(solution)/shard_map/ppermute | solution.py:559
  81.3 1.6 copy-start.5
  82.8 9.2 %copy-start.6 = (bf16[20,576,128]{2,1,0:T(8,128)(2,1)S(1)}, bf16[20,576,128]{2,1,0:T(8,128)(2,1)}, u32[]{:S(2)}) copy-start(bf16[20,576,128]{2,1,0:T(8,128)(2,1)} %copy-done.5) | copy-start | bytes 8847364
  82.8 33.4 %all-to-all-start.1 = ((bf16[768,8,128]{2,1,0:T(8,128)(2,1)}), bf16[768,8,128]{2,1,0:T(8,128)(2,1)}, u32[]{:S(2)}, u32[]{:S(2)}) async-start(bf16[768,8,128]{2,1,0:T(8,128)(2,1)} %get-tuple-element.51), calls=%async_computation.1 | async-start | bytes 3145728 | tf_op jit(solution)/shard_map/all_to_all | solution.py:552
  97.5 1.0 copy-start.3
  98.4 2.7 %collective-permute-start.4 = (bf16[16,128,128]{2,1,0:T(8,128)(2,1)S(1)}, bf16[16,128,128]{2,1,0:T(8,128)(2,1)S(1)}, u32[]{:S(2)}, u32[]{:S(2)}) collective-permute-start(bf16[16,128,128]{2,1,0:T(8,128)(2,1)S(1)} %get-tuple-element.45), channel_id=1, source_target_pairs={{0,1},{1,0},{2,3},{3,2},{4,5},{5,4},{6,7},{7,6},{8,9},{9,8},{10,11... | collective-permute-start | bytes 1572872 | tf_op jit(solution)/shard_map/ppermute | solution.py:515
  101.1 0.8 copy-start.9
  104.4 15.4 %collective-permute-start.5 = (bf16[128,4,128]{2,1,0:T(4,128)(2,1)}, bf16[128,4,128]{2,1,0:T(4,128)(2,1)S(1)}, u32[]{:S(2)}, u32[]{:S(2)}) collective-permute-start(bf16[128,4,128]{2,1,0:T(4,128)(2,1)} %get-tuple-element.47), channel_id=1, source_target_pairs={{0,2},{1,3},{2,4},{3,5},{4,6},{5,7},{6,0},{7,1},{8,10},{9,11},{10,... | collective-permute-start | bytes 393224 | tf_op jit(solution)/shard_map/ppermute | solution.py:519
  105.0 14.8 %collective-permute-start.6 = (bf16[128,4,128]{2,1,0:T(4,128)(2,1)}, bf16[128,4,128]{2,1,0:T(4,128)(2,1)S(1)}, u32[]{:S(2)}, u32[]{:S(2)}) collective-permute-start(bf16[128,4,128]{2,1,0:T(4,128)(2,1)} %get-tuple-element.48), channel_id=1, source_target_pairs={{0,4},{1,5},{2,6},{3,7},{4,0},{5,1},{6,2},{7,3},{8,12},{9,13},{10,... | collective-permute-start | bytes 393224 | tf_op jit(solution)/shard_map/ppermute | solution.py:519
  107.4 12.4 %copy-start.11 = (f32[128,4,128]{2,1,0:T(4,128)S(1)}, f32[128,4,128]{2,1,0:T(4,128)}, u32[]{:S(2)}) copy-start(f32[128,4,128]{2,1,0:T(4,128)} %get-tuple-element.53) | copy-start | bytes 786436
  107.4 12.4 %collective-permute-start.7 = (bf16[128,4,128]{2,1,0:T(4,128)(2,1)}, bf16[128,4,128]{2,1,0:T(4,128)(2,1)S(1)}, u32[]{:S(2)}, u32[]{:S(2)}) collective-permute-start(bf16[128,4,128]{2,1,0:T(4,128)(2,1)} %get-tuple-element.49), channel_id=1, source_target_pairs={{0,6},{1,7},{2,0},{3,1},{4,2},{5,3},{6,4},{7,5},{8,14},{9,15},{10,... | collective-permute-start | bytes 393224 | tf_op jit(solution)/shard_map/ppermute | solution.py:519
  119.8 7.5 %copy-start.8 = (bf16[512,128]{1,0:T(8,128)(2,1)S(1)}, bf16[512,128]{1,0:T(8,128)(2,1)}, u32[]{:S(2)}) copy-start(bf16[512,128]{1,0:T(8,128)(2,1)} %w_hbm.1) | copy-start | bytes 393220
  119.8 7.5 %copy-start.10 = (bf16[1536,128]{1,0:T(8,128)(2,1)S(1)}, bf16[1536,128]{1,0:T(8,128)(2,1)}, u32[]{:S(2)}) copy-start(bf16[1536,128]{1,0:T(8,128)(2,1)} %get-tuple-element.58) | copy-start | bytes 1179652
  121.7 16.6 %all-to-all-start.2 = ((bf16[128,8,128]{2,1,0:T(8,128)(2,1)}), bf16[128,8,128]{2,1,0:T(8,128)(2,1)S(1)}, u32[]{:S(2)}, u32[]{:S(2)}) async-start(bf16[128,8,128]{2,1,0:T(8,128)(2,1)} %pad_maximum_fusion), calls=%async_computation.2 | async-start | bytes 524288 | tf_op jit(solution)/shard_map/all_to_all | solution.py:552
  158.9 2.8 %collective-permute-start.8 = (bf16[2048,128]{1,0:T(8,128)(2,1)S(1)}, bf16[2048,128]{1,0:T(8,128)(2,1)S(1)}, u32[]{:S(2)}, u32[]{:S(2)}) collective-permute-start(bf16[2048,128]{1,0:T(8,128)(2,1)S(1)} %bitcast.37), channel_id=1, source_target_pairs={{0,1},{1,0},{2,3},{3,2},{4,5},{5,4},{6,7},{7,6},{8,9},{9,8},{10,11... | collective-permute-start | bytes 1572872 | tf_op jit(solution)/shard_map/ppermute | solution.py:639

commit v3 on v2

--- a/solution.py
+++ b/solution.py
@@ -22,8 +22,10 @@
 CODE = 16
 SIDE = 2 * SZ
 BRICKS = 384
+KEPT = 84
 PARTS = 4
 VMEM = pltpu.CompilerParams(vmem_limit_bytes=24 * 1024 * 1024)
+MOST_VMEM = pltpu.CompilerParams(vmem_limit_bytes=48 * 1024 * 1024)
 ALL_VMEM = pltpu.CompilerParams(vmem_limit_bytes=63 * 1024 * 1024)
 BF = jnp.bfloat16
 F32 = jnp.float32
@@ -88,10 +90,10 @@
     for i in range(PARTS):
         copies[2 + i].wait()
         vals = matmul(feats[i * part : (i + 1) * part, :], w_stride[...])
-        rows[i * bricks : (i + 1) * bricks] = vals.reshape(bricks, CELLS, CH)
+        rows[i * bricks : (i + 1) * bricks] = vals.reshape(bricks, CELLS, CH).astype(BF)
 
     def put(i, c):
-        buf[place[i]] = rows[i].astype(BF)
+        buf[place[i]] = rows[i]
         return c
 
     lax.fori_loop(0, per_dev, put, 0, unroll=8)
@@ -118,7 +120,7 @@
             pltpu.SMEM((per_dev,), jnp.int32),
             pltpu.VMEM(feats.shape, BF),
             pltpu.VMEM(w_stride.shape, BF),
-            pltpu.VMEM((per_dev, CELLS, CH), F32),
+            pltpu.VMEM((per_dev, CELLS, CH), BF),
             pltpu.VMEM((devs * cap, CELLS, CH), BF),
             pltpu.SMEM((devs,), jnp.int32),
             pltpu.SemaphoreType.DMA((2 + PARTS,)),
@@ -139,14 +141,14 @@
     held[...] = jnp.zeros_like(held)
 
     def put(j, c):
-        held[index[j]] = arrived[j].astype(F32)
+        held[index[j]] = arrived[j]
         return c
 
     lax.fori_loop(0, index.shape[0], put, 0, unroll=8)
     for big_x in range(SX // 2):
         for big_y in range(SY // 2):
             start = (big_x * (SY // 2) + big_y) * (SZ // 2)
-            block = held[start : start + SZ // 2].reshape(4 * SZ, CH).astype(BF)
+            block = held[start : start + SZ // 2].astype(F32).reshape(4 * SZ, CH).astype(BF)
             moved = matmul(order[...], block).astype(BF)
             for i in range(2):
                 for l in range(2):
@@ -165,7 +167,7 @@
         out_shape=tuple(jax.ShapeDtypeStruct(s, BF) for s in shapes),
         in_specs=[smem(), whole(arrived.shape), whole(order.shape), whole(code.shape)],
         out_specs=tuple(whole(s) for s in shapes),
-        scratch_shapes=[pltpu.VMEM((BRICKS + 8, CELLS, CH), F32)],
+        scratch_shapes=[pltpu.VMEM((BRICKS + 8, CELLS, CH), BF)],
         compiler_params=ALL_VMEM,
         name="land_bricks",
     )(index, arrived, order, code)
@@ -213,16 +215,23 @@
     return jnp.concatenate([eye * block for block in blocks], axis=0).astype(BF)
 
 
-def front(taps, spread, w_fwd, head, head_t):
+def convolve(columns, w_side, w_mid):
+    sides = [
+        jnp.concatenate([columns[i + e][f] for e in range(3) for f in range(3)], axis=1)
+        for i in range(2)
+    ]
+    outer = matmul(jnp.concatenate(sides, axis=0), w_side)
+    middle = matmul(jnp.concatenate([part for four in columns for part in four], axis=1), w_mid)
+    middle = jnp.concatenate([middle[:, :CH], middle[:, CH:]], axis=0)
+    return outer[:, :CH], middle, outer[:, CH:]
+
+
+def front(columns, spread, w_side, w_mid, head, head_t):
     rows = spread.shape[0]
     lane = iota((rows, CH), 1)
     z = iota((rows // SZ, SZ, CH), 1).reshape(rows, CH)
-    parts = matmul(jnp.concatenate(taps, axis=1), w_fwd)
-    pre = (
-        shifted(parts[:, :CH], z, 1)
-        + parts[:, CH : 2 * CH]
-        + shifted(parts[:, 2 * CH :], z, -1)
-    )
+    below, middle, above = convolve(columns, w_side, w_mid)
+    pre = shifted(below, z, 1) + middle + shifted(above, z, -1)
     code = matmul(spread, jnp.ones((CH, CH), BF))
     mask = code > 0.5
     pre = jnp.where(mask, pre, 0.0)
@@ -244,19 +253,26 @@
     return pl.CostEstimate(flops=flops, bytes_accessed=4 * 2**20, transcendentals=0)
 
 
-def inner_kernel(slab, w_fwd, head, head_t, grad):
-    def step(x, carry):
-        taps = [slab[x + e, f * SZ : f * SZ + INNER, :] for e in range(3) for f in range(3)]
-        codes = slab[x + 1, ROWS:, :].astype(F32)
-        spread = spread_codes([codes[y : y + 1] for y in range(3, SY + 1)])
-        grad[x] = front(taps, spread, w_fwd[...], head[...], head_t[...])
+def inner_kernel(slab, w_side, w_mid, head, head_t, grad):
+    def step(pair, carry):
+        x = 2 * pair
+        columns = [[slab[x + i, f * SZ : f * SZ + INNER, :] for f in range(3)] for i in range(4)]
+        blocks = []
+        for i in range(2):
+            codes = slab[x + i + 1, ROWS:, :].astype(F32)
+            blocks += [codes[y : y + 1] for y in range(3, SY + 1)]
+        vals = front(
+            columns, spread_codes(blocks), w_side[...], w_mid[...], head[...], head_t[...]
+        )
+        for i in range(2):
+            grad[x + i] = vals[i * INNER : (i + 1) * INNER]
         return carry
 
-    lax.fori_loop(0, SX - 2, step, 0, unroll=2)
-
-
-def inner(slab, w_fwd, head, head_t):
-    arrays = (slab, w_fwd, head, head_t)
+    lax.fori_loop(0, SX // 2 - 1, step, 0, unroll=SX // 2 - 1)
+
+
+def inner(slab, weights):
+    arrays = (slab,) + weights
     shape = (SX - 2, INNER, CH)
     return pl.pallas_call(
         inner_kernel,
@@ -269,25 +285,30 @@
     )(*arrays)
 
 
-def x_sides_kernel(slab, before, after, w_fwd, head, head_t, grad):
+def x_sides_kernel(slab, before, after, w_side, w_mid, head, head_t, grad):
     def source(x):
         if x < 2:
             return before, x
         return (slab, x - 2) if x < SX + 2 else (after, x - SX - 2)
 
-    for i, x in enumerate((0, 1, SX, SX + 1)):
-        taps = []
-        for e in range(3):
-            ref, at = source(x + e)
-            taps += [ref[at, f * SZ : f * SZ + INNER, :] for f in range(3)]
-        ref, at = source(x + 1)
-        codes = ref[at, ROWS:, :].astype(F32)
-        spread = spread_codes([codes[y : y + 1] for y in range(3, SY + 1)])
-        grad[i] = front(taps, spread, w_fwd[...], head[...], head_t[...])
-
-
-def x_sides(slab, before, after, w_fwd, head, head_t):
-    arrays = (slab, before, after, w_fwd, head, head_t)
+    for pair, x in enumerate((0, SX)):
+        slabs = [source(x + i) for i in range(4)]
+        columns = [
+            [ref[at, f * SZ : f * SZ + INNER, :] for f in range(3)] for ref, at in slabs
+        ]
+        blocks = []
+        for ref, at in slabs[1:3]:
+            codes = ref[at, ROWS:, :].astype(F32)
+            blocks += [codes[y : y + 1] for y in range(3, SY + 1)]
+        vals = front(
+            columns, spread_codes(blocks), w_side[...], w_mid[...], head[...], head_t[...]
+        )
+        for i in range(2):
+            grad[2 * pair + i] = vals[i * INNER : (i + 1) * INNER]
+
+
+def x_sides(slab, before, after, weights):
+    arrays = (slab, before, after) + weights
     shape = (4, INNER, CH)
     return pl.pallas_call(
         x_sides_kernel,
@@ -301,7 +322,8 @@
 
 
 def core_kernel(
-    index, slab, before, after, left, right, inside, at_x, w_fwd, w_bwd, head, head_t, order_t,
+    index, slab, before, after, left, right, inside, at_x,
+    w_side, w_mid, head, head_t, w_side_t, w_mid_t, order_t,
     back_hbm, kept_hbm, low, high, codes, grad, coarse, held, back, sems,
 ):
     middle = pl.ds(SIDE, ROWS)
@@ -327,27 +349,26 @@
     grad[2:SX, SIDE : SIDE + INNER, :] = inside[...]
     grad[SX:, SIDE : SIDE + INNER, :] = at_x[2:]
 
-    z_own = iota((SY, SZ, CH), 1).reshape(ROWS, CH)
+    z_own = iota((2 * SY, SZ, CH), 1).reshape(2 * ROWS, CH)
 
     def forward(pair, carry):
         x = 2 * pair
-        taps = [
-            jnp.concatenate(
-                [
-                    ref[x + i + e, f * SZ : f * SZ + SIDE, :]
-                    for i in range(2)
-                    for ref in (low, high)
-                ],
-                axis=0,
-            )
-            for e in range(3)
-            for f in range(3)
+        columns = [
+            [
+                jnp.concatenate(
+                    [ref[x + i, f * SZ : f * SZ + SIDE, :] for ref in (low, high)], axis=0
+                )
+                for f in range(3)
+            ]
+            for i in range(4)
         ]
         blocks = []
         for i in range(2):
             here = codes[x + i + 1]
             blocks += [here[y : y + 1] for y in (1, 2, SY + 1, SY + 2)]
-        vals = front(taps, spread_codes(blocks), w_fwd[...], head[...], head_t[...])
+        vals = front(
+            columns, spread_codes(blocks), w_side[...], w_mid[...], head[...], head_t[...]
+        )
         for i in range(2):
             grad[x + i, :SIDE, :] = vals[2 * i * SIDE : (2 * i + 1) * SIDE]
             grad[x + i, SIDE + INNER :, :] = vals[(2 * i + 1) * SIDE : (2 * i + 2) * SIDE]
@@ -362,24 +383,16 @@
     out.start()
     copies.append(out)
 
-    def backward(x, carry):
-        taps = jnp.concatenate(
-            [
-                grad[x + 2 - e, (2 - f) * SZ : (2 - f) * SZ + ROWS, :]
-                for e in range(3)
-                for f in range(3)
-            ],
-            axis=1,
-        )
-        parts = matmul(taps, w_bwd[...])
-        coarse[x] = (
-            shifted(parts[:, :CH], z_own, -1)
-            + parts[:, CH : 2 * CH]
-            + shifted(parts[:, 2 * CH :], z_own, 1)
-        ).astype(BF)
+    def backward(pair, carry):
+        x = 2 * pair
+        columns = [[grad[x + i, f * SZ : f * SZ + ROWS, :] for f in range(3)] for i in range(4)]
+        below, middle, above = convolve(columns, w_side_t[...], w_mid_t[...])
+        vals = (shifted(below, z_own, -1) + middle + shifted(above, z_own, 1)).astype(BF)
+        for i in range(2):
+            coarse[x + i] = vals[i * ROWS : (i + 1) * ROWS]
         return carry
 
-    lax.fori_loop(0, SX, backward, 0, unroll=2)
+    lax.fori_loop(0, SX // 2, backward, 0, unroll=2)
 
     for big_x in range(SX // 2):
         for big_y in range(SY // 2):
@@ -392,10 +405,11 @@
                 axis=0,
             )
             start = (big_x * (SY // 2) + big_y) * (SZ // 2)
-            held[start : start + SZ // 2] = matmul(order_t[...], block).reshape(SZ // 2, CELLS, CH)
+            moved = matmul(order_t[...], block).reshape(SZ // 2, CELLS, CH)
+            held[start : start + SZ // 2] = moved.astype(BF)
 
     def put(j, carry):
-        back[j] = held[index[j]].astype(BF)
+        back[j] = held[index[j]]
         return carry
 
     part = index.shape[0] // PARTS
@@ -410,12 +424,10 @@
 
 
 def core(
-    index, slab, before, after, left, right, inside, at_x, w_fwd, w_bwd, head, head_t, order_t
+    index, slab, before, after, left, right, inside, at_x, weights, weights_t, order_t
 ):
-    arrays = (
-        slab, before, after, left, right, inside, at_x, w_fwd, w_bwd, head, head_t, order_t
-    )
-    shapes = ((index.shape[0], CELLS, CH), (FX + SX, FY * SZ, CH))
+    arrays = (slab, before, after, left, right, inside, at_x) + weights + weights_t + (order_t,)
+    shapes = ((index.shape[0], CELLS, CH), (KEPT, FY * SZ, CH))
     return pl.pallas_call(
         core_kernel,
         out_shape=tuple(jax.ShapeDtypeStruct(s, BF) for s in shapes),
@@ -427,16 +439,19 @@
             pltpu.VMEM((FX, CODE, CH), F32),
             pltpu.VMEM((SX + 2, ROWS + SIDE, CH), BF),
             pltpu.VMEM((SX, ROWS, CH), BF),
-            pltpu.VMEM((BRICKS, CELLS, CH), F32),
+            pltpu.VMEM((BRICKS, CELLS, CH), BF),
             pltpu.VMEM((index.shape[0], CELLS, CH), BF),
             pltpu.SemaphoreType.DMA((6 + PARTS,)),
         ],
-        compiler_params=VMEM,
+        compiler_params=MOST_VMEM,
         name="conv_both_ways",
     )(index, *arrays)
 
 
-def weights_kernel(half, kept, keep, give, total, taps_out):
+def weights_kernel(half, kept_hbm, keep, give, kept, total, taps_out, sem):
+    copy = pltpu.make_async_copy(kept_hbm.at[pl.ds(0, FX + SX)], kept, sem)
+    copy.start()
+    copy.wait()
     z_own = iota((SY, SZ, CH), 1).reshape(ROWS, CH)
     total[...] = jnp.zeros_like(total)
 
@@ -471,10 +486,15 @@
     return pl.pallas_call(
         weights_kernel,
         out_shape=(jax.ShapeDtypeStruct(shape, F32), jax.ShapeDtypeStruct(shape, BF)),
-        in_specs=[smem(), whole(kept.shape)],
+        in_specs=[smem(), hbm()],
         out_specs=(whole(shape),) * 2,
-        scratch_shapes=[pltpu.VMEM((3, 3 * CH, 3 * CH), F32), pltpu.VMEM((32, CH, CH), F32)],
-        compiler_params=VMEM,
+        scratch_shapes=[
+            pltpu.VMEM((FX + SX, FY * SZ, CH), BF),
+            pltpu.VMEM((3, 3 * CH, 3 * CH), F32),
+            pltpu.VMEM((32, CH, CH), F32),
+            pltpu.SemaphoreType.DMA,
+        ],
+        compiler_params=ALL_VMEM,
         cost_estimate=pl.CostEstimate(
             flops=2 * 27 * CH * CH * SX * ROWS, bytes_accessed=6 * 2**20, transcendentals=0
         ),
@@ -484,18 +504,18 @@
 
 def pair_kernel(me, keep, got, *outs):
     both = keep[...] + got[...].astype(F32).reshape(keep.shape)
-    turned = jnp.concatenate([both[:, :, 4:], both[:, :, :4]], axis=2)
     for by, out in enumerate(outs):
         y = lax.rem(me[0] + by, len(outs))
-        part = jnp.where(y % 2 == 0, both, turned)
-        part = jnp.where(y < 2, part[:, 0], part[:, 1])
-        out[...] = part[:, :4].astype(out.dtype)
+        part = jnp.where(y < 2, both[:, :, 0], both[:, :, 1])
+        low = jnp.concatenate([part[:, 0, :4], part[:, 1, :4]], axis=1)
+        high = jnp.concatenate([part[:, 0, 4:], part[:, 1, 4:]], axis=1)
+        out[...] = jnp.where(y % 2 == 0, low, high).astype(out.dtype)
 
 
 def add_pair(y, keep, got, ring, devs):
-    shape = (devs, 4, CH)
+    shape = (devs // 2, 8, CH)
     kinds = (F32,) + (BF,) * (ring - 1)
-    keep = keep.reshape(devs, 2, 8, CH)
+    keep = keep.reshape(devs // 2, 2, 2, 8, CH)
     got = got.reshape(devs, 16, CH)
     return pl.pallas_call(
         pair_kernel,
@@ -524,11 +544,11 @@
     per_dev = place.shape[0]
 
     def take(i, carry):
-        rows[i] = came[place[i]].astype(F32)
+        rows[i] = came[place[i]]
         return carry
 
     lax.fori_loop(0, per_dev, take, 0, unroll=8)
-    vals = rows[...].reshape(per_dev * CELLS, CH).astype(BF)
+    vals = rows[...].astype(F32).reshape(per_dev * CELLS, CH).astype(BF)
     mine[...] = vals
     stride[...] = lax.dot_general(
         feats[...], vals, (((0,), (0,)), ((), ())), preferred_element_type=F32
@@ -542,10 +562,31 @@
         out_shape=tuple(jax.ShapeDtypeStruct(s, BF) for s in shapes),
         in_specs=[smem(), whole(came.shape), whole(feats.shape)],
         out_specs=tuple(whole(s) for s in shapes),
-        scratch_shapes=[pltpu.VMEM((place.shape[0], CELLS, CH), F32)],
+        scratch_shapes=[pltpu.VMEM((place.shape[0], CELLS, CH), BF)],
         compiler_params=ALL_VMEM,
         name="stride_term",
     )(place, came, feats)
+
+
+def terms_kernel(stride, *refs):
+    terms, out = refs[:-1], refs[-1]
+    conv = sum(term[...].astype(F32) for term in terms)
+    both = stride[...].astype(F32)
+    out[:, 0] = jnp.concatenate([conv[:, :4], both[:, :4]], axis=1).astype(BF)
+    out[:, 1] = jnp.concatenate([conv[:, 4:], both[:, 4:]], axis=1).astype(BF)
+
+
+def put_together(stride, terms):
+    shape = terms[0].shape
+    arrays = (stride.reshape(shape),) + tuple(terms)
+    return pl.pallas_call(
+        terms_kernel,
+        out_shape=jax.ShapeDtypeStruct((shape[0], 2) + shape[1:], BF),
+        in_specs=[whole(shape) for a in arrays],
+        out_specs=whole((shape[0], 2) + shape[1:]),
+        compiler_params=VMEM,
+        name="put_together",
+    )(*arrays)
 
 
 def to_all(buffer):
@@ -567,6 +608,16 @@
     cells = labels.reshape(BX, BR, BY, BR, SZ // BR, BR)
     codes = jnp.where(filled, cells + 1, 0).reshape(SX, SY, SZ).astype(BF)
     return jnp.pad(codes, ((0, 0), (2, CODE - 2 - SY), (0, CH - SZ)))
+
+
+def arrange(taps):
+    side = taps[:, :, ::2].transpose(0, 1, 3, 2, 4).reshape(9 * CH, 2 * CH)
+    middle = taps[:, :, 1]
+    rest = ((0, 0),) * 3
+    middle = jnp.stack(
+        [jnp.pad(middle, ((0, 1),) + rest), jnp.pad(middle, ((1, 0),) + rest)], axis=3
+    )
+    return side, middle.reshape(12 * CH, 2 * CH)
 
 
 def per_device(fine_feats, owner_of, arrival_slot, w_stride, w_conv, w_head, labels):
@@ -585,18 +636,19 @@
     code = label_codes(arrival_slot, labels)
     order = brick_order()
     place, w_conv = lax.optimization_barrier((place, w_conv))
-    taps = w_conv.reshape(9, 3, CH, CH)
-    w_fwd = taps.transpose(0, 2, 1, 3).reshape(9 * CH, 3 * CH)
-    w_bwd = taps.transpose(0, 3, 1, 2).reshape(9 * CH, 3 * CH)
+    taps = w_conv.reshape(3, 3, 3, CH, CH)
+    w_fwd = arrange(taps)
+    w_bwd = arrange(taps[::-1, ::-1].swapaxes(3, 4))
     head = jnp.pad(jnp.concatenate([w_head, w_head], axis=1), ((0, 0), (0, CH - 16)))
 
     arrived, w_fwd, w_bwd = lax.optimization_barrier((to_all(buffer), w_fwd, w_bwd))
     slab, first, last_part = land(arrived, index, order, code)
     before, after = both_ways(first, last_part, "gx")
-    inside = inner(slab, w_fwd, head, head.T)
+    weights_fwd = w_fwd + (head, head.T)
+    inside = inner(slab, weights_fwd)
     up, down = sides(slab, before, after, inside)
     left, right = both_ways(down, up, "gy")
-    at_x = x_sides(slab, before, after, w_fwd, head, head.T)
+    at_x = x_sides(slab, before, after, weights_fwd)
     returned, kept = core(
         jnp.minimum(index, BRICKS - 1),
         slab,
@@ -606,10 +658,8 @@
         right,
         inside,
         at_x,
-        w_fwd,
+        weights_fwd,
         w_bwd,
-        head,
-        head.T,
         order.T,
     )
     came = to_all(returned)
@@ -617,10 +667,8 @@
     terms = sum_over_gy(*weights(half, kept), devs)
     mine, stride = last(came, place, feats)
     terms, stride = lax.optimization_barrier((terms, stride))
-    conv = sum(term.astype(F32) for term in terms).astype(BF)
-    share = in_width // devs
-    rows = conv.shape[1]
-    terms = to_all(jnp.concatenate([conv, stride.reshape(devs, share, CH)], axis=1))
+    share = rows = 4
+    terms = to_all(put_together(stride, terms).reshape(devs, rows + share, CH))
     grad_fine = lax.dot_general(
         mine, w_stride, (((1,), (1,)), ((), ())), preferred_element_type=F32
     ).astype(BF)

time: 164 us -> 161 us (0.982)
  waiting for transfers between devices: 41 us -> 34.8 us
  local copies, waits for them, and re-layouts: 9.83 us -> 14 us
  other arithmetic: 6.62 us -> 4.1 us
    all_to_all x3, waiting for transfers between devices: 35.7 us -> 28.5 us  [to_all(): lax.all_to_all(buffer, ('gx', 'gy'), split_axis=0, concat_axis=0, tiled=T...]
    transpose x0 -> x5, local copies, waits for them, and re-layouts: none -> 3.33 us  [the longest x4 3.25 us: arrange(): side = taps[:, :, ::2].transpose(0, 1, 3, 2, 4).reshape(9 * CH, 2 * CH)]
    pallas_call x1, Pallas kernels: 5.46 us -> 8.47 us  [weights(): pl.pallas_call(weights_kernel, out_shape=(jax.ShapeDtypeStruct(shape, F32...]
    concatenate x1 -> x0, other arithmetic: 1.78 us -> none  [per_device(): jnp.concatenate([conv, stride.reshape(devs, share, CH)], axis=1)]
    another operation x0 -> x4, local copies, waits for them, and re-layouts: none -> 1.7 us  [arrange(): jnp.stack([jnp.pad(middle, ((0, 1),) + rest), jnp.pad(middle, ((1, 0),) +...]
    unnamed x28 -> x36, local copies, waits for them, and re-layouts: 5.7 us -> 5.08 us
  transfers between devices with their start and end apart: 12 -> 12, of which waited for: 6 -> 6; matrix products, arithmetic and copies ran while one was open for 5% -> 8% of each run, Pallas kernels for 12% -> 13%
where the time goes in v3:
time: 161 us; the launch traced here: 160 us
  starting transfers between devices  42.3 us (26%)
  Pallas kernels  41.9 us (26%)
  waiting for transfers between devices  34.8 us (22%)
  blocking collectives  20.3 us (13%)
  local copies, waits for them, and re-layouts  14 us (9%)
  other arithmetic  4.1 us (3%)
  matrix products  1.72 us (1%)
    all_to_all x3, waiting for transfers between devices, to_all(): lax.all_to_all(buffer, ('gx', 'gy'), split_axis=0, concat_axis=0, tiled=T...  28.5 us
    all_to_all x3, starting transfers between devices, to_all(): lax.all_to_all(buffer, ('gx', 'gy'), split_axis=0, concat_axis=0, tiled=T...  27 us
    all_to_all x1, blocking collectives, to_all(): lax.all_to_all(buffer, ('gx', 'gy'), split_axis=0, concat_axis=0, tiled=T...  20.3 us
    pallas_call x1, Pallas kernels, core(): pl.pallas_call(core_kernel, out_shape=tuple((jax.ShapeDtypeStruct(s, BF)...  11.3 us
    ppermute x4, starting transfers between devices, both_ways(): return (lax.ppermute(last_part, axis, up), lax.ppermute(first, axis, down))  8.62 us
    pallas_call x1, Pallas kernels, weights(): pl.pallas_call(weights_kernel, out_shape=(jax.ShapeDtypeStruct(shape, F32...  8.47 us
    pallas_call x1, Pallas kernels, send(): pl.pallas_call(functools.partial(send_kernel, cap), out_shape=(jax.ShapeD...  5.16 us
    unnamed x36, local copies, waits for them, and re-layouts  5.08 us
  transfers between devices with their start and end apart: 12, of which 6 were waited for; matrix products, arithmetic and copies ran while one was open for 8% of the time, Pallas kernels for 13%

profile of v3, /device:TPU:1, one launch (start us, length us, event | category | flops | bytes accessed | tf_op | source)
XLA Modules:
  0.0 160.3 jit_solution(5412619768902669808)
XLA Ops:
  0.6 5.2 %send_bricks.1 = (bf16[768,8,128]{2,1,0:T(8,128)(2,1)}, s32[192]{0:T(256)}) custom-call(s32[192]{0:T(256)} %owner_hbm.1, bf16[1536,512]{1,0:T(8,128)(2,1)} %bitcast.58, bf16[512,128]{1,0:T(8,128)(2,1)} %w_hbm.1), custom_call_target="tpu_custom_call" | custom-call | tf_op jit(solution)/shard_map/send_bricks/pallas_call | solution.py:111
  5.8 11.9 %all-to-all-start = ((bf16[768,8,128]{2,1,0:T(8,128)(2,1)}), bf16[768,8,128]{2,1,0:T(8,128)(2,1)}, u32[]{:S(2)}, u32[]{:S(2)}) async-start(bf16[768,8,128]{2,1,0:T(8,128)(2,1)} %get-tuple-element.34), calls=%async_computation | async-start | bytes 3145728 | tf_op jit(solution)/shard_map/all_to_all | solution.py:593
  19.9 1.7 %copy.58 = bf16[3,3,128,2,128]{4,3,2,1,0:T(2,128)(2,1)} copy(bf16[3,3,128,2,128]{2,4,3,1,0:T(8,128)(2,1)S(1)} %slice_bitcast_fusion) | data formatting | bytes 1179648 | tf_op jit(solution)/shard_map/transpose | solution.py:614
  21.6 1.4 copy.56
  25.8 1.2 copy_bitcast_fusion
  27.0 1.3 copy_bitcast_fusion.2
  28.4 13.6 %all-to-all-done.arrived = bf16[768,8,128]{2,1,0:T(8,128)(2,1)} async-done(((bf16[768,8,128]{2,1,0:T(8,128)(2,1)}), bf16[768,8,128]{2,1,0:T(8,128)(2,1)}, u32[]{:S(2)}, u32[]{:S(2)}) %all-to-all-start) | async-done | bytes 1572896 | tf_op jit(solution)/shard_map/all_to_all | solution.py:593
  42.0 4.5 %land_bricks.1 = (bf16[8,400,128]{2,1,0:T(8,128)(2,1)}, bf16[2,400,128]{2,1,0:T(8,128)(2,1)}, bf16[2,400,128]{2,1,0:T(8,128)(2,1)}) custom-call(s32[768]{0:T(1024)} %get-tuple-element.66.index, bf16[768,8,128]{2,1,0:T(8,128)(2,1)} %all-to-all-done.arrived, bf16[192,192]{1,0:T(8,128)(2,1)} %get-tuple-element.72.order, bf16[8,16,128]{2,1,0:T(8,128)(2,1)} %pad.26.code), custom_call_target="tpu_custom_call" | custom-call | tf_op jit(solution)/shard_map/land_bricks/pallas_call | solution.py:165
  46.5 2.3 %collective-permute-start = (bf16[2,400,128]{2,1,0:T(8,128)(2,1)}, bf16[2,400,128]{2,1,0:T(8,128)(2,1)S(1)}, u32[]{:S(2)}, u32[]{:S(2)}) collective-permute-start(bf16[2,400,128]{2,1,0:T(8,128)(2,1)} %get-tuple-element.39), channel_id=1, source_target_pairs={{0,8},{8,16},{16,24},{24,32},{32,40},{40,48},{48,56},{56,64},{64,7... | collective-permute-start | bytes 614408 | tf_op jit(solution)/shard_map/ppermute | solution.py:600
  48.8 1.3 collective-permute-start.1
  50.3 1.1 copy-done
  53.6 3.4 %grad_pre_inside.1.inside = bf16[6,288,128]{2,1,0:T(8,128)(2,1)S(1)} custom-call(bf16[8,400,128]{2,1,0:T(8,128)(2,1)S(1)} %copy-done, bf16[1152,256]{1,0:T(8,128)(2,1)S(1)} %copy-done.5, bf16[1536,256]{1,0:T(8,128)(2,1)S(1)} %copy-done.2, bf16[128,128]{1,0:T(8,128)(2,1)S(1)} %copy.62.head, bf16[128,128]{1,0:T(8,128)(2,1)S(1)} %get-tuple-element.74.head_t), custom_call_target="tpu_custom_call" | custom-call | flops 1528823808 | bytes 4194304 | tf_op jit(solution)/shard_map/grad_pre_inside/pallas_call | solution.py:277
  57.1 2.6 %collective-permute-start.2 = (bf16[12,112,128]{2,1,0:T(8,128)(2,1)S(1)}, bf16[12,112,128]{2,1,0:T(8,128)(2,1)S(1)}, u32[]{:S(2)}, u32[]{:S(2)}) collective-permute-start(bf16[12,112,128]{2,1,0:T(8,128)(2,1)S(1)} %get-tuple-element.43), channel_id=1, source_target_pairs={{0,1},{1,2},{2,3},{3,4},{4,5},{5,6},{6,7},{8,9},{9,10},{10,11},{11... | collective-permute-start | bytes 1032200 | tf_op jit(solution)/shard_map/ppermute | solution.py:600
  59.7 2.4 %collective-permute-start.3 = (bf16[12,112,128]{2,1,0:T(8,128)(2,1)S(1)}, bf16[12,112,128]{2,1,0:T(8,128)(2,1)S(1)}, u32[]{:S(2)}, u32[]{:S(2)}) collective-permute-start(bf16[12,112,128]{2,1,0:T(8,128)(2,1)S(1)} %get-tuple-element.44), channel_id=1, source_target_pairs={{1,0},{2,1},{3,2},{4,3},{5,4},{6,5},{7,6},{9,8},{10,9},{11,10},{12... | collective-permute-start | bytes 1032200 | tf_op jit(solution)/shard_map/ppermute | solution.py:600
  62.2 2.4 %grad_pre_x_sides.1.at_x = bf16[4,288,128]{2,1,0:T(8,128)(2,1)S(1)} custom-call(bf16[8,400,128]{2,1,0:T(8,128)(2,1)S(1)} %copy-done, bf16[2,400,128]{2,1,0:T(8,128)(2,1)S(1)} %collective-permute-done.before, bf16[2,400,128]{2,1,0:T(8,128)(2,1)S(1)} %collective-permute-done.1.after, bf16[1152,256]{1,0:T(8,128)(2,1)S(1)} %copy-done.6, ...), custom_call_target="tpu_custom_call" | custom-call | flops 1019215872 | bytes 4194304 | tf_op jit(solution)/shard_map/grad_pre_x_sides/pallas_call | solution.py:313
  64.6 3.8 %collective-permute-done.3.right = bf16[12,112,128]{2,1,0:T(8,128)(2,1)S(1)} collective-permute-done((bf16[12,112,128]{2,1,0:T(8,128)(2,1)S(1)}, bf16[12,112,128]{2,1,0:T(8,128)(2,1)S(1)}, u32[]{:S(2)}, u32[]{:S(2)}) %collective-permute-start.3) | collective-permute-done | bytes 344096 | tf_op jit(solution)/shard_map/ppermute | solution.py:600
  68.4 11.3 %conv_both_ways.1 = (bf16[768,8,128]{2,1,0:T(8,128)(2,1)}, bf16[84,576,128]{2,1,0:T(8,128)(2,1)}) custom-call(s32[768]{0:T(1024)S(1)} %get-tuple-element.65.index, bf16[8,400,128]{2,1,0:T(8,128)(2,1)S(1)} %copy-done.1, bf16[2,400,128]{2,1,0:T(8,128)(2,1)S(1)} %collective-permute-done.before, bf16[2,400,128]{2,1,0:T(8,128)(2,1)S(1)} %collective-permute-done.1.after, ...), custom_call_target="tpu_custom_call" | custom-call | tf_op jit(solution)/shard_map/conv_both_ways/pallas_call | solution.py:431
  79.7 8.9 %all-to-all-start.1 = ((bf16[768,8,128]{2,1,0:T(8,128)(2,1)}), bf16[768,8,128]{2,1,0:T(8,128)(2,1)}, u32[]{:S(2)}, u32[]{:S(2)}) async-start(bf16[768,8,128]{2,1,0:T(8,128)(2,1)} %get-tuple-element.55), calls=%async_computation.1 | async-start | bytes 3145728 | tf_op jit(solution)/shard_map/all_to_all | solution.py:593
  88.6 8.5 %conv_weight_grad.1 = (f32[16,128,128]{2,1,0:T(8,128)}, bf16[16,128,128]{2,1,0:T(8,128)(2,1)}) custom-call(s32[1]{0:T(128)} %bitcast.1.half, bf16[84,576,128]{2,1,0:T(8,128)(2,1)} %get-tuple-element.47.kept_hbm), custom_call_target="tpu_custom_call" | custom-call | flops 2717908992 | bytes 6291456 | tf_op jit(solution)/shard_map/conv_weight_grad/pallas_call | solution.py:486
  97.1 1.2 collective-permute-start.4
  98.3 1.7 %collective-permute-done.4 = bf16[16,128,128]{2,1,0:T(8,128)(2,1)S(1)} collective-permute-done((bf16[16,128,128]{2,1,0:T(8,128)(2,1)}, bf16[16,128,128]{2,1,0:T(8,128)(2,1)S(1)}, u32[]{:S(2)}, u32[]{:S(2)}) %collective-permute-start.4) | collective-permute-done | bytes 524320 | tf_op jit(solution)/shard_map/ppermute | solution.py:535
  100.8 2.3 %add_pair.1 = (f32[64,8,128]{2,1,0:T(8,128)}, bf16[64,8,128]{2,1,0:T(8,128)(2,1)}, bf16[64,8,128]{2,1,0:T(8,128)(2,1)}, bf16[64,8,128]{2,1,0:T(8,128)(2,1)}) custom-call(s32[1]{0:T(128)} %bitcast.me, f32[64,2,2,8,128]{4,3,2,1,0:T(8,128)} %bitcast.72, bf16[128,16,128]{2,1,0:T(8,128)(2,1)} %bitcast.74), custom_call_target="tpu_custom_call" | custom-call | tf_op jit(solution)/shard_map/add_pair/pallas_call | solution.py:520
  103.8 2.4 %collective-permute-start.6 = (bf16[64,8,128]{2,1,0:T(8,128)(2,1)}, bf16[64,8,128]{2,1,0:T(8,128)(2,1)S(1)}, u32[]{:S(2)}, u32[]{:S(2)}) collective-permute-start(bf16[64,8,128]{2,1,0:T(8,128)(2,1)} %get-tuple-element.52), channel_id=1, source_target_pairs={{0,4},{1,5},{2,6},{3,7},{4,0},{5,1},{6,2},{7,3},{8,12},{9,13},{10,... | collective-permute-start | bytes 393224 | tf_op jit(solution)/shard_map/ppermute | solution.py:539
  106.3 1.1 collective-permute-start.7
  107.4 5.5 %all-to-all-done.1.came = bf16[768,8,128]{2,1,0:T(8,128)(2,1)} async-done(((bf16[768,8,128]{2,1,0:T(8,128)(2,1)}), bf16[768,8,128]{2,1,0:T(8,128)(2,1)}, u32[]{:S(2)}, u32[]{:S(2)}) %all-to-all-start.1) | async-done | bytes 1572896 | tf_op jit(solution)/shard_map/all_to_all | solution.py:593
  112.9 3.5 %stride_term.1 = (bf16[1536,128]{1,0:T(8,128)(2,1)}, bf16[512,128]{1,0:T(8,128)(2,1)}) custom-call(s32[192]{0:T(256)} %get-tuple-element.54.place, bf16[768,8,128]{2,1,0:T(8,128)(2,1)} %all-to-all-done.1.came, bf16[1536,512]{1,0:T(8,128)(2,1)} %bitcast.59), custom_call_target="tpu_custom_call" | custom-call | tf_op jit(solution)/shard_map/stride_term/pallas_call | solution.py:560
  118.1 6.2 %all-to-all-start.2 = ((bf16[128,8,128]{2,1,0:T(8,128)(2,1)}), bf16[128,8,128]{2,1,0:T(8,128)(2,1)S(1)}, u32[]{:S(2)}, u32[]{:S(2)}) async-start(bf16[128,8,128]{2,1,0:T(8,128)(2,1)} %bitcast.17), calls=%async_computation.2 | async-start | bytes 524288 | tf_op jit(solution)/shard_map/all_to_all | solution.py:593
  124.3 1.7 %convolution_convert_fusion = bf16[1536,512]{1,0:T(8,128)(2,1)} fusion(bf16[1536,128]{1,0:T(8,128)(2,1)S(1)} %copy-done.14, bf16[512,128]{1,0:T(8,128)(2,1)S(1)} %copy-done.12), kind=kOutput, calls=%fused_computation | convolution fusion | flops 202113024 | bytes 2097152 | tf_op jit(solution)/shard_map/dot_general | solution.py:672
  126.1 9.3 %all-to-all-done.2 = bf16[128,8,128]{2,1,0:T(8,128)(2,1)S(1)} async-done(((bf16[128,8,128]{2,1,0:T(8,128)(2,1)}), bf16[128,8,128]{2,1,0:T(8,128)(2,1)S(1)}, u32[]{:S(2)}, u32[]{:S(2)}) %all-to-all-start.2) | async-done | bytes 262176 | tf_op jit(solution)/shard_map/all_to_all | solution.py:593
  135.6 20.3 %all_to_all.20 = bf16[128,20,128]{2,1,0:T(8,128)(2,1)S(1)} all-to-all(bf16[128,20,128]{2,1,0:T(8,128)(2,1)S(1)} %bitcast.65), channel_id=1, replica_groups=mesh['gx'=16,'gy'=8] {'gx','gy'}, dimensions={0} | all-to-all | bytes 1310720 | tf_op jit(solution)/shard_map/all_to_all | solution.py:593
  155.9 1.3 collective-permute-start.8
  158.9 1.3 convert_multiply_fusion
  (80 shorter events, 12.2 us)
Async XLA Ops:
  5.8 11.9 %copy-start.9 = (bf16[27,128,128]{2,1,0:T(8,128)(2,1)S(1)}, bf16[27,128,128]{2,1,0:T(8,128)(2,1)}, u32[]{:S(2)}) copy-start(bf16[27,128,128]{2,1,0:T(8,128)(2,1)} %param.11) | copy-start | bytes 2654212
  5.8 36.2 %all-to-all-start = ((bf16[768,8,128]{2,1,0:T(8,128)(2,1)}), bf16[768,8,128]{2,1,0:T(8,128)(2,1)}, u32[]{:S(2)}, u32[]{:S(2)}) async-start(bf16[768,8,128]{2,1,0:T(8,128)(2,1)} %get-tuple-element.34), calls=%async_computation | async-start | bytes 3145728 | tf_op jit(solution)/shard_map/all_to_all | solution.py:593
  19.1 4.0 %copy-start.16 = (s32[768]{0:T(1024)S(1)}, s32[768]{0:T(1024)}, u32[]{:S(2)}) copy-start(s32[768]{0:T(1024)} %param.9) | copy-start | bytes 9220
  19.1 5.2 %copy-start.15 = (s32[8,8,48]{2,1,0:T(8,128)S(1)}, s32[8,8,48]{2,1,0:T(8,128)}, u32[]{:S(2)}) copy-start(s32[8,8,48]{2,1,0:T(8,128)} %param.13) | copy-start | bytes 36868
  24.3 2.7 %copy-start.10 = (bf16[3,3,128,2,128]{4,3,2,1,0:T(2,128)(2,1)S(1)}, bf16[3,3,128,2,128]{4,3,2,1,0:T(2,128)(2,1)}, u32[]{:S(2)}) copy-start(bf16[3,3,128,2,128]{4,3,2,1,0:T(2,128)(2,1)} %copy.58) | copy-start | bytes 1769476
  24.3 2.7 %copy-start.11 = (bf16[3,3,128,2,128]{4,3,2,1,0:T(2,128)(2,1)S(1)}, bf16[3,3,128,2,128]{4,3,2,1,0:T(2,128)(2,1)}, u32[]{:S(2)}) copy-start(bf16[3,3,128,2,128]{4,3,2,1,0:T(2,128)(2,1)} %copy.56) | copy-start | bytes 1769476
  27.0 23.1 %copy-start.17 = (bf16[128,8]{0,1:T(8,128)(2,1)S(1)}, bf16[128,8]{0,1:T(8,128)(2,1)}, u32[]{:S(2)}) copy-start(bf16[128,8]{0,1:T(8,128)(2,1)} %param.12) | copy-start | bytes 6148
  46.5 10.6 %collective-permute-start = (bf16[2,400,128]{2,1,0:T(8,128)(2,1)}, bf16[2,400,128]{2,1,0:T(8,128)(2,1)S(1)}, u32[]{:S(2)}, u32[]{:S(2)}) collective-permute-start(bf16[2,400,128]{2,1,0:T(8,128)(2,1)} %get-tuple-element.39), channel_id=1, source_target_pairs={{0,8},{8,16},{16,24},{24,32},{32,40},{40,48},{48,56},{56,64},{64,7... | collective-permute-start | bytes 614408 | tf_op jit(solution)/shard_map/ppermute | solution.py:600
  48.8 8.2 %collective-permute-start.1 = (bf16[2,400,128]{2,1,0:T(8,128)(2,1)}, bf16[2,400,128]{2,1,0:T(8,128)(2,1)S(1)}, u32[]{:S(2)}, u32[]{:S(2)}) collective-permute-start(bf16[2,400,128]{2,1,0:T(8,128)(2,1)} %get-tuple-element.40), channel_id=1, source_target_pairs={{8,0},{16,8},{24,16},{32,24},{40,32},{48,40},{56,48},{64,56},{72,6... | collective-permute-start | bytes 614408 | tf_op jit(solution)/shard_map/ppermute | solution.py:600
  50.3 1.2 copy-start
  51.4 1.1 copy-start.2
  52.5 1.1 copy-start.5
  53.6 8.5 %copy-start.3 = (bf16[1536,256]{1,0:T(8,128)(2,1)S(1)}, bf16[1536,256]{1,0:T(8,128)(2,1)}, u32[]{:S(2)}) copy-start(bf16[1536,256]{1,0:T(8,128)(2,1)} %get-tuple-element.42.w_mid) | copy-start | bytes 2359300
  53.6 8.5 %copy-start.6 = (bf16[1152,256]{1,0:T(8,128)(2,1)S(1)}, bf16[1152,256]{1,0:T(8,128)(2,1)}, u32[]{:S(2)}) copy-start(bf16[1152,256]{1,0:T(8,128)(2,1)} %get-tuple-element.41.w_side) | copy-start | bytes 1769476
  57.1 7.5 %collective-permute-start.2 = (bf16[12,112,128]{2,1,0:T(8,128)(2,1)S(1)}, bf16[12,112,128]{2,1,0:T(8,128)(2,1)S(1)}, u32[]{:S(2)}, u32[]{:S(2)}) collective-permute-start(bf16[12,112,128]{2,1,0:T(8,128)(2,1)S(1)} %get-tuple-element.43), channel_id=1, source_target_pairs={{0,1},{1,2},{2,3},{3,4},{4,5},{5,6},{6,7},{8,9},{9,10},{10,11},{11... | collective-permute-start | bytes 1032200 | tf_op jit(solution)/shard_map/ppermute | solution.py:600
  59.7 8.7 %copy-start.1 = (bf16[8,400,128]{2,1,0:T(8,128)(2,1)S(1)}, bf16[8,400,128]{2,1,0:T(8,128)(2,1)}, u32[]{:S(2)}) copy-start(bf16[8,400,128]{2,1,0:T(8,128)(2,1)} %get-tuple-element.38.slab) | copy-start | bytes 2457604
  59.7 8.7 %copy-start.4 = (bf16[1152,256]{1,0:T(8,128)(2,1)S(1)}, bf16[1152,256]{1,0:T(8,128)(2,1)}, u32[]{:S(2)}) copy-start(bf16[1152,256]{1,0:T(8,128)(2,1)} %get-tuple-element.45.w_side_t) | copy-start | bytes 1769476
  59.7 8.7 %collective-permute-start.3 = (bf16[12,112,128]{2,1,0:T(8,128)(2,1)S(1)}, bf16[12,112,128]{2,1,0:T(8,128)(2,1)S(1)}, u32[]{:S(2)}, u32[]{:S(2)}) collective-permute-start(bf16[12,112,128]{2,1,0:T(8,128)(2,1)S(1)} %get-tuple-element.44), channel_id=1, source_target_pairs={{1,0},{2,1},{3,2},{4,3},{5,4},{6,5},{7,6},{9,8},{10,9},{11,10},{12... | collective-permute-start | bytes 1032200 | tf_op jit(solution)/shard_map/ppermute | solution.py:600
  79.7 33.2 %all-to-all-start.1 = ((bf16[768,8,128]{2,1,0:T(8,128)(2,1)}), bf16[768,8,128]{2,1,0:T(8,128)(2,1)}, u32[]{:S(2)}, u32[]{:S(2)}) async-start(bf16[768,8,128]{2,1,0:T(8,128)(2,1)} %get-tuple-element.55), calls=%async_computation.1 | async-start | bytes 3145728 | tf_op jit(solution)/shard_map/all_to_all | solution.py:593
  97.1 3.0 %collective-permute-start.4 = (bf16[16,128,128]{2,1,0:T(8,128)(2,1)}, bf16[16,128,128]{2,1,0:T(8,128)(2,1)S(1)}, u32[]{:S(2)}, u32[]{:S(2)}) collective-permute-start(bf16[16,128,128]{2,1,0:T(8,128)(2,1)} %get-tuple-element.49), channel_id=1, source_target_pairs={{0,1},{1,0},{2,3},{3,2},{4,5},{5,4},{6,7},{7,6},{8,9},{9,8},{10,11... | collective-permute-start | bytes 1572872 | tf_op jit(solution)/shard_map/ppermute | solution.py:535
  100.1 0.8 copy-start.13
  103.2 13.2 %copy-start.7 = (f32[64,8,128]{2,1,0:T(8,128)S(1)}, f32[64,8,128]{2,1,0:T(8,128)}, u32[]{:S(2)}) copy-start(f32[64,8,128]{2,1,0:T(8,128)} %get-tuple-element.58.refs_0_) | copy-start | bytes 786436
  103.2 13.2 %collective-permute-start.5 = (bf16[64,8,128]{2,1,0:T(8,128)(2,1)}, bf16[64,8,128]{2,1,0:T(8,128)(2,1)S(1)}, u32[]{:S(2)}, u32[]{:S(2)}) collective-permute-start(bf16[64,8,128]{2,1,0:T(8,128)(2,1)} %get-tuple-element.51), channel_id=1, source_target_pairs={{0,2},{1,3},{2,4},{3,5},{4,6},{5,7},{6,0},{7,1},{8,10},{9,11},{10,... | collective-permute-start | bytes 393224 | tf_op jit(solution)/shard_map/ppermute | solution.py:539
  103.8 12.6 %collective-permute-start.6 = (bf16[64,8,128]{2,1,0:T(8,128)(2,1)}, bf16[64,8,128]{2,1,0:T(8,128)(2,1)S(1)}, u32[]{:S(2)}, u32[]{:S(2)}) collective-permute-start(bf16[64,8,128]{2,1,0:T(8,128)(2,1)} %get-tuple-element.52), channel_id=1, source_target_pairs={{0,4},{1,5},{2,6},{3,7},{4,0},{5,1},{6,2},{7,3},{8,12},{9,13},{10,... | collective-permute-start | bytes 393224 | tf_op jit(solution)/shard_map/ppermute | solution.py:539
  106.3 18.1 %copy-start.12 = (bf16[512,128]{1,0:T(8,128)(2,1)S(1)}, bf16[512,128]{1,0:T(8,128)(2,1)}, u32[]{:S(2)}) copy-start(bf16[512,128]{1,0:T(8,128)(2,1)} %w_hbm.1) | copy-start | bytes 393220
  106.3 10.1 %collective-permute-start.7 = (bf16[64,8,128]{2,1,0:T(8,128)(2,1)}, bf16[64,8,128]{2,1,0:T(8,128)(2,1)S(1)}, u32[]{:S(2)}, u32[]{:S(2)}) collective-permute-start(bf16[64,8,128]{2,1,0:T(8,128)(2,1)} %get-tuple-element.53), channel_id=1, source_target_pairs={{0,6},{1,7},{2,0},{3,1},{4,2},{5,3},{6,4},{7,5},{8,14},{9,15},{10,... | collective-permute-start | bytes 393224 | tf_op jit(solution)/shard_map/ppermute | solution.py:539
  116.4 0.9 copy-start.8
  117.3 7.0 %copy-start.14 = (bf16[1536,128]{1,0:T(8,128)(2,1)S(1)}, bf16[1536,128]{1,0:T(8,128)(2,1)}, u32[]{:S(2)}) copy-start(bf16[1536,128]{1,0:T(8,128)(2,1)} %get-tuple-element.62) | copy-start | bytes 1179652
  118.1 17.3 %all-to-all-start.2 = ((bf16[128,8,128]{2,1,0:T(8,128)(2,1)}), bf16[128,8,128]{2,1,0:T(8,128)(2,1)S(1)}, u32[]{:S(2)}, u32[]{:S(2)}) async-start(bf16[128,8,128]{2,1,0:T(8,128)(2,1)} %bitcast.17), calls=%async_computation.2 | async-start | bytes 524288 | tf_op jit(solution)/shard_map/all_to_all | solution.py:593
  155.9 2.8 %collective-permute-start.8 = (bf16[2048,128]{1,0:T(8,128)(2,1)S(1)}, bf16[2048,128]{1,0:T(8,128)(2,1)S(1)}, u32[]{:S(2)}, u32[]{:S(2)}) collective-permute-start(bf16[2048,128]{1,0:T(8,128)(2,1)S(1)} %bitcast.60), channel_id=1, source_target_pairs={{0,1},{1,0},{2,3},{3,2},{4,5},{5,4},{6,7},{7,6},{8,9},{9,8},{10,11... | collective-permute-start | bytes 1572872 | tf_op jit(solution)/shard_map/ppermute | solution.py:687

commit v4 on v3

--- a/solution.py
+++ b/solution.py
@@ -77,26 +77,27 @@
     buf[...] = jnp.zeros_like(buf)
     copies[0].wait()
 
-    def find(i, c):
+    def find(i):
         who = owner[i]
         pos = count[who]
         count[who] = pos + 1
         place[i] = who * cap + pos
-        return c
-
-    lax.fori_loop(0, per_dev, find, 0, unroll=8)
+
+    def put(i):
+        buf[place[i]] = rows[i]
+
     copies[1].wait()
     bricks = per_dev // PARTS
-    for i in range(PARTS):
-        copies[2 + i].wait()
-        vals = matmul(feats[i * part : (i + 1) * part, :], w_stride[...])
-        rows[i * bricks : (i + 1) * bricks] = vals.reshape(bricks, CELLS, CH).astype(BF)
-
-    def put(i, c):
-        buf[place[i]] = rows[i]
-        return c
-
-    lax.fori_loop(0, per_dev, put, 0, unroll=8)
+    for i in range(PARTS + 1):
+        if i < PARTS:
+            copies[2 + i].wait()
+            vals = matmul(feats[i * part : (i + 1) * part, :], w_stride[...])
+            rows[i * bricks : (i + 1) * bricks] = vals.reshape(bricks, CELLS, CH).astype(BF)
+            for j in range(i * bricks, (i + 1) * bricks):
+                find(j)
+        if i > 0:
+            for j in range((i - 1) * bricks, i * bricks):
+                put(j)
     out = pltpu.make_async_copy(buf, buf_hbm, sems.at[0])
     out.start()
     out.wait()
@@ -140,11 +141,8 @@
 def land_kernel(index, arrived, order, code, slab, first, last, held):
     held[...] = jnp.zeros_like(held)
 
-    def put(j, c):
+    for j in range(index.shape[0]):
         held[index[j]] = arrived[j]
-        return c
-
-    lax.fori_loop(0, index.shape[0], put, 0, unroll=8)
     for big_x in range(SX // 2):
         for big_y in range(SY // 2):
             start = (big_x * (SY // 2) + big_y) * (SZ // 2)
@@ -392,7 +390,7 @@
             coarse[x + i] = vals[i * ROWS : (i + 1) * ROWS]
         return carry
 
-    lax.fori_loop(0, SX // 2, backward, 0, unroll=2)
+    lax.fori_loop(0, SX // 2, backward, 0, unroll=4)
 
     for big_x in range(SX // 2):
         for big_y in range(SY // 2):
@@ -408,13 +406,10 @@
             moved = matmul(order_t[...], block).reshape(SZ // 2, CELLS, CH)
             held[start : start + SZ // 2] = moved.astype(BF)
 
-    def put(j, carry):
-        back[j] = held[index[j]]
-        return carry
-
     part = index.shape[0] // PARTS
     for i in range(PARTS):
-        lax.fori_loop(i * part, (i + 1) * part, put, 0, unroll=8)
+        for j in range(i * part, (i + 1) * part):
+            back[j] = held[index[j]]
         rows = pl.ds(i * part, part)
         copy = pltpu.make_async_copy(back.at[rows], back_hbm.at[rows], sems.at[6 + i])
         copy.start()
@@ -543,11 +538,8 @@
 def last_kernel(place, came, feats, mine, stride, rows):
     per_dev = place.shape[0]
 
-    def take(i, carry):
+    for i in range(per_dev):
         rows[i] = came[place[i]]
-        return carry
-
-    lax.fori_loop(0, per_dev, take, 0, unroll=8)
     vals = rows[...].astype(F32).reshape(per_dev * CELLS, CH).astype(BF)
     mine[...] = vals
     stride[...] = lax.dot_general(
@@ -563,7 +555,7 @@
         in_specs=[smem(), whole(came.shape), whole(feats.shape)],
         out_specs=tuple(whole(s) for s in shapes),
         scratch_shapes=[pltpu.VMEM((place.shape[0], CELLS, CH), BF)],
-        compiler_params=ALL_VMEM,
+        compiler_params=VMEM,
         name="stride_term",
     )(place, came, feats)
 

time: 161 us -> 157 us (0.975)
  Pallas kernels: 41.9 us -> 37.9 us
  transfers between devices with their start and end apart: 12 -> 12, of which waited for: 6 -> 6; matrix products, arithmetic and copies ran while one was open for 8% -> 8% of each run, Pallas kernels for 13% -> 12%
where the time goes in v4:
time: 157 us
  starting transfers between devices  42.2 us (27%)
  Pallas kernels  37.9 us (24%)
  waiting for transfers between devices  34.8 us (22%)
  blocking collectives  20.3 us (13%)
  local copies, waits for them, and re-layouts  14.5 us (9%)
  other arithmetic  4.1 us (3%)
  matrix products  1.72 us (1%)
    all_to_all x3, waiting for transfers between devices, to_all(): lax.all_to_all(buffer, ('gx', 'gy'), split_axis=0, concat_axis=0, tiled=T...  28.5 us
    all_to_all x3, starting transfers between devices, to_all(): lax.all_to_all(buffer, ('gx', 'gy'), split_axis=0, concat_axis=0, tiled=T...  26.9 us
    all_to_all x1, blocking collectives, to_all(): lax.all_to_all(buffer, ('gx', 'gy'), split_axis=0, concat_axis=0, tiled=T...  20.3 us
    pallas_call x1, Pallas kernels, core(): pl.pallas_call(core_kernel, out_shape=tuple((jax.ShapeDtypeStruct(s, BF)...  10.1 us
    ppermute x4, starting transfers between devices, both_ways(): return (lax.ppermute(last_part, axis, up), lax.ppermute(first, axis, down))  8.61 us
    pallas_call x1, Pallas kernels, weights(): pl.pallas_call(weights_kernel, out_shape=(jax.ShapeDtypeStruct(shape, F32...  8.47 us
    unnamed x36, local copies, waits for them, and re-layouts  5.59 us
    pallas_call x1, Pallas kernels, send(): pl.pallas_call(functools.partial(send_kernel, cap), out_shape=(jax.ShapeD...  4.28 us
  transfers between devices with their start and end apart: 12, of which 6 were waited for; matrix products, arithmetic and copies ran while one was open for 8% of the time, Pallas kernels for 12%

profile of v4, /device:TPU:1, one launch (start us, length us, event | category | flops | bytes accessed | tf_op | source)
XLA Modules:
  0.0 156.6 jit_solution(15169012958805296315)
XLA Ops:
  0.6 4.3 %send_bricks.1 = (bf16[768,8,128]{2,1,0:T(8,128)(2,1)}, s32[192]{0:T(256)}) custom-call(s32[192]{0:T(256)} %owner_hbm.1, bf16[1536,512]{1,0:T(8,128)(2,1)} %bitcast.57, bf16[512,128]{1,0:T(8,128)(2,1)} %w_hbm.1), custom_call_target="tpu_custom_call" | custom-call | tf_op jit(solution)/shard_map/send_bricks/pallas_call | solution.py:112
  4.9 11.9 %all-to-all-start = ((bf16[768,8,128]{2,1,0:T(8,128)(2,1)}), bf16[768,8,128]{2,1,0:T(8,128)(2,1)}, u32[]{:S(2)}, u32[]{:S(2)}) async-start(bf16[768,8,128]{2,1,0:T(8,128)(2,1)} %get-tuple-element.34), calls=%async_computation | async-start | bytes 3145728 | tf_op jit(solution)/shard_map/all_to_all | solution.py:585
  19.0 1.7 %copy.58 = bf16[3,3,128,2,128]{4,3,2,1,0:T(2,128)(2,1)} copy(bf16[3,3,128,2,128]{2,4,3,1,0:T(8,128)(2,1)S(1)} %slice_bitcast_fusion) | data formatting | bytes 1179648 | tf_op jit(solution)/shard_map/transpose | solution.py:606
  20.8 1.4 copy.56
  24.9 1.2 copy_bitcast_fusion
  26.1 1.3 copy_bitcast_fusion.2
  27.5 13.6 %all-to-all-done.arrived = bf16[768,8,128]{2,1,0:T(8,128)(2,1)} async-done(((bf16[768,8,128]{2,1,0:T(8,128)(2,1)}), bf16[768,8,128]{2,1,0:T(8,128)(2,1)}, u32[]{:S(2)}, u32[]{:S(2)}) %all-to-all-start) | async-done | bytes 1572896 | tf_op jit(solution)/shard_map/all_to_all | solution.py:585
  41.1 3.8 %land_bricks.1 = (bf16[8,400,128]{2,1,0:T(8,128)(2,1)}, bf16[2,400,128]{2,1,0:T(8,128)(2,1)}, bf16[2,400,128]{2,1,0:T(8,128)(2,1)}) custom-call(s32[768]{0:T(1024)} %get-tuple-element.66.index, bf16[768,8,128]{2,1,0:T(8,128)(2,1)} %all-to-all-done.arrived, bf16[192,192]{1,0:T(8,128)(2,1)} %get-tuple-element.72.order, bf16[8,16,128]{2,1,0:T(8,128)(2,1)} %pad.26.code), custom_call_target="tpu_custom_call" | custom-call | tf_op jit(solution)/shard_map/land_bricks/pallas_call | solution.py:163
  44.9 2.3 %collective-permute-start = (bf16[2,400,128]{2,1,0:T(8,128)(2,1)}, bf16[2,400,128]{2,1,0:T(8,128)(2,1)S(1)}, u32[]{:S(2)}, u32[]{:S(2)}) collective-permute-start(bf16[2,400,128]{2,1,0:T(8,128)(2,1)} %get-tuple-element.39), channel_id=1, source_target_pairs={{0,8},{8,16},{16,24},{24,32},{32,40},{40,48},{48,56},{56,64},{64,7... | collective-permute-start | bytes 614408 | tf_op jit(solution)/shard_map/ppermute | solution.py:592
  47.2 1.3 collective-permute-start.1
  48.7 1.1 copy-done.1
  52.0 3.4 %grad_pre_inside.1.inside = bf16[6,288,128]{2,1,0:T(8,128)(2,1)S(1)} custom-call(bf16[8,400,128]{2,1,0:T(8,128)(2,1)S(1)} %copy-done.1, bf16[1152,256]{1,0:T(8,128)(2,1)S(1)} %copy-done.6, bf16[1536,256]{1,0:T(8,128)(2,1)S(1)} %copy-done.3, bf16[128,128]{1,0:T(8,128)(2,1)S(1)} %copy.62.head, bf16[128,128]{1,0:T(8,128)(2,1)S(1)} %get-tuple-element.74.head_t), custom_call_target="tpu_custom_call" | custom-call | flops 1528823808 | bytes 4194304 | tf_op jit(solution)/shard_map/grad_pre_inside/pallas_call | solution.py:275
  55.5 2.6 %collective-permute-start.2 = (bf16[12,112,128]{2,1,0:T(8,128)(2,1)S(1)}, bf16[12,112,128]{2,1,0:T(8,128)(2,1)S(1)}, u32[]{:S(2)}, u32[]{:S(2)}) collective-permute-start(bf16[12,112,128]{2,1,0:T(8,128)(2,1)S(1)} %get-tuple-element.43), channel_id=1, source_target_pairs={{0,1},{1,2},{2,3},{3,4},{4,5},{5,6},{6,7},{8,9},{9,10},{10,11},{11... | collective-permute-start | bytes 1032200 | tf_op jit(solution)/shard_map/ppermute | solution.py:592
  58.1 2.4 %collective-permute-start.3 = (bf16[12,112,128]{2,1,0:T(8,128)(2,1)S(1)}, bf16[12,112,128]{2,1,0:T(8,128)(2,1)S(1)}, u32[]{:S(2)}, u32[]{:S(2)}) collective-permute-start(bf16[12,112,128]{2,1,0:T(8,128)(2,1)S(1)} %get-tuple-element.44), channel_id=1, source_target_pairs={{1,0},{2,1},{3,2},{4,3},{5,4},{6,5},{7,6},{9,8},{10,9},{11,10},{12... | collective-permute-start | bytes 1032200 | tf_op jit(solution)/shard_map/ppermute | solution.py:592
  60.6 2.4 %grad_pre_x_sides.1.at_x = bf16[4,288,128]{2,1,0:T(8,128)(2,1)S(1)} custom-call(bf16[8,400,128]{2,1,0:T(8,128)(2,1)S(1)} %copy-done.1, bf16[2,400,128]{2,1,0:T(8,128)(2,1)S(1)} %collective-permute-done.before, bf16[2,400,128]{2,1,0:T(8,128)(2,1)S(1)} %collective-permute-done.1.after, bf16[1152,256]{1,0:T(8,128)(2,1)S(1)} %copy-done.7, ...), custom_call_target="tpu_custom_call" | custom-call | flops 1019215872 | bytes 4194304 | tf_op jit(solution)/shard_map/grad_pre_x_sides/pallas_call | solution.py:311
  63.0 3.8 %collective-permute-done.3.right = bf16[12,112,128]{2,1,0:T(8,128)(2,1)S(1)} collective-permute-done((bf16[12,112,128]{2,1,0:T(8,128)(2,1)S(1)}, bf16[12,112,128]{2,1,0:T(8,128)(2,1)S(1)}, u32[]{:S(2)}, u32[]{:S(2)}) %collective-permute-start.3) | collective-permute-done | bytes 344096 | tf_op jit(solution)/shard_map/ppermute | solution.py:592
  66.8 10.1 %conv_both_ways.1 = (bf16[768,8,128]{2,1,0:T(8,128)(2,1)}, bf16[84,576,128]{2,1,0:T(8,128)(2,1)}) custom-call(s32[768]{0:T(1024)S(1)} %get-tuple-element.65.index, bf16[8,400,128]{2,1,0:T(8,128)(2,1)S(1)} %copy-done.2, bf16[2,400,128]{2,1,0:T(8,128)(2,1)S(1)} %collective-permute-done.before, bf16[2,400,128]{2,1,0:T(8,128)(2,1)S(1)} %collective-permute-done.1.after, ...), custom_call_target="tpu_custom_call" | custom-call | tf_op jit(solution)/shard_map/conv_both_ways/pallas_call | solution.py:426
  77.0 8.9 %all-to-all-start.1 = ((bf16[768,8,128]{2,1,0:T(8,128)(2,1)}), bf16[768,8,128]{2,1,0:T(8,128)(2,1)}, u32[]{:S(2)}, u32[]{:S(2)}) async-start(bf16[768,8,128]{2,1,0:T(8,128)(2,1)} %get-tuple-element.55), calls=%async_computation.1 | async-start | bytes 3145728 | tf_op jit(solution)/shard_map/all_to_all | solution.py:585
  85.9 8.5 %conv_weight_grad.1 = (f32[16,128,128]{2,1,0:T(8,128)}, bf16[16,128,128]{2,1,0:T(8,128)(2,1)}) custom-call(s32[1]{0:T(128)} %bitcast.1.half, bf16[84,576,128]{2,1,0:T(8,128)(2,1)} %get-tuple-element.47.kept_hbm), custom_call_target="tpu_custom_call" | custom-call | flops 2717908992 | bytes 6291456 | tf_op jit(solution)/shard_map/conv_weight_grad/pallas_call | solution.py:481
  94.4 1.2 collective-permute-start.4
  95.6 1.7 %collective-permute-done.4 = bf16[16,128,128]{2,1,0:T(8,128)(2,1)S(1)} collective-permute-done((bf16[16,128,128]{2,1,0:T(8,128)(2,1)}, bf16[16,128,128]{2,1,0:T(8,128)(2,1)S(1)}, u32[]{:S(2)}, u32[]{:S(2)}) %collective-permute-start.4) | collective-permute-done | bytes 524320 | tf_op jit(solution)/shard_map/ppermute | solution.py:530
  98.1 2.3 %add_pair.1 = (f32[64,8,128]{2,1,0:T(8,128)}, bf16[64,8,128]{2,1,0:T(8,128)(2,1)}, bf16[64,8,128]{2,1,0:T(8,128)(2,1)}, bf16[64,8,128]{2,1,0:T(8,128)(2,1)}) custom-call(s32[1]{0:T(128)} %bitcast.me, f32[64,2,2,8,128]{4,3,2,1,0:T(8,128)} %bitcast.72, bf16[128,16,128]{2,1,0:T(8,128)(2,1)} %bitcast.74), custom_call_target="tpu_custom_call" | custom-call | tf_op jit(solution)/shard_map/add_pair/pallas_call | solution.py:515
  101.1 2.4 %collective-permute-start.6 = (bf16[64,8,128]{2,1,0:T(8,128)(2,1)}, bf16[64,8,128]{2,1,0:T(8,128)(2,1)S(1)}, u32[]{:S(2)}, u32[]{:S(2)}) collective-permute-start(bf16[64,8,128]{2,1,0:T(8,128)(2,1)} %get-tuple-element.52), channel_id=1, source_target_pairs={{0,4},{1,5},{2,6},{3,7},{4,0},{5,1},{6,2},{7,3},{8,12},{9,13},{10,... | collective-permute-start | bytes 393224 | tf_op jit(solution)/shard_map/ppermute | solution.py:534
  104.7 5.5 %all-to-all-done.1.came = bf16[768,8,128]{2,1,0:T(8,128)(2,1)} async-done(((bf16[768,8,128]{2,1,0:T(8,128)(2,1)}), bf16[768,8,128]{2,1,0:T(8,128)(2,1)}, u32[]{:S(2)}, u32[]{:S(2)}) %all-to-all-start.1) | async-done | bytes 1572896 | tf_op jit(solution)/shard_map/all_to_all | solution.py:585
  110.2 1.4 copy-done
  111.6 2.2 %stride_term.1 = (bf16[1536,128]{1,0:T(8,128)(2,1)S(1)}, bf16[512,128]{1,0:T(8,128)(2,1)S(1)}) custom-call(s32[192]{0:T(256)S(1)} %copy-done.9, bf16[768,8,128]{2,1,0:T(8,128)(2,1)} %all-to-all-done.1.came, bf16[1536,512]{1,0:T(8,128)(2,1)S(1)} %bitcast.58), custom_call_target="tpu_custom_call" | custom-call | tf_op jit(solution)/shard_map/stride_term/pallas_call | solution.py:552
  114.6 6.1 %all-to-all-start.2 = ((bf16[128,8,128]{2,1,0:T(8,128)(2,1)}), bf16[128,8,128]{2,1,0:T(8,128)(2,1)S(1)}, u32[]{:S(2)}, u32[]{:S(2)}) async-start(bf16[128,8,128]{2,1,0:T(8,128)(2,1)} %bitcast.17), calls=%async_computation.2 | async-start | bytes 524288 | tf_op jit(solution)/shard_map/all_to_all | solution.py:585
  120.7 1.7 %convolution_convert_fusion = bf16[1536,512]{1,0:T(8,128)(2,1)} fusion(bf16[1536,128]{1,0:T(8,128)(2,1)S(1)} %get-tuple-element.62, bf16[512,128]{1,0:T(8,128)(2,1)S(1)} %copy-done.13), kind=kOutput, calls=%fused_computation | convolution fusion | flops 202113024 | bytes 2097152 | tf_op jit(solution)/shard_map/dot_general | solution.py:664
  122.4 9.4 %all-to-all-done.2 = bf16[128,8,128]{2,1,0:T(8,128)(2,1)S(1)} async-done(((bf16[128,8,128]{2,1,0:T(8,128)(2,1)}), bf16[128,8,128]{2,1,0:T(8,128)(2,1)S(1)}, u32[]{:S(2)}, u32[]{:S(2)}) %all-to-all-start.2) | async-done | bytes 262176 | tf_op jit(solution)/shard_map/all_to_all | solution.py:585
  132.0 20.3 %all_to_all.20 = bf16[128,20,128]{2,1,0:T(8,128)(2,1)S(1)} all-to-all(bf16[128,20,128]{2,1,0:T(8,128)(2,1)S(1)} %bitcast.65), channel_id=1, replica_groups=mesh['gx'=16,'gy'=8] {'gx','gy'}, dimensions={0} | all-to-all | bytes 1310720 | tf_op jit(solution)/shard_map/all_to_all | solution.py:585
  152.3 1.3 collective-permute-start.8
  155.3 1.3 convert_multiply_fusion
  (80 shorter events, 12.5 us)
Async XLA Ops:
  4.9 11.9 %copy-start.10 = (bf16[27,128,128]{2,1,0:T(8,128)(2,1)S(1)}, bf16[27,128,128]{2,1,0:T(8,128)(2,1)}, u32[]{:S(2)}) copy-start(bf16[27,128,128]{2,1,0:T(8,128)(2,1)} %param.11) | copy-start | bytes 2654212
  4.9 36.2 %all-to-all-start = ((bf16[768,8,128]{2,1,0:T(8,128)(2,1)}), bf16[768,8,128]{2,1,0:T(8,128)(2,1)}, u32[]{:S(2)}, u32[]{:S(2)}) async-start(bf16[768,8,128]{2,1,0:T(8,128)(2,1)} %get-tuple-element.34), calls=%async_computation | async-start | bytes 3145728 | tf_op jit(solution)/shard_map/all_to_all | solution.py:585
  18.2 4.0 %copy-start.16 = (s32[768]{0:T(1024)S(1)}, s32[768]{0:T(1024)}, u32[]{:S(2)}) copy-start(s32[768]{0:T(1024)} %param.9) | copy-start | bytes 9220
  18.2 5.2 %copy-start.15 = (s32[8,8,48]{2,1,0:T(8,128)S(1)}, s32[8,8,48]{2,1,0:T(8,128)}, u32[]{:S(2)}) copy-start(s32[8,8,48]{2,1,0:T(8,128)} %param.13) | copy-start | bytes 36868
  23.4 2.7 %copy-start.11 = (bf16[3,3,128,2,128]{4,3,2,1,0:T(2,128)(2,1)S(1)}, bf16[3,3,128,2,128]{4,3,2,1,0:T(2,128)(2,1)}, u32[]{:S(2)}) copy-start(bf16[3,3,128,2,128]{4,3,2,1,0:T(2,128)(2,1)} %copy.58) | copy-start | bytes 1769476
  23.4 2.7 %copy-start.12 = (bf16[3,3,128,2,128]{4,3,2,1,0:T(2,128)(2,1)S(1)}, bf16[3,3,128,2,128]{4,3,2,1,0:T(2,128)(2,1)}, u32[]{:S(2)}) copy-start(bf16[3,3,128,2,128]{4,3,2,1,0:T(2,128)(2,1)} %copy.56) | copy-start | bytes 1769476
  26.1 22.4 %copy-start.17 = (bf16[128,8]{0,1:T(8,128)(2,1)S(1)}, bf16[128,8]{0,1:T(8,128)(2,1)}, u32[]{:S(2)}) copy-start(bf16[128,8]{0,1:T(8,128)(2,1)} %param.12) | copy-start | bytes 6148
  44.9 10.6 %collective-permute-start = (bf16[2,400,128]{2,1,0:T(8,128)(2,1)}, bf16[2,400,128]{2,1,0:T(8,128)(2,1)S(1)}, u32[]{:S(2)}, u32[]{:S(2)}) collective-permute-start(bf16[2,400,128]{2,1,0:T(8,128)(2,1)} %get-tuple-element.39), channel_id=1, source_target_pairs={{0,8},{8,16},{16,24},{24,32},{32,40},{40,48},{48,56},{56,64},{64,7... | collective-permute-start | bytes 614408 | tf_op jit(solution)/shard_map/ppermute | solution.py:592
  47.2 8.2 %collective-permute-start.1 = (bf16[2,400,128]{2,1,0:T(8,128)(2,1)}, bf16[2,400,128]{2,1,0:T(8,128)(2,1)S(1)}, u32[]{:S(2)}, u32[]{:S(2)}) collective-permute-start(bf16[2,400,128]{2,1,0:T(8,128)(2,1)} %get-tuple-element.40), channel_id=1, source_target_pairs={{8,0},{16,8},{24,16},{32,24},{40,32},{48,40},{56,48},{64,56},{72,6... | collective-permute-start | bytes 614408 | tf_op jit(solution)/shard_map/ppermute | solution.py:592
  48.7 1.2 copy-start.1
  49.8 1.1 copy-start.3
  51.0 1.1 copy-start.6
  52.0 8.5 %copy-start.4 = (bf16[1536,256]{1,0:T(8,128)(2,1)S(1)}, bf16[1536,256]{1,0:T(8,128)(2,1)}, u32[]{:S(2)}) copy-start(bf16[1536,256]{1,0:T(8,128)(2,1)} %get-tuple-element.42.w_mid) | copy-start | bytes 2359300
  52.0 8.5 %copy-start.7 = (bf16[1152,256]{1,0:T(8,128)(2,1)S(1)}, bf16[1152,256]{1,0:T(8,128)(2,1)}, u32[]{:S(2)}) copy-start(bf16[1152,256]{1,0:T(8,128)(2,1)} %get-tuple-element.41.w_side) | copy-start | bytes 1769476
  55.5 7.5 %collective-permute-start.2 = (bf16[12,112,128]{2,1,0:T(8,128)(2,1)S(1)}, bf16[12,112,128]{2,1,0:T(8,128)(2,1)S(1)}, u32[]{:S(2)}, u32[]{:S(2)}) collective-permute-start(bf16[12,112,128]{2,1,0:T(8,128)(2,1)S(1)} %get-tuple-element.43), channel_id=1, source_target_pairs={{0,1},{1,2},{2,3},{3,4},{4,5},{5,6},{6,7},{8,9},{9,10},{10,11},{11... | collective-permute-start | bytes 1032200 | tf_op jit(solution)/shard_map/ppermute | solution.py:592
  58.1 8.7 %copy-start.2 = (bf16[8,400,128]{2,1,0:T(8,128)(2,1)S(1)}, bf16[8,400,128]{2,1,0:T(8,128)(2,1)}, u32[]{:S(2)}) copy-start(bf16[8,400,128]{2,1,0:T(8,128)(2,1)} %get-tuple-element.38.slab) | copy-start | bytes 2457604
  58.1 8.7 %copy-start.5 = (bf16[1152,256]{1,0:T(8,128)(2,1)S(1)}, bf16[1152,256]{1,0:T(8,128)(2,1)}, u32[]{:S(2)}) copy-start(bf16[1152,256]{1,0:T(8,128)(2,1)} %get-tuple-element.45.w_side_t) | copy-start | bytes 1769476
  58.1 8.7 %collective-permute-start.3 = (bf16[12,112,128]{2,1,0:T(8,128)(2,1)S(1)}, bf16[12,112,128]{2,1,0:T(8,128)(2,1)S(1)}, u32[]{:S(2)}, u32[]{:S(2)}) collective-permute-start(bf16[12,112,128]{2,1,0:T(8,128)(2,1)S(1)} %get-tuple-element.44), channel_id=1, source_target_pairs={{1,0},{2,1},{3,2},{4,3},{5,4},{6,5},{7,6},{9,8},{10,9},{11,10},{12... | collective-permute-start | bytes 1032200 | tf_op jit(solution)/shard_map/ppermute | solution.py:592
  77.0 33.2 %all-to-all-start.1 = ((bf16[768,8,128]{2,1,0:T(8,128)(2,1)}), bf16[768,8,128]{2,1,0:T(8,128)(2,1)}, u32[]{:S(2)}, u32[]{:S(2)}) async-start(bf16[768,8,128]{2,1,0:T(8,128)(2,1)} %get-tuple-element.55), calls=%async_computation.1 | async-start | bytes 3145728 | tf_op jit(solution)/shard_map/all_to_all | solution.py:585
  85.9 24.3 %copy-start.9 = (s32[192]{0:T(256)S(1)}, s32[192]{0:T(256)}, u32[]{:S(2)}) copy-start(s32[192]{0:T(256)} %get-tuple-element.54.place) | copy-start | bytes 2308
  94.4 3.0 %collective-permute-start.4 = (bf16[16,128,128]{2,1,0:T(8,128)(2,1)}, bf16[16,128,128]{2,1,0:T(8,128)(2,1)S(1)}, u32[]{:S(2)}, u32[]{:S(2)}) collective-permute-start(bf16[16,128,128]{2,1,0:T(8,128)(2,1)} %get-tuple-element.49), channel_id=1, source_target_pairs={{0,1},{1,0},{2,3},{3,2},{4,5},{5,4},{6,7},{7,6},{8,9},{9,8},{10,11... | collective-permute-start | bytes 1572872 | tf_op jit(solution)/shard_map/ppermute | solution.py:530
  97.3 0.8 copy-start.14
  100.5 13.3 %collective-permute-start.5 = (bf16[64,8,128]{2,1,0:T(8,128)(2,1)}, bf16[64,8,128]{2,1,0:T(8,128)(2,1)S(1)}, u32[]{:S(2)}, u32[]{:S(2)}) collective-permute-start(bf16[64,8,128]{2,1,0:T(8,128)(2,1)} %get-tuple-element.51), channel_id=1, source_target_pairs={{0,2},{1,3},{2,4},{3,5},{4,6},{5,7},{6,0},{7,1},{8,10},{9,11},{10,... | collective-permute-start | bytes 393224 | tf_op jit(solution)/shard_map/ppermute | solution.py:534
  101.1 12.7 %collective-permute-start.6 = (bf16[64,8,128]{2,1,0:T(8,128)(2,1)}, bf16[64,8,128]{2,1,0:T(8,128)(2,1)S(1)}, u32[]{:S(2)}, u32[]{:S(2)}) collective-permute-start(bf16[64,8,128]{2,1,0:T(8,128)(2,1)} %get-tuple-element.52), channel_id=1, source_target_pairs={{0,4},{1,5},{2,6},{3,7},{4,0},{5,1},{6,2},{7,3},{8,12},{9,13},{10,... | collective-permute-start | bytes 393224 | tf_op jit(solution)/shard_map/ppermute | solution.py:534
  103.5 10.2 %collective-permute-start.7 = (bf16[64,8,128]{2,1,0:T(8,128)(2,1)}, bf16[64,8,128]{2,1,0:T(8,128)(2,1)S(1)}, u32[]{:S(2)}, u32[]{:S(2)}) collective-permute-start(bf16[64,8,128]{2,1,0:T(8,128)(2,1)} %get-tuple-element.53), channel_id=1, source_target_pairs={{0,6},{1,7},{2,0},{3,1},{4,2},{5,3},{6,4},{7,5},{8,14},{9,15},{10,... | collective-permute-start | bytes 393224 | tf_op jit(solution)/shard_map/ppermute | solution.py:534
  110.2 1.4 copy-start
  111.6 2.2 %copy-start.8 = (f32[64,8,128]{2,1,0:T(8,128)S(1)}, f32[64,8,128]{2,1,0:T(8,128)}, u32[]{:S(2)}) copy-start(f32[64,8,128]{2,1,0:T(8,128)} %get-tuple-element.58.refs_0_) | copy-start | bytes 786436
  111.6 9.1 %copy-start.13 = (bf16[512,128]{1,0:T(8,128)(2,1)S(1)}, bf16[512,128]{1,0:T(8,128)(2,1)}, u32[]{:S(2)}) copy-start(bf16[512,128]{1,0:T(8,128)(2,1)} %w_hbm.1) | copy-start | bytes 393220
  114.6 17.2 %all-to-all-start.2 = ((bf16[128,8,128]{2,1,0:T(8,128)(2,1)}), bf16[128,8,128]{2,1,0:T(8,128)(2,1)S(1)}, u32[]{:S(2)}, u32[]{:S(2)}) async-start(bf16[128,8,128]{2,1,0:T(8,128)(2,1)} %bitcast.17), calls=%async_computation.2 | async-start | bytes 524288 | tf_op jit(solution)/shard_map/all_to_all | solution.py:585
  152.3 2.8 %collective-permute-start.8 = (bf16[2048,128]{1,0:T(8,128)(2,1)S(1)}, bf16[2048,128]{1,0:T(8,128)(2,1)S(1)}, u32[]{:S(2)}, u32[]{:S(2)}) collective-permute-start(bf16[2048,128]{1,0:T(8,128)(2,1)S(1)} %bitcast.60), channel_id=1, source_target_pairs={{0,1},{1,0},{2,3},{3,2},{4,5},{5,4},{6,7},{7,6},{8,9},{9,8},{10,11... | collective-permute-start | bytes 1572872 | tf_op jit(solution)/shard_map/ppermute | solution.py:679

commit v5 on v4

--- a/solution.py
+++ b/solution.py
@@ -143,16 +143,24 @@
 
     for j in range(index.shape[0]):
         held[index[j]] = arrived[j]
+    deep = SZ // 2
     for big_x in range(SX // 2):
-        for big_y in range(SY // 2):
-            start = (big_x * (SY // 2) + big_y) * (SZ // 2)
-            block = held[start : start + SZ // 2].astype(F32).reshape(4 * SZ, CH).astype(BF)
+        for half in range(SY // 4):
+            start = (big_x * (SY // 2) + 2 * half) * deep
+            block = jnp.concatenate(
+                [
+                    held[at : at + deep].astype(F32).reshape(4 * SZ, CH)
+                    for at in (start, start + deep)
+                ],
+                axis=1,
+            ).astype(BF)
             moved = matmul(order[...], block).astype(BF)
             for i in range(2):
                 for l in range(2):
                     piece = moved[(2 * i + l) * SZ : (2 * i + l + 1) * SZ]
-                    row = (2 * big_y + l) * SZ
-                    slab[2 * big_x + i, row : row + SZ, :] = piece
+                    for j in range(2):
+                        row = (4 * half + 2 * j + l) * SZ
+                        slab[2 * big_x + i, row : row + SZ, :] = piece[:, j * CH : (j + 1) * CH]
     slab[:, ROWS:, :] = code[...]
     first[...] = slab[:2]
     last[...] = slab[SX - 2 :]
@@ -210,7 +218,7 @@
 
 def spread_codes(blocks):
     eye = (iota((SZ, CH), 0) == iota((SZ, CH), 1)).astype(F32)
-    return jnp.concatenate([eye * block for block in blocks], axis=0).astype(BF)
+    return jnp.concatenate([eye * block for block in blocks], axis=0)
 
 
 def convolve(columns, w_side, w_mid):
@@ -230,7 +238,7 @@
     z = iota((rows // SZ, SZ, CH), 1).reshape(rows, CH)
     below, middle, above = convolve(columns, w_side, w_mid)
     pre = shifted(below, z, 1) + middle + shifted(above, z, -1)
-    code = matmul(spread, jnp.ones((CH, CH), BF))
+    code = jnp.sum(spread, axis=1, keepdims=True)
     mask = code > 0.5
     pre = jnp.where(mask, pre, 0.0)
     gate = jax.nn.sigmoid(pre)
@@ -392,19 +400,28 @@
 
     lax.fori_loop(0, SX // 2, backward, 0, unroll=4)
 
+    deep = SZ // 2
     for big_x in range(SX // 2):
-        for big_y in range(SY // 2):
+        for half in range(SY // 4):
             block = jnp.concatenate(
                 [
-                    coarse[2 * big_x + i, (2 * big_y + l) * SZ : (2 * big_y + l + 1) * SZ, :]
-                    for i in range(2)
-                    for l in range(2)
+                    jnp.concatenate(
+                        [
+                            coarse[2 * big_x + i, (2 * big_y + l) * SZ : (2 * big_y + l + 1) * SZ, :]
+                            for i in range(2)
+                            for l in range(2)
+                        ],
+                        axis=0,
+                    )
+                    for big_y in (2 * half, 2 * half + 1)
                 ],
-                axis=0,
+                axis=1,
             )
-            start = (big_x * (SY // 2) + big_y) * (SZ // 2)
-            moved = matmul(order_t[...], block).reshape(SZ // 2, CELLS, CH)
-            held[start : start + SZ // 2] = moved.astype(BF)
+            moved = matmul(order_t[...], block)
+            for j in range(2):
+                start = (big_x * (SY // 2) + 2 * half + j) * deep
+                one = moved[:, j * CH : (j + 1) * CH].reshape(deep, CELLS, CH)
+                held[start : start + deep] = one.astype(BF)
 
     part = index.shape[0] // PARTS
     for i in range(PARTS):
@@ -443,10 +460,15 @@
     )(index, *arrays)
 
 
-def weights_kernel(half, kept_hbm, keep, give, kept, total, taps_out, sem):
-    copy = pltpu.make_async_copy(kept_hbm.at[pl.ds(0, FX + SX)], kept, sem)
-    copy.start()
-    copy.wait()
+def weights_kernel(half, kept_hbm, keep, give, kept, total, taps_out, sems):
+    half_x = SX // 2
+    copies = []
+    for i, (at, many) in enumerate(
+        ((0, half_x + 3), (FX, half_x), (half_x + 3, FX - half_x - 3), (FX + half_x, half_x))
+    ):
+        slabs = pl.ds(at, many)
+        copies.append(pltpu.make_async_copy(kept_hbm.at[slabs], kept.at[slabs], sems.at[i]))
+        copies[-1].start()
     z_own = iota((SY, SZ, CH), 1).reshape(ROWS, CH)
     total[...] = jnp.zeros_like(total)
 
@@ -466,7 +488,10 @@
             )
         return carry
 
-    lax.fori_loop(0, SX, add, 0, unroll=2)
+    for part in range(2):
+        copies[2 * part].wait()
+        copies[2 * part + 1].wait()
+        lax.fori_loop(half_x * part, half_x * (part + 1), add, 0, unroll=2)
     for tap in range(27):
         e, f, g = tap // 9, tap // 3 % 3, tap % 3
         taps_out[tap] = total[e, f * CH : (f + 1) * CH, g * CH : (g + 1) * CH]
@@ -487,7 +512,7 @@
             pltpu.VMEM((FX + SX, FY * SZ, CH), BF),
             pltpu.VMEM((3, 3 * CH, 3 * CH), F32),
             pltpu.VMEM((32, CH, CH), F32),
-            pltpu.SemaphoreType.DMA,
+            pltpu.SemaphoreType.DMA((4,)),
         ],
         compiler_params=ALL_VMEM,
         cost_estimate=pl.CostEstimate(
@@ -545,6 +570,24 @@
     stride[...] = lax.dot_general(
         feats[...], vals, (((0,), (0,)), ((), ())), preferred_element_type=F32
     ).astype(BF)
+
+
+def fetch_kernel(source, out, sem):
+    copy = pltpu.make_async_copy(source, out, sem)
+    copy.start()
+    copy.wait()
+
+
+def fetch(feats):
+    return pl.pallas_call(
+        fetch_kernel,
+        out_shape=jax.ShapeDtypeStruct(feats.shape, BF),
+        in_specs=[hbm()],
+        out_specs=whole(feats.shape),
+        scratch_shapes=[pltpu.SemaphoreType.DMA],
+        compiler_params=VMEM,
+        name="fetch_feats",
+    )(feats)
 
 
 def last(came, place, feats):
@@ -657,6 +700,10 @@
     came = to_all(returned)
     half = (lax.axis_index("gy") % 2).astype(jnp.int32).reshape(1)
     terms = sum_over_gy(*weights(half, kept), devs)
+    feats, first_term = lax.optimization_barrier((feats, terms[0]))
+    terms = (first_term,) + tuple(terms[1:])
+    feats = fetch(feats)
+    came, feats = lax.optimization_barrier((came, feats))
     mine, stride = last(came, place, feats)
     terms, stride = lax.optimization_barrier((terms, stride))
     share = rows = 4

time: 157 us -> 157 us (level)
  no operation moved by 1% of the time
where the time goes in v5:
time: 157 us; the launch traced here: 156 us
  starting transfers between devices  43.6 us (28%)
  Pallas kernels  37 us (24%)
  waiting for transfers between devices  33.7 us (21%)
  blocking collectives  20.3 us (13%)
  local copies, waits for them, and re-layouts  14.5 us (9%)
  other arithmetic  4.1 us (3%)
  matrix products  1.71 us (1%)
    all_to_all x3, starting transfers between devices, to_all(): lax.all_to_all(buffer, ('gx', 'gy'), split_axis=0, concat_axis=0, tiled=T...  28.1 us
    all_to_all x3, waiting for transfers between devices, to_all(): lax.all_to_all(buffer, ('gx', 'gy'), split_axis=0, concat_axis=0, tiled=T...  27.3 us
    all_to_all x1, blocking collectives, to_all(): lax.all_to_all(buffer, ('gx', 'gy'), split_axis=0, concat_axis=0, tiled=T...  20.3 us
    pallas_call x1, Pallas kernels, core(): pl.pallas_call(core_kernel, out_shape=tuple((jax.ShapeDtypeStruct(s, BF)...  10 us
    ppermute x4, starting transfers between devices, both_ways(): return (lax.ppermute(last_part, axis, up), lax.ppermute(first, axis, down))  8.61 us
    pallas_call x1, Pallas kernels, weights(): pl.pallas_call(weights_kernel, out_shape=(jax.ShapeDtypeStruct(shape, F32...  7.91 us
    unnamed x36, local copies, waits for them, and re-layouts  5.6 us
    pallas_call x1, Pallas kernels, send(): pl.pallas_call(functools.partial(send_kernel, cap), out_shape=(jax.ShapeD...  4.28 us
  transfers between devices with their start and end apart: 12, of which 6 were waited for; matrix products, arithmetic and copies ran while one was open for 8% of the time, Pallas kernels for 12%

profile of v5, /device:TPU:1, one launch (start us, length us, event | category | flops | bytes accessed | tf_op | source)
XLA Modules:
  0.0 156.1 jit_solution(4680174682061664767)
XLA Ops:
  0.6 4.3 %send_bricks.1 = (bf16[768,8,128]{2,1,0:T(8,128)(2,1)}, s32[192]{0:T(256)}) custom-call(s32[192]{0:T(256)} %owner_hbm.1, bf16[1536,512]{1,0:T(8,128)(2,1)} %bitcast.57, bf16[512,128]{1,0:T(8,128)(2,1)} %w_hbm.1), custom_call_target="tpu_custom_call" | custom-call | tf_op jit(solution)/shard_map/send_bricks/pallas_call | solution.py:112
  4.9 11.9 %all-to-all-start = ((bf16[768,8,128]{2,1,0:T(8,128)(2,1)}), bf16[768,8,128]{2,1,0:T(8,128)(2,1)}, u32[]{:S(2)}, u32[]{:S(2)}) async-start(bf16[768,8,128]{2,1,0:T(8,128)(2,1)} %get-tuple-element.38), calls=%async_computation | async-start | bytes 3145728 | tf_op jit(solution)/shard_map/all_to_all | solution.py:628
  19.0 1.7 %copy.58 = bf16[3,3,128,2,128]{4,3,2,1,0:T(2,128)(2,1)} copy(bf16[3,3,128,2,128]{2,4,3,1,0:T(8,128)(2,1)S(1)} %slice_bitcast_fusion) | data formatting | bytes 1179648 | tf_op jit(solution)/shard_map/transpose | solution.py:649
  20.8 1.4 copy.56
  24.9 1.2 copy_bitcast_fusion
  26.1 1.3 copy_bitcast_fusion.2
  27.5 13.6 %all-to-all-done.arrived = bf16[768,8,128]{2,1,0:T(8,128)(2,1)} async-done(((bf16[768,8,128]{2,1,0:T(8,128)(2,1)}), bf16[768,8,128]{2,1,0:T(8,128)(2,1)}, u32[]{:S(2)}, u32[]{:S(2)}) %all-to-all-start) | async-done | bytes 1572896 | tf_op jit(solution)/shard_map/all_to_all | solution.py:628
  41.1 3.5 %land_bricks.1 = (bf16[8,400,128]{2,1,0:T(8,128)(2,1)}, bf16[2,400,128]{2,1,0:T(8,128)(2,1)}, bf16[2,400,128]{2,1,0:T(8,128)(2,1)}) custom-call(s32[768]{0:T(1024)} %get-tuple-element.74.index, bf16[768,8,128]{2,1,0:T(8,128)(2,1)} %all-to-all-done.arrived, bf16[192,192]{1,0:T(8,128)(2,1)} %get-tuple-element.80.order, bf16[8,16,128]{2,1,0:T(8,128)(2,1)} %pad.26.code), custom_call_target="tpu_custom_call" | custom-call | tf_op jit(solution)/shard_map/land_bricks/pallas_call | solution.py:171
  44.6 2.3 %collective-permute-start = (bf16[2,400,128]{2,1,0:T(8,128)(2,1)}, bf16[2,400,128]{2,1,0:T(8,128)(2,1)S(1)}, u32[]{:S(2)}, u32[]{:S(2)}) collective-permute-start(bf16[2,400,128]{2,1,0:T(8,128)(2,1)} %get-tuple-element.43), channel_id=1, source_target_pairs={{0,8},{8,16},{16,24},{24,32},{32,40},{40,48},{48,56},{56,64},{64,7... | collective-permute-start | bytes 614408 | tf_op jit(solution)/shard_map/ppermute | solution.py:635
  47.0 1.3 collective-permute-start.1
  48.4 1.1 copy-done.1
  51.8 3.4 %grad_pre_inside.1.inside = bf16[6,288,128]{2,1,0:T(8,128)(2,1)S(1)} custom-call(bf16[8,400,128]{2,1,0:T(8,128)(2,1)S(1)} %copy-done.1, bf16[1152,256]{1,0:T(8,128)(2,1)S(1)} %copy-done.6, bf16[1536,256]{1,0:T(8,128)(2,1)S(1)} %copy-done.3, bf16[128,128]{1,0:T(8,128)(2,1)S(1)} %copy.62.head, bf16[128,128]{1,0:T(8,128)(2,1)S(1)} %get-tuple-element.82.head_t), custom_call_target="tpu_custom_call" | custom-call | flops 1528823808 | bytes 4194304 | tf_op jit(solution)/shard_map/grad_pre_inside/pallas_call | solution.py:283
  55.3 2.6 %collective-permute-start.2 = (bf16[12,112,128]{2,1,0:T(8,128)(2,1)S(1)}, bf16[12,112,128]{2,1,0:T(8,128)(2,1)S(1)}, u32[]{:S(2)}, u32[]{:S(2)}) collective-permute-start(bf16[12,112,128]{2,1,0:T(8,128)(2,1)S(1)} %get-tuple-element.47), channel_id=1, source_target_pairs={{0,1},{1,2},{2,3},{3,4},{4,5},{5,6},{6,7},{8,9},{9,10},{10,11},{11... | collective-permute-start | bytes 1032200 | tf_op jit(solution)/shard_map/ppermute | solution.py:635
  57.9 2.4 %collective-permute-start.3 = (bf16[12,112,128]{2,1,0:T(8,128)(2,1)S(1)}, bf16[12,112,128]{2,1,0:T(8,128)(2,1)S(1)}, u32[]{:S(2)}, u32[]{:S(2)}) collective-permute-start(bf16[12,112,128]{2,1,0:T(8,128)(2,1)S(1)} %get-tuple-element.48), channel_id=1, source_target_pairs={{1,0},{2,1},{3,2},{4,3},{5,4},{6,5},{7,6},{9,8},{10,9},{11,10},{12... | collective-permute-start | bytes 1032200 | tf_op jit(solution)/shard_map/ppermute | solution.py:635
  60.3 2.4 %grad_pre_x_sides.1.at_x = bf16[4,288,128]{2,1,0:T(8,128)(2,1)S(1)} custom-call(bf16[8,400,128]{2,1,0:T(8,128)(2,1)S(1)} %copy-done.1, bf16[2,400,128]{2,1,0:T(8,128)(2,1)S(1)} %collective-permute-done.before, bf16[2,400,128]{2,1,0:T(8,128)(2,1)S(1)} %collective-permute-done.1.after, bf16[1152,256]{1,0:T(8,128)(2,1)S(1)} %copy-done.7, ...), custom_call_target="tpu_custom_call" | custom-call | flops 1019215872 | bytes 4194304 | tf_op jit(solution)/shard_map/grad_pre_x_sides/pallas_call | solution.py:319
  62.7 3.9 %collective-permute-done.3.right = bf16[12,112,128]{2,1,0:T(8,128)(2,1)S(1)} collective-permute-done((bf16[12,112,128]{2,1,0:T(8,128)(2,1)S(1)}, bf16[12,112,128]{2,1,0:T(8,128)(2,1)S(1)}, u32[]{:S(2)}, u32[]{:S(2)}) %collective-permute-start.3) | collective-permute-done | bytes 344096 | tf_op jit(solution)/shard_map/ppermute | solution.py:635
  66.6 10.0 %conv_both_ways.1 = (bf16[768,8,128]{2,1,0:T(8,128)(2,1)}, bf16[84,576,128]{2,1,0:T(8,128)(2,1)}) custom-call(s32[768]{0:T(1024)S(1)} %get-tuple-element.73.index, bf16[8,400,128]{2,1,0:T(8,128)(2,1)S(1)} %copy-done.2, bf16[2,400,128]{2,1,0:T(8,128)(2,1)S(1)} %collective-permute-done.before, bf16[2,400,128]{2,1,0:T(8,128)(2,1)S(1)} %collective-permute-done.1.after, ...), custom_call_target="tpu_custom_call" | custom-call | tf_op jit(solution)/shard_map/conv_both_ways/pallas_call | solution.py:443
  76.7 8.9 %all-to-all-start.1 = ((bf16[768,8,128]{2,1,0:T(8,128)(2,1)}), bf16[768,8,128]{2,1,0:T(8,128)(2,1)}, u32[]{:S(2)}, u32[]{:S(2)}) async-start(bf16[768,8,128]{2,1,0:T(8,128)(2,1)} %get-tuple-element.60), calls=%async_computation.1 | async-start | bytes 3145728 | tf_op jit(solution)/shard_map/all_to_all | solution.py:628
  85.6 7.9 %conv_weight_grad.1 = (f32[16,128,128]{2,1,0:T(8,128)}, bf16[16,128,128]{2,1,0:T(8,128)(2,1)}) custom-call(s32[1]{0:T(128)} %bitcast.2.half, bf16[84,576,128]{2,1,0:T(8,128)(2,1)} %get-tuple-element.51.kept_hbm), custom_call_target="tpu_custom_call" | custom-call | flops 2717908992 | bytes 6291456 | tf_op jit(solution)/shard_map/conv_weight_grad/pallas_call | solution.py:506
  93.5 1.4 collective-permute-start.4
  94.9 1.7 %collective-permute-done.4 = bf16[16,128,128]{2,1,0:T(8,128)(2,1)S(1)} collective-permute-done((bf16[16,128,128]{2,1,0:T(8,128)(2,1)}, bf16[16,128,128]{2,1,0:T(8,128)(2,1)S(1)}, u32[]{:S(2)}, u32[]{:S(2)}) %collective-permute-start.4) | collective-permute-done | bytes 524320 | tf_op jit(solution)/shard_map/ppermute | solution.py:555
  97.5 2.3 %add_pair.1 = (f32[64,8,128]{2,1,0:T(8,128)}, bf16[64,8,128]{2,1,0:T(8,128)(2,1)}, bf16[64,8,128]{2,1,0:T(8,128)(2,1)}, bf16[64,8,128]{2,1,0:T(8,128)(2,1)}) custom-call(s32[1]{0:T(128)} %bitcast.1.me, f32[64,2,2,8,128]{4,3,2,1,0:T(8,128)} %bitcast.72, bf16[128,16,128]{2,1,0:T(8,128)(2,1)} %bitcast.74), custom_call_target="tpu_custom_call" | custom-call | tf_op jit(solution)/shard_map/add_pair/pallas_call | solution.py:540
  100.4 2.4 %collective-permute-start.6 = (bf16[64,8,128]{2,1,0:T(8,128)(2,1)}, bf16[64,8,128]{2,1,0:T(8,128)(2,1)S(1)}, u32[]{:S(2)}, u32[]{:S(2)}) collective-permute-start(bf16[64,8,128]{2,1,0:T(8,128)(2,1)} %get-tuple-element.57), channel_id=1, source_target_pairs={{0,4},{1,5},{2,6},{3,7},{4,0},{5,1},{6,2},{7,3},{8,12},{9,13},{10,... | collective-permute-start | bytes 393224 | tf_op jit(solution)/shard_map/ppermute | solution.py:559
  104.0 1.4 copy-done
  105.6 4.3 %all-to-all-done.1.came = bf16[768,8,128]{2,1,0:T(8,128)(2,1)} async-done(((bf16[768,8,128]{2,1,0:T(8,128)(2,1)}), bf16[768,8,128]{2,1,0:T(8,128)(2,1)}, u32[]{:S(2)}, u32[]{:S(2)}) %all-to-all-start.1) | async-done | bytes 1572896 | tf_op jit(solution)/shard_map/all_to_all | solution.py:628
  109.8 2.1 %stride_term.1 = (bf16[1536,128]{1,0:T(8,128)(2,1)S(1)}, bf16[512,128]{1,0:T(8,128)(2,1)S(1)}) custom-call(s32[192]{0:T(256)S(1)} %copy-done.9, bf16[768,8,128]{2,1,0:T(8,128)(2,1)} %all-to-all-done.1.came, bf16[1536,512]{1,0:T(8,128)(2,1)S(1)} %fetch_feats.1.feats), custom_call_target="tpu_custom_call" | custom-call | tf_op jit(solution)/shard_map/stride_term/pallas_call | solution.py:595
  112.8 7.3 %all-to-all-start.2 = ((bf16[128,8,128]{2,1,0:T(8,128)(2,1)}), bf16[128,8,128]{2,1,0:T(8,128)(2,1)S(1)}, u32[]{:S(2)}, u32[]{:S(2)}) async-start(bf16[128,8,128]{2,1,0:T(8,128)(2,1)} %bitcast.17), calls=%async_computation.2 | async-start | bytes 524288 | tf_op jit(solution)/shard_map/all_to_all | solution.py:628
  120.1 1.7 %convolution_convert_fusion = bf16[1536,512]{1,0:T(8,128)(2,1)} fusion(bf16[1536,128]{1,0:T(8,128)(2,1)S(1)} %get-tuple-element.70, bf16[512,128]{1,0:T(8,128)(2,1)S(1)} %copy-done.13), kind=kOutput, calls=%fused_computation | convolution fusion | flops 202113024 | bytes 2097152 | tf_op jit(solution)/shard_map/dot_general | solution.py:711
  121.8 9.4 %all-to-all-done.2 = bf16[128,8,128]{2,1,0:T(8,128)(2,1)S(1)} async-done(((bf16[128,8,128]{2,1,0:T(8,128)(2,1)}), bf16[128,8,128]{2,1,0:T(8,128)(2,1)S(1)}, u32[]{:S(2)}, u32[]{:S(2)}) %all-to-all-start.2) | async-done | bytes 262176 | tf_op jit(solution)/shard_map/all_to_all | solution.py:628
  131.4 20.3 %all_to_all.20 = bf16[128,20,128]{2,1,0:T(8,128)(2,1)S(1)} all-to-all(bf16[128,20,128]{2,1,0:T(8,128)(2,1)S(1)} %bitcast.65), channel_id=1, replica_groups=mesh['gx'=16,'gy'=8] {'gx','gy'}, dimensions={0} | all-to-all | bytes 1310720 | tf_op jit(solution)/shard_map/all_to_all | solution.py:628
  151.7 1.3 collective-permute-start.8
  154.7 1.3 convert_multiply_fusion
  (81 shorter events, 12.6 us)
Async XLA Ops:
  4.9 11.9 %copy-start.10 = (bf16[27,128,128]{2,1,0:T(8,128)(2,1)S(1)}, bf16[27,128,128]{2,1,0:T(8,128)(2,1)}, u32[]{:S(2)}) copy-start(bf16[27,128,128]{2,1,0:T(8,128)(2,1)} %param.11) | copy-start | bytes 2654212
  4.9 36.2 %all-to-all-start = ((bf16[768,8,128]{2,1,0:T(8,128)(2,1)}), bf16[768,8,128]{2,1,0:T(8,128)(2,1)}, u32[]{:S(2)}, u32[]{:S(2)}) async-start(bf16[768,8,128]{2,1,0:T(8,128)(2,1)} %get-tuple-element.38), calls=%async_computation | async-start | bytes 3145728 | tf_op jit(solution)/shard_map/all_to_all | solution.py:628
  18.2 4.0 %copy-start.16 = (s32[768]{0:T(1024)S(1)}, s32[768]{0:T(1024)}, u32[]{:S(2)}) copy-start(s32[768]{0:T(1024)} %param.9) | copy-start | bytes 9220
  18.2 5.2 %copy-start.15 = (s32[8,8,48]{2,1,0:T(8,128)S(1)}, s32[8,8,48]{2,1,0:T(8,128)}, u32[]{:S(2)}) copy-start(s32[8,8,48]{2,1,0:T(8,128)} %param.13) | copy-start | bytes 36868
  23.4 2.7 %copy-start.11 = (bf16[3,3,128,2,128]{4,3,2,1,0:T(2,128)(2,1)S(1)}, bf16[3,3,128,2,128]{4,3,2,1,0:T(2,128)(2,1)}, u32[]{:S(2)}) copy-start(bf16[3,3,128,2,128]{4,3,2,1,0:T(2,128)(2,1)} %copy.58) | copy-start | bytes 1769476
  23.4 2.7 %copy-start.12 = (bf16[3,3,128,2,128]{4,3,2,1,0:T(2,128)(2,1)S(1)}, bf16[3,3,128,2,128]{4,3,2,1,0:T(2,128)(2,1)}, u32[]{:S(2)}) copy-start(bf16[3,3,128,2,128]{4,3,2,1,0:T(2,128)(2,1)} %copy.56) | copy-start | bytes 1769476
  26.1 22.1 %copy-start.17 = (bf16[128,8]{0,1:T(8,128)(2,1)S(1)}, bf16[128,8]{0,1:T(8,128)(2,1)}, u32[]{:S(2)}) copy-start(bf16[128,8]{0,1:T(8,128)(2,1)} %param.12) | copy-start | bytes 6148
  44.6 10.6 %collective-permute-start = (bf16[2,400,128]{2,1,0:T(8,128)(2,1)}, bf16[2,400,128]{2,1,0:T(8,128)(2,1)S(1)}, u32[]{:S(2)}, u32[]{:S(2)}) collective-permute-start(bf16[2,400,128]{2,1,0:T(8,128)(2,1)} %get-tuple-element.43), channel_id=1, source_target_pairs={{0,8},{8,16},{16,24},{24,32},{32,40},{40,48},{48,56},{56,64},{64,7... | collective-permute-start | bytes 614408 | tf_op jit(solution)/shard_map/ppermute | solution.py:635
  47.0 8.2 %collective-permute-start.1 = (bf16[2,400,128]{2,1,0:T(8,128)(2,1)}, bf16[2,400,128]{2,1,0:T(8,128)(2,1)S(1)}, u32[]{:S(2)}, u32[]{:S(2)}) collective-permute-start(bf16[2,400,128]{2,1,0:T(8,128)(2,1)} %get-tuple-element.44), channel_id=1, source_target_pairs={{8,0},{16,8},{24,16},{32,24},{40,32},{48,40},{56,48},{64,56},{72,6... | collective-permute-start | bytes 614408 | tf_op jit(solution)/shard_map/ppermute | solution.py:635
  48.4 1.2 copy-start.1
  49.6 1.1 copy-start.3
  50.7 1.1 copy-start.6
  51.8 8.5 %copy-start.4 = (bf16[1536,256]{1,0:T(8,128)(2,1)S(1)}, bf16[1536,256]{1,0:T(8,128)(2,1)}, u32[]{:S(2)}) copy-start(bf16[1536,256]{1,0:T(8,128)(2,1)} %get-tuple-element.46.w_mid) | copy-start | bytes 2359300
  51.8 8.5 %copy-start.7 = (bf16[1152,256]{1,0:T(8,128)(2,1)S(1)}, bf16[1152,256]{1,0:T(8,128)(2,1)}, u32[]{:S(2)}) copy-start(bf16[1152,256]{1,0:T(8,128)(2,1)} %get-tuple-element.45.w_side) | copy-start | bytes 1769476
  55.3 7.5 %collective-permute-start.2 = (bf16[12,112,128]{2,1,0:T(8,128)(2,1)S(1)}, bf16[12,112,128]{2,1,0:T(8,128)(2,1)S(1)}, u32[]{:S(2)}, u32[]{:S(2)}) collective-permute-start(bf16[12,112,128]{2,1,0:T(8,128)(2,1)S(1)} %get-tuple-element.47), channel_id=1, source_target_pairs={{0,1},{1,2},{2,3},{3,4},{4,5},{5,6},{6,7},{8,9},{9,10},{10,11},{11... | collective-permute-start | bytes 1032200 | tf_op jit(solution)/shard_map/ppermute | solution.py:635
  57.9 8.7 %copy-start.2 = (bf16[8,400,128]{2,1,0:T(8,128)(2,1)S(1)}, bf16[8,400,128]{2,1,0:T(8,128)(2,1)}, u32[]{:S(2)}) copy-start(bf16[8,400,128]{2,1,0:T(8,128)(2,1)} %get-tuple-element.42.slab) | copy-start | bytes 2457604
  57.9 8.7 %copy-start.5 = (bf16[1152,256]{1,0:T(8,128)(2,1)S(1)}, bf16[1152,256]{1,0:T(8,128)(2,1)}, u32[]{:S(2)}) copy-start(bf16[1152,256]{1,0:T(8,128)(2,1)} %get-tuple-element.49.w_side_t) | copy-start | bytes 1769476
  57.9 8.7 %collective-permute-start.3 = (bf16[12,112,128]{2,1,0:T(8,128)(2,1)S(1)}, bf16[12,112,128]{2,1,0:T(8,128)(2,1)S(1)}, u32[]{:S(2)}, u32[]{:S(2)}) collective-permute-start(bf16[12,112,128]{2,1,0:T(8,128)(2,1)S(1)} %get-tuple-element.48), channel_id=1, source_target_pairs={{1,0},{2,1},{3,2},{4,3},{5,4},{6,5},{7,6},{9,8},{10,9},{11,10},{12... | collective-permute-start | bytes 1032200 | tf_op jit(solution)/shard_map/ppermute | solution.py:635
  76.7 33.2 %all-to-all-start.1 = ((bf16[768,8,128]{2,1,0:T(8,128)(2,1)}), bf16[768,8,128]{2,1,0:T(8,128)(2,1)}, u32[]{:S(2)}, u32[]{:S(2)}) async-start(bf16[768,8,128]{2,1,0:T(8,128)(2,1)} %get-tuple-element.60), calls=%async_computation.1 | async-start | bytes 3145728 | tf_op jit(solution)/shard_map/all_to_all | solution.py:628
  93.5 3.2 %collective-permute-start.4 = (bf16[16,128,128]{2,1,0:T(8,128)(2,1)}, bf16[16,128,128]{2,1,0:T(8,128)(2,1)S(1)}, u32[]{:S(2)}, u32[]{:S(2)}) collective-permute-start(bf16[16,128,128]{2,1,0:T(8,128)(2,1)} %get-tuple-element.53), channel_id=1, source_target_pairs={{0,1},{1,0},{2,3},{3,2},{4,5},{5,4},{6,7},{7,6},{8,9},{9,8},{10,11... | collective-permute-start | bytes 1572872 | tf_op jit(solution)/shard_map/ppermute | solution.py:555
  96.7 0.8 copy-start.14
  99.8 10.0 %copy-start.9 = (s32[192]{0:T(256)S(1)}, s32[192]{0:T(256)}, u32[]{:S(2)}) copy-start(s32[192]{0:T(256)} %get-tuple-element.59.place) | copy-start | bytes 2308
  99.8 12.2 %collective-permute-start.5 = (bf16[64,8,128]{2,1,0:T(8,128)(2,1)}, bf16[64,8,128]{2,1,0:T(8,128)(2,1)S(1)}, u32[]{:S(2)}, u32[]{:S(2)}) collective-permute-start(bf16[64,8,128]{2,1,0:T(8,128)(2,1)} %get-tuple-element.56), channel_id=1, source_target_pairs={{0,2},{1,3},{2,4},{3,5},{4,6},{5,7},{6,0},{7,1},{8,10},{9,11},{10,... | collective-permute-start | bytes 393224 | tf_op jit(solution)/shard_map/ppermute | solution.py:559
  100.4 11.6 %collective-permute-start.6 = (bf16[64,8,128]{2,1,0:T(8,128)(2,1)}, bf16[64,8,128]{2,1,0:T(8,128)(2,1)S(1)}, u32[]{:S(2)}, u32[]{:S(2)}) collective-permute-start(bf16[64,8,128]{2,1,0:T(8,128)(2,1)} %get-tuple-element.57), channel_id=1, source_target_pairs={{0,4},{1,5},{2,6},{3,7},{4,0},{5,1},{6,2},{7,3},{8,12},{9,13},{10,... | collective-permute-start | bytes 393224 | tf_op jit(solution)/shard_map/ppermute | solution.py:559
  102.9 9.1 %collective-permute-start.7 = (bf16[64,8,128]{2,1,0:T(8,128)(2,1)}, bf16[64,8,128]{2,1,0:T(8,128)(2,1)S(1)}, u32[]{:S(2)}, u32[]{:S(2)}) collective-permute-start(bf16[64,8,128]{2,1,0:T(8,128)(2,1)} %get-tuple-element.58), channel_id=1, source_target_pairs={{0,6},{1,7},{2,0},{3,1},{4,2},{5,3},{6,4},{7,5},{8,14},{9,15},{10,... | collective-permute-start | bytes 393224 | tf_op jit(solution)/shard_map/ppermute | solution.py:559
  104.0 1.4 copy-start
  105.5 6.5 %copy-start.8 = (f32[64,8,128]{2,1,0:T(8,128)S(1)}, f32[64,8,128]{2,1,0:T(8,128)}, u32[]{:S(2)}) copy-start(f32[64,8,128]{2,1,0:T(8,128)} %get-tuple-element.66.refs_0_) | copy-start | bytes 786436
  105.5 14.6 %copy-start.13 = (bf16[512,128]{1,0:T(8,128)(2,1)S(1)}, bf16[512,128]{1,0:T(8,128)(2,1)}, u32[]{:S(2)}) copy-start(bf16[512,128]{1,0:T(8,128)(2,1)} %w_hbm.1) | copy-start | bytes 393220
  112.8 18.4 %all-to-all-start.2 = ((bf16[128,8,128]{2,1,0:T(8,128)(2,1)}), bf16[128,8,128]{2,1,0:T(8,128)(2,1)S(1)}, u32[]{:S(2)}, u32[]{:S(2)}) async-start(bf16[128,8,128]{2,1,0:T(8,128)(2,1)} %bitcast.17), calls=%async_computation.2 | async-start | bytes 524288 | tf_op jit(solution)/shard_map/all_to_all | solution.py:628
  151.7 2.8 %collective-permute-start.8 = (bf16[2048,128]{1,0:T(8,128)(2,1)S(1)}, bf16[2048,128]{1,0:T(8,128)(2,1)S(1)}, u32[]{:S(2)}, u32[]{:S(2)}) collective-permute-start(bf16[2048,128]{1,0:T(8,128)(2,1)S(1)} %bitcast.60), channel_id=1, source_target_pairs={{0,1},{1,0},{2,3},{3,2},{4,5},{5,4},{6,7},{7,6},{8,9},{9,8},{10,11... | collective-permute-start | bytes 1572872 | tf_op jit(solution)/shard_map/ppermute | solution.py:726

commit v6 on v5

--- a/solution.py
+++ b/solution.py
@@ -23,7 +23,7 @@
 SIDE = 2 * SZ
 BRICKS = 384
 KEPT = 84
-PARTS = 4
+PARTS = 8
 VMEM = pltpu.CompilerParams(vmem_limit_bytes=24 * 1024 * 1024)
 MOST_VMEM = pltpu.CompilerParams(vmem_limit_bytes=48 * 1024 * 1024)
 ALL_VMEM = pltpu.CompilerParams(vmem_limit_bytes=63 * 1024 * 1024)
@@ -69,11 +69,8 @@
     for copy in copies:
         copy.start()
 
-    def clear(i, c):
+    for i in range(devs):
         count[i] = 0
-        return c
-
-    lax.fori_loop(0, devs, clear, 0, unroll=8)
     buf[...] = jnp.zeros_like(buf)
     copies[0].wait()
 

time: 157 us -> 157 us (level)
  no operation moved by 1% of the time
where the time goes in v6:
time: 157 us; the launch traced here: 156 us
  starting transfers between devices  43.6 us (28%)
  Pallas kernels  37.1 us (24%)
  waiting for transfers between devices  33.7 us (21%)
  blocking collectives  20.3 us (13%)
  local copies, waits for them, and re-layouts  14.5 us (9%)
  other arithmetic  4.1 us (3%)
  matrix products  1.71 us (1%)
    all_to_all x3, starting transfers between devices, to_all(): lax.all_to_all(buffer, ('gx', 'gy'), split_axis=0, concat_axis=0, tiled=T...  28.1 us
    all_to_all x3, waiting for transfers between devices, to_all(): lax.all_to_all(buffer, ('gx', 'gy'), split_axis=0, concat_axis=0, tiled=T...  27.3 us
    all_to_all x1, blocking collectives, to_all(): lax.all_to_all(buffer, ('gx', 'gy'), split_axis=0, concat_axis=0, tiled=T...  20.3 us
    pallas_call x1, Pallas kernels, core(): pl.pallas_call(core_kernel, out_shape=tuple((jax.ShapeDtypeStruct(s, BF)...  10 us
    ppermute x4, starting transfers between devices, both_ways(): return (lax.ppermute(last_part, axis, up), lax.ppermute(first, axis, down))  8.62 us
    pallas_call x1, Pallas kernels, weights(): pl.pallas_call(weights_kernel, out_shape=(jax.ShapeDtypeStruct(shape, F32...  7.92 us
    unnamed x36, local copies, waits for them, and re-layouts  5.6 us
    pallas_call x1, Pallas kernels, send(): pl.pallas_call(functools.partial(send_kernel, cap), out_shape=(jax.ShapeD...  4.39 us
  transfers between devices with their start and end apart: 12, of which 6 were waited for; matrix products, arithmetic and copies ran while one was open for 8% of the time, Pallas kernels for 12%

profile of v6, /device:TPU:1, one launch (start us, length us, event | category | flops | bytes accessed | tf_op | source)
XLA Modules:
  0.0 156.2 jit_solution(6438288712405842477)
XLA Ops:
  0.6 4.4 %send_bricks.1 = (bf16[768,8,128]{2,1,0:T(8,128)(2,1)}, s32[192]{0:T(256)}) custom-call(s32[192]{0:T(256)} %owner_hbm.1, bf16[1536,512]{1,0:T(8,128)(2,1)} %bitcast.57, bf16[512,128]{1,0:T(8,128)(2,1)} %w_hbm.1), custom_call_target="tpu_custom_call" | custom-call | tf_op jit(solution)/shard_map/send_bricks/pallas_call | solution.py:109
  5.0 11.9 %all-to-all-start = ((bf16[768,8,128]{2,1,0:T(8,128)(2,1)}), bf16[768,8,128]{2,1,0:T(8,128)(2,1)}, u32[]{:S(2)}, u32[]{:S(2)}) async-start(bf16[768,8,128]{2,1,0:T(8,128)(2,1)} %get-tuple-element.38), calls=%async_computation | async-start | bytes 3145728 | tf_op jit(solution)/shard_map/all_to_all | solution.py:625
  19.1 1.7 %copy.58 = bf16[3,3,128,2,128]{4,3,2,1,0:T(2,128)(2,1)} copy(bf16[3,3,128,2,128]{2,4,3,1,0:T(8,128)(2,1)S(1)} %slice_bitcast_fusion) | data formatting | bytes 1179648 | tf_op jit(solution)/shard_map/transpose | solution.py:646
  20.9 1.4 copy.56
  25.1 1.2 copy_bitcast_fusion
  26.3 1.3 copy_bitcast_fusion.2
  27.6 13.6 %all-to-all-done.arrived = bf16[768,8,128]{2,1,0:T(8,128)(2,1)} async-done(((bf16[768,8,128]{2,1,0:T(8,128)(2,1)}), bf16[768,8,128]{2,1,0:T(8,128)(2,1)}, u32[]{:S(2)}, u32[]{:S(2)}) %all-to-all-start) | async-done | bytes 1572896 | tf_op jit(solution)/shard_map/all_to_all | solution.py:625
  41.2 3.5 %land_bricks.1 = (bf16[8,400,128]{2,1,0:T(8,128)(2,1)}, bf16[2,400,128]{2,1,0:T(8,128)(2,1)}, bf16[2,400,128]{2,1,0:T(8,128)(2,1)}) custom-call(s32[768]{0:T(1024)} %get-tuple-element.74.index, bf16[768,8,128]{2,1,0:T(8,128)(2,1)} %all-to-all-done.arrived, bf16[192,192]{1,0:T(8,128)(2,1)} %get-tuple-element.80.order, bf16[8,16,128]{2,1,0:T(8,128)(2,1)} %pad.26.code), custom_call_target="tpu_custom_call" | custom-call | tf_op jit(solution)/shard_map/land_bricks/pallas_call | solution.py:168
  44.7 2.3 %collective-permute-start = (bf16[2,400,128]{2,1,0:T(8,128)(2,1)}, bf16[2,400,128]{2,1,0:T(8,128)(2,1)S(1)}, u32[]{:S(2)}, u32[]{:S(2)}) collective-permute-start(bf16[2,400,128]{2,1,0:T(8,128)(2,1)} %get-tuple-element.43), channel_id=1, source_target_pairs={{0,8},{8,16},{16,24},{24,32},{32,40},{40,48},{48,56},{56,64},{64,7... | collective-permute-start | bytes 614408 | tf_op jit(solution)/shard_map/ppermute | solution.py:632
  47.1 1.3 collective-permute-start.1
  48.5 1.1 copy-done.1
  51.9 3.4 %grad_pre_inside.1.inside = bf16[6,288,128]{2,1,0:T(8,128)(2,1)S(1)} custom-call(bf16[8,400,128]{2,1,0:T(8,128)(2,1)S(1)} %copy-done.1, bf16[1152,256]{1,0:T(8,128)(2,1)S(1)} %copy-done.6, bf16[1536,256]{1,0:T(8,128)(2,1)S(1)} %copy-done.3, bf16[128,128]{1,0:T(8,128)(2,1)S(1)} %copy.62.head, bf16[128,128]{1,0:T(8,128)(2,1)S(1)} %get-tuple-element.82.head_t), custom_call_target="tpu_custom_call" | custom-call | flops 1528823808 | bytes 4194304 | tf_op jit(solution)/shard_map/grad_pre_inside/pallas_call | solution.py:280
  55.4 2.6 %collective-permute-start.2 = (bf16[12,112,128]{2,1,0:T(8,128)(2,1)S(1)}, bf16[12,112,128]{2,1,0:T(8,128)(2,1)S(1)}, u32[]{:S(2)}, u32[]{:S(2)}) collective-permute-start(bf16[12,112,128]{2,1,0:T(8,128)(2,1)S(1)} %get-tuple-element.47), channel_id=1, source_target_pairs={{0,1},{1,2},{2,3},{3,4},{4,5},{5,6},{6,7},{8,9},{9,10},{10,11},{11... | collective-permute-start | bytes 1032200 | tf_op jit(solution)/shard_map/ppermute | solution.py:632
  58.0 2.4 %collective-permute-start.3 = (bf16[12,112,128]{2,1,0:T(8,128)(2,1)S(1)}, bf16[12,112,128]{2,1,0:T(8,128)(2,1)S(1)}, u32[]{:S(2)}, u32[]{:S(2)}) collective-permute-start(bf16[12,112,128]{2,1,0:T(8,128)(2,1)S(1)} %get-tuple-element.48), channel_id=1, source_target_pairs={{1,0},{2,1},{3,2},{4,3},{5,4},{6,5},{7,6},{9,8},{10,9},{11,10},{12... | collective-permute-start | bytes 1032200 | tf_op jit(solution)/shard_map/ppermute | solution.py:632
  60.4 2.4 %grad_pre_x_sides.1.at_x = bf16[4,288,128]{2,1,0:T(8,128)(2,1)S(1)} custom-call(bf16[8,400,128]{2,1,0:T(8,128)(2,1)S(1)} %copy-done.1, bf16[2,400,128]{2,1,0:T(8,128)(2,1)S(1)} %collective-permute-done.before, bf16[2,400,128]{2,1,0:T(8,128)(2,1)S(1)} %collective-permute-done.1.after, bf16[1152,256]{1,0:T(8,128)(2,1)S(1)} %copy-done.7, ...), custom_call_target="tpu_custom_call" | custom-call | flops 1019215872 | bytes 4194304 | tf_op jit(solution)/shard_map/grad_pre_x_sides/pallas_call | solution.py:316
  62.9 3.9 %collective-permute-done.3.right = bf16[12,112,128]{2,1,0:T(8,128)(2,1)S(1)} collective-permute-done((bf16[12,112,128]{2,1,0:T(8,128)(2,1)S(1)}, bf16[12,112,128]{2,1,0:T(8,128)(2,1)S(1)}, u32[]{:S(2)}, u32[]{:S(2)}) %collective-permute-start.3) | collective-permute-done | bytes 344096 | tf_op jit(solution)/shard_map/ppermute | solution.py:632
  66.7 10.0 %conv_both_ways.1 = (bf16[768,8,128]{2,1,0:T(8,128)(2,1)}, bf16[84,576,128]{2,1,0:T(8,128)(2,1)}) custom-call(s32[768]{0:T(1024)S(1)} %get-tuple-element.73.index, bf16[8,400,128]{2,1,0:T(8,128)(2,1)S(1)} %copy-done.2, bf16[2,400,128]{2,1,0:T(8,128)(2,1)S(1)} %collective-permute-done.before, bf16[2,400,128]{2,1,0:T(8,128)(2,1)S(1)} %collective-permute-done.1.after, ...), custom_call_target="tpu_custom_call" | custom-call | tf_op jit(solution)/shard_map/conv_both_ways/pallas_call | solution.py:440
  76.7 8.9 %all-to-all-start.1 = ((bf16[768,8,128]{2,1,0:T(8,128)(2,1)}), bf16[768,8,128]{2,1,0:T(8,128)(2,1)}, u32[]{:S(2)}, u32[]{:S(2)}) async-start(bf16[768,8,128]{2,1,0:T(8,128)(2,1)} %get-tuple-element.60), calls=%async_computation.1 | async-start | bytes 3145728 | tf_op jit(solution)/shard_map/all_to_all | solution.py:625
  85.7 7.9 %conv_weight_grad.1 = (f32[16,128,128]{2,1,0:T(8,128)}, bf16[16,128,128]{2,1,0:T(8,128)(2,1)}) custom-call(s32[1]{0:T(128)} %bitcast.2.half, bf16[84,576,128]{2,1,0:T(8,128)(2,1)} %get-tuple-element.51.kept_hbm), custom_call_target="tpu_custom_call" | custom-call | flops 2717908992 | bytes 6291456 | tf_op jit(solution)/shard_map/conv_weight_grad/pallas_call | solution.py:503
  93.6 1.4 collective-permute-start.4
  95.0 1.7 %collective-permute-done.4 = bf16[16,128,128]{2,1,0:T(8,128)(2,1)S(1)} collective-permute-done((bf16[16,128,128]{2,1,0:T(8,128)(2,1)}, bf16[16,128,128]{2,1,0:T(8,128)(2,1)S(1)}, u32[]{:S(2)}, u32[]{:S(2)}) %collective-permute-start.4) | collective-permute-done | bytes 524320 | tf_op jit(solution)/shard_map/ppermute | solution.py:552
  97.5 2.3 %add_pair.1 = (f32[64,8,128]{2,1,0:T(8,128)}, bf16[64,8,128]{2,1,0:T(8,128)(2,1)}, bf16[64,8,128]{2,1,0:T(8,128)(2,1)}, bf16[64,8,128]{2,1,0:T(8,128)(2,1)}) custom-call(s32[1]{0:T(128)} %bitcast.1.me, f32[64,2,2,8,128]{4,3,2,1,0:T(8,128)} %bitcast.72, bf16[128,16,128]{2,1,0:T(8,128)(2,1)} %bitcast.74), custom_call_target="tpu_custom_call" | custom-call | tf_op jit(solution)/shard_map/add_pair/pallas_call | solution.py:537
  100.5 2.4 %collective-permute-start.6 = (bf16[64,8,128]{2,1,0:T(8,128)(2,1)}, bf16[64,8,128]{2,1,0:T(8,128)(2,1)S(1)}, u32[]{:S(2)}, u32[]{:S(2)}) collective-permute-start(bf16[64,8,128]{2,1,0:T(8,128)(2,1)} %get-tuple-element.57), channel_id=1, source_target_pairs={{0,4},{1,5},{2,6},{3,7},{4,0},{5,1},{6,2},{7,3},{8,12},{9,13},{10,... | collective-permute-start | bytes 393224 | tf_op jit(solution)/shard_map/ppermute | solution.py:556
  104.1 1.4 copy-done
  105.6 4.3 %all-to-all-done.1.came = bf16[768,8,128]{2,1,0:T(8,128)(2,1)} async-done(((bf16[768,8,128]{2,1,0:T(8,128)(2,1)}), bf16[768,8,128]{2,1,0:T(8,128)(2,1)}, u32[]{:S(2)}, u32[]{:S(2)}) %all-to-all-start.1) | async-done | bytes 1572896 | tf_op jit(solution)/shard_map/all_to_all | solution.py:625
  109.9 2.1 %stride_term.1 = (bf16[1536,128]{1,0:T(8,128)(2,1)S(1)}, bf16[512,128]{1,0:T(8,128)(2,1)S(1)}) custom-call(s32[192]{0:T(256)S(1)} %copy-done.9, bf16[768,8,128]{2,1,0:T(8,128)(2,1)} %all-to-all-done.1.came, bf16[1536,512]{1,0:T(8,128)(2,1)S(1)} %fetch_feats.1.feats), custom_call_target="tpu_custom_call" | custom-call | tf_op jit(solution)/shard_map/stride_term/pallas_call | solution.py:592
  112.9 7.3 %all-to-all-start.2 = ((bf16[128,8,128]{2,1,0:T(8,128)(2,1)}), bf16[128,8,128]{2,1,0:T(8,128)(2,1)S(1)}, u32[]{:S(2)}, u32[]{:S(2)}) async-start(bf16[128,8,128]{2,1,0:T(8,128)(2,1)} %bitcast.17), calls=%async_computation.2 | async-start | bytes 524288 | tf_op jit(solution)/shard_map/all_to_all | solution.py:625
  120.2 1.7 %convolution_convert_fusion = bf16[1536,512]{1,0:T(8,128)(2,1)} fusion(bf16[1536,128]{1,0:T(8,128)(2,1)S(1)} %get-tuple-element.70, bf16[512,128]{1,0:T(8,128)(2,1)S(1)} %copy-done.13), kind=kOutput, calls=%fused_computation | convolution fusion | flops 202113024 | bytes 2097152 | tf_op jit(solution)/shard_map/dot_general | solution.py:708
  121.9 9.4 %all-to-all-done.2 = bf16[128,8,128]{2,1,0:T(8,128)(2,1)S(1)} async-done(((bf16[128,8,128]{2,1,0:T(8,128)(2,1)}), bf16[128,8,128]{2,1,0:T(8,128)(2,1)S(1)}, u32[]{:S(2)}, u32[]{:S(2)}) %all-to-all-start.2) | async-done | bytes 262176 | tf_op jit(solution)/shard_map/all_to_all | solution.py:625
  131.5 20.3 %all_to_all.20 = bf16[128,20,128]{2,1,0:T(8,128)(2,1)S(1)} all-to-all(bf16[128,20,128]{2,1,0:T(8,128)(2,1)S(1)} %bitcast.65), channel_id=1, replica_groups=mesh['gx'=16,'gy'=8] {'gx','gy'}, dimensions={0} | all-to-all | bytes 1310720 | tf_op jit(solution)/shard_map/all_to_all | solution.py:625
  151.8 1.3 collective-permute-start.8
  154.8 1.3 convert_multiply_fusion
  (81 shorter events, 12.6 us)
Async XLA Ops:
  5.0 11.9 %copy-start.10 = (bf16[27,128,128]{2,1,0:T(8,128)(2,1)S(1)}, bf16[27,128,128]{2,1,0:T(8,128)(2,1)}, u32[]{:S(2)}) copy-start(bf16[27,128,128]{2,1,0:T(8,128)(2,1)} %param.11) | copy-start | bytes 2654212
  5.0 36.2 %all-to-all-start = ((bf16[768,8,128]{2,1,0:T(8,128)(2,1)}), bf16[768,8,128]{2,1,0:T(8,128)(2,1)}, u32[]{:S(2)}, u32[]{:S(2)}) async-start(bf16[768,8,128]{2,1,0:T(8,128)(2,1)} %get-tuple-element.38), calls=%async_computation | async-start | bytes 3145728 | tf_op jit(solution)/shard_map/all_to_all | solution.py:625
  18.3 4.0 %copy-start.16 = (s32[768]{0:T(1024)S(1)}, s32[768]{0:T(1024)}, u32[]{:S(2)}) copy-start(s32[768]{0:T(1024)} %param.9) | copy-start | bytes 9220
  18.3 5.2 %copy-start.15 = (s32[8,8,48]{2,1,0:T(8,128)S(1)}, s32[8,8,48]{2,1,0:T(8,128)}, u32[]{:S(2)}) copy-start(s32[8,8,48]{2,1,0:T(8,128)} %param.13) | copy-start | bytes 36868
  23.5 2.7 %copy-start.11 = (bf16[3,3,128,2,128]{4,3,2,1,0:T(2,128)(2,1)S(1)}, bf16[3,3,128,2,128]{4,3,2,1,0:T(2,128)(2,1)}, u32[]{:S(2)}) copy-start(bf16[3,3,128,2,128]{4,3,2,1,0:T(2,128)(2,1)} %copy.58) | copy-start | bytes 1769476
  23.5 2.7 %copy-start.12 = (bf16[3,3,128,2,128]{4,3,2,1,0:T(2,128)(2,1)S(1)}, bf16[3,3,128,2,128]{4,3,2,1,0:T(2,128)(2,1)}, u32[]{:S(2)}) copy-start(bf16[3,3,128,2,128]{4,3,2,1,0:T(2,128)(2,1)} %copy.56) | copy-start | bytes 1769476
  26.3 22.1 %copy-start.17 = (bf16[128,8]{0,1:T(8,128)(2,1)S(1)}, bf16[128,8]{0,1:T(8,128)(2,1)}, u32[]{:S(2)}) copy-start(bf16[128,8]{0,1:T(8,128)(2,1)} %param.12) | copy-start | bytes 6148
  44.7 10.6 %collective-permute-start = (bf16[2,400,128]{2,1,0:T(8,128)(2,1)}, bf16[2,400,128]{2,1,0:T(8,128)(2,1)S(1)}, u32[]{:S(2)}, u32[]{:S(2)}) collective-permute-start(bf16[2,400,128]{2,1,0:T(8,128)(2,1)} %get-tuple-element.43), channel_id=1, source_target_pairs={{0,8},{8,16},{16,24},{24,32},{32,40},{40,48},{48,56},{56,64},{64,7... | collective-permute-start | bytes 614408 | tf_op jit(solution)/shard_map/ppermute | solution.py:632
  47.1 8.2 %collective-permute-start.1 = (bf16[2,400,128]{2,1,0:T(8,128)(2,1)}, bf16[2,400,128]{2,1,0:T(8,128)(2,1)S(1)}, u32[]{:S(2)}, u32[]{:S(2)}) collective-permute-start(bf16[2,400,128]{2,1,0:T(8,128)(2,1)} %get-tuple-element.44), channel_id=1, source_target_pairs={{8,0},{16,8},{24,16},{32,24},{40,32},{48,40},{56,48},{64,56},{72,6... | collective-permute-start | bytes 614408 | tf_op jit(solution)/shard_map/ppermute | solution.py:632
  48.5 1.2 copy-start.1
  49.7 1.1 copy-start.3
  50.8 1.1 copy-start.6
  51.9 8.5 %copy-start.4 = (bf16[1536,256]{1,0:T(8,128)(2,1)S(1)}, bf16[1536,256]{1,0:T(8,128)(2,1)}, u32[]{:S(2)}) copy-start(bf16[1536,256]{1,0:T(8,128)(2,1)} %get-tuple-element.46.w_mid) | copy-start | bytes 2359300
  51.9 8.5 %copy-start.7 = (bf16[1152,256]{1,0:T(8,128)(2,1)S(1)}, bf16[1152,256]{1,0:T(8,128)(2,1)}, u32[]{:S(2)}) copy-start(bf16[1152,256]{1,0:T(8,128)(2,1)} %get-tuple-element.45.w_side) | copy-start | bytes 1769476
  55.4 7.5 %collective-permute-start.2 = (bf16[12,112,128]{2,1,0:T(8,128)(2,1)S(1)}, bf16[12,112,128]{2,1,0:T(8,128)(2,1)S(1)}, u32[]{:S(2)}, u32[]{:S(2)}) collective-permute-start(bf16[12,112,128]{2,1,0:T(8,128)(2,1)S(1)} %get-tuple-element.47), channel_id=1, source_target_pairs={{0,1},{1,2},{2,3},{3,4},{4,5},{5,6},{6,7},{8,9},{9,10},{10,11},{11... | collective-permute-start | bytes 1032200 | tf_op jit(solution)/shard_map/ppermute | solution.py:632
  58.0 8.7 %copy-start.2 = (bf16[8,400,128]{2,1,0:T(8,128)(2,1)S(1)}, bf16[8,400,128]{2,1,0:T(8,128)(2,1)}, u32[]{:S(2)}) copy-start(bf16[8,400,128]{2,1,0:T(8,128)(2,1)} %get-tuple-element.42.slab) | copy-start | bytes 2457604
  58.0 8.7 %copy-start.5 = (bf16[1152,256]{1,0:T(8,128)(2,1)S(1)}, bf16[1152,256]{1,0:T(8,128)(2,1)}, u32[]{:S(2)}) copy-start(bf16[1152,256]{1,0:T(8,128)(2,1)} %get-tuple-element.49.w_side_t) | copy-start | bytes 1769476
  58.0 8.7 %collective-permute-start.3 = (bf16[12,112,128]{2,1,0:T(8,128)(2,1)S(1)}, bf16[12,112,128]{2,1,0:T(8,128)(2,1)S(1)}, u32[]{:S(2)}, u32[]{:S(2)}) collective-permute-start(bf16[12,112,128]{2,1,0:T(8,128)(2,1)S(1)} %get-tuple-element.48), channel_id=1, source_target_pairs={{1,0},{2,1},{3,2},{4,3},{5,4},{6,5},{7,6},{9,8},{10,9},{11,10},{12... | collective-permute-start | bytes 1032200 | tf_op jit(solution)/shard_map/ppermute | solution.py:632
  76.7 33.2 %all-to-all-start.1 = ((bf16[768,8,128]{2,1,0:T(8,128)(2,1)}), bf16[768,8,128]{2,1,0:T(8,128)(2,1)}, u32[]{:S(2)}, u32[]{:S(2)}) async-start(bf16[768,8,128]{2,1,0:T(8,128)(2,1)} %get-tuple-element.60), calls=%async_computation.1 | async-start | bytes 3145728 | tf_op jit(solution)/shard_map/all_to_all | solution.py:625
  93.6 3.2 %collective-permute-start.4 = (bf16[16,128,128]{2,1,0:T(8,128)(2,1)}, bf16[16,128,128]{2,1,0:T(8,128)(2,1)S(1)}, u32[]{:S(2)}, u32[]{:S(2)}) collective-permute-start(bf16[16,128,128]{2,1,0:T(8,128)(2,1)} %get-tuple-element.53), channel_id=1, source_target_pairs={{0,1},{1,0},{2,3},{3,2},{4,5},{5,4},{6,7},{7,6},{8,9},{9,8},{10,11... | collective-permute-start | bytes 1572872 | tf_op jit(solution)/shard_map/ppermute | solution.py:552
  96.8 0.8 copy-start.14
  99.9 10.1 %copy-start.9 = (s32[192]{0:T(256)S(1)}, s32[192]{0:T(256)}, u32[]{:S(2)}) copy-start(s32[192]{0:T(256)} %get-tuple-element.59.place) | copy-start | bytes 2308
  99.9 12.2 %collective-permute-start.5 = (bf16[64,8,128]{2,1,0:T(8,128)(2,1)}, bf16[64,8,128]{2,1,0:T(8,128)(2,1)S(1)}, u32[]{:S(2)}, u32[]{:S(2)}) collective-permute-start(bf16[64,8,128]{2,1,0:T(8,128)(2,1)} %get-tuple-element.56), channel_id=1, source_target_pairs={{0,2},{1,3},{2,4},{3,5},{4,6},{5,7},{6,0},{7,1},{8,10},{9,11},{10,... | collective-permute-start | bytes 393224 | tf_op jit(solution)/shard_map/ppermute | solution.py:556
  100.5 11.6 %collective-permute-start.6 = (bf16[64,8,128]{2,1,0:T(8,128)(2,1)}, bf16[64,8,128]{2,1,0:T(8,128)(2,1)S(1)}, u32[]{:S(2)}, u32[]{:S(2)}) collective-permute-start(bf16[64,8,128]{2,1,0:T(8,128)(2,1)} %get-tuple-element.57), channel_id=1, source_target_pairs={{0,4},{1,5},{2,6},{3,7},{4,0},{5,1},{6,2},{7,3},{8,12},{9,13},{10,... | collective-permute-start | bytes 393224 | tf_op jit(solution)/shard_map/ppermute | solution.py:556
  103.0 9.1 %collective-permute-start.7 = (bf16[64,8,128]{2,1,0:T(8,128)(2,1)}, bf16[64,8,128]{2,1,0:T(8,128)(2,1)S(1)}, u32[]{:S(2)}, u32[]{:S(2)}) collective-permute-start(bf16[64,8,128]{2,1,0:T(8,128)(2,1)} %get-tuple-element.58), channel_id=1, source_target_pairs={{0,6},{1,7},{2,0},{3,1},{4,2},{5,3},{6,4},{7,5},{8,14},{9,15},{10,... | collective-permute-start | bytes 393224 | tf_op jit(solution)/shard_map/ppermute | solution.py:556
  104.1 1.4 copy-start
  105.6 6.5 %copy-start.8 = (f32[64,8,128]{2,1,0:T(8,128)S(1)}, f32[64,8,128]{2,1,0:T(8,128)}, u32[]{:S(2)}) copy-start(f32[64,8,128]{2,1,0:T(8,128)} %get-tuple-element.66.refs_0_) | copy-start | bytes 786436
  105.6 14.6 %copy-start.13 = (bf16[512,128]{1,0:T(8,128)(2,1)S(1)}, bf16[512,128]{1,0:T(8,128)(2,1)}, u32[]{:S(2)}) copy-start(bf16[512,128]{1,0:T(8,128)(2,1)} %w_hbm.1) | copy-start | bytes 393220
  112.9 18.4 %all-to-all-start.2 = ((bf16[128,8,128]{2,1,0:T(8,128)(2,1)}), bf16[128,8,128]{2,1,0:T(8,128)(2,1)S(1)}, u32[]{:S(2)}, u32[]{:S(2)}) async-start(bf16[128,8,128]{2,1,0:T(8,128)(2,1)} %bitcast.17), calls=%async_computation.2 | async-start | bytes 524288 | tf_op jit(solution)/shard_map/all_to_all | solution.py:625
  151.8 2.8 %collective-permute-start.8 = (bf16[2048,128]{1,0:T(8,128)(2,1)S(1)}, bf16[2048,128]{1,0:T(8,128)(2,1)S(1)}, u32[]{:S(2)}, u32[]{:S(2)}) collective-permute-start(bf16[2048,128]{1,0:T(8,128)(2,1)S(1)} %bitcast.60), channel_id=1, source_target_pairs={{0,1},{1,0},{2,3},{3,2},{4,5},{5,4},{6,7},{7,6},{8,9},{9,8},{10,11... | collective-permute-start | bytes 1572872 | tf_op jit(solution)/shard_map/ppermute | solution.py:723
